TPU v7x, 32 devices: a whole 2x2x4 slice. The times are simulated.
32 devices in a mesh: ctx: 8 (over y, x, core), fsdp: 4 (over z).
Axes of the slice: x: 2, y: 2, z: 4, core: 2. Of those that a mesh axis runs over, the one named last changes fastest.
Arguments:
- tokens: bfloat16 [4, 1024, 2048], P('fsdp', 'ctx'), may hold values from -6 to 6
- cotangent: bfloat16 [4, 1024, 2048], P('fsdp', 'ctx'), may hold values from -6 to 6
- doc_ids: int32 [4, 1024], P('fsdp', 'ctx'), may hold values from 0 to 2, as said below
- in_proj: bfloat16 [2048, 6656], P('fsdp'), may hold values from -0.125 to 0.125
- dt_proj: bfloat16 [2048, 48], P('fsdp'), may hold values from -0.125 to 0.125
- conv_weight: float32 [4, 3584], replicated, may hold values from -3 to 3
- conv_bias: float32 [3584], replicated, may hold values from -3 to 3
- dt_bias: float32 [48], replicated, may hold values from -7 to -3
- a_log: float32 [48], replicated, may hold values from -2 to 2
- d_skip: float32 [48], replicated, may hold values from 0.5 to 1.5
- mixer_gain: float32 [3072], replicated, may hold values from 0.5 to 1.5
- out_proj: bfloat16 [3072, 2048], P('fsdp'), may hold values from -0.109375 to 0.109375
- qkv_proj: bfloat16 [2048, 1536], P('fsdp'), may hold values from -0.125 to 0.125
- o_proj: bfloat16 [1024, 2048], P('fsdp'), may hold values from -3 to 3
- first_gain: float32 [2048], replicated, may hold values from 0.5 to 1.5
- second_gain: float32 [2048], replicated, may hold values from 0.5 to 1.5
- gate_up: bfloat16 [2048, 8192], P('fsdp'), may hold values from -0.125 to 0.125
- down_proj: bfloat16 [4096, 2048], P('fsdp'), may hold values from -0.09375 to 0.09375
Outputs:
- mixed: bfloat16 [4, 1024, 2048], P('fsdp', 'ctx')
- d_tokens: float32 [4, 1024, 2048], P('fsdp', 'ctx')
- in_proj_grad: float32 [2048, 6656], P('fsdp')
- dt_proj_grad: float32 [2048, 48], P('fsdp')
- conv_weight_grad: float32 [4, 3584], replicated
- conv_bias_grad: float32 [3584], replicated
- dt_bias_grad: float32 [48], replicated
- a_log_grad: float32 [48], replicated
- d_skip_grad: float32 [48], replicated
- mixer_gain_grad: float32 [3072], replicated
- out_proj_grad: float32 [3072, 2048], P('fsdp')
- qkv_proj_grad: float32 [2048, 1536], P('fsdp')
- o_proj_grad: float32 [1024, 2048], P('fsdp')
- first_gain_grad: float32 [2048], replicated
- second_gain_grad: float32 [2048], replicated
- gate_up_grad: float32 [2048, 8192], P('fsdp')
- down_proj_grad: float32 [4096, 2048], P('fsdp')
Inputs may be any that keep to these rules, and one draw needn't show every extreme that they name: `doc_ids`: in each sequence, never falling; document 0 ends inside the first 128 tokens and document 2 begins inside the last 128, so document 1 covers every other token.
All inputs are finite; a program needn't handle non-finite values.
Results may differ from a plain program's by a relative error of at most 0.022.
Values may be sent and summed in bfloat16 or wider, within the bound.
No kernel may reach another device: no remote copies, remote signals or barrier semaphores. Data moves between devices by JAX's collectives and lax.ppermute only.
A program may use at most 640 MiB of HBM per device.

v0:
```python
import jax
import jax.numpy as jnp
from jax import lax
from jax.sharding import PartitionSpec as P

FF = 4096
NH = 48
HP = 64
NS = 256
KC = 4
HQ = 8
HK = 2
HA = 128
DS = 3072


HIGH = lax.Precision.HIGHEST
epsilon = 1e-05
rope_base = 100000000000.0


def from_behind(block, axis, distance):
    devices = range(lax.axis_size(axis))
    route = [(i - distance, i) for i in devices if i - distance in devices]
    return lax.ppermute(block, axis, route)


def carried_in(array, axis, join, neutral):
    place = lax.axis_index(axis)
    gathered = jax.tree.map(
        lambda a, kind: lax.all_gather(a.astype(kind), axis), array, (jnp.bfloat16, jnp.bfloat16)
    )
    state = jax.tree.map(lambda a, e: jnp.zeros_like(a) + jnp.asarray(e, a.dtype), array, neutral)

    def one(lap, state):
        return join(
            state,
            jax.tree.map(
                lambda a, own: lax.dynamic_index_in_dim(a, lap, 0, False).astype(own.dtype),
                gathered,
                array,
            ),
        )

    return lax.fori_loop(0, place, one, state)


def prefix(array, axis, combine, identity):
    peers, mine = (lax.axis_size(axis), lax.axis_index(axis))
    everything = jax.tree.map(
        lambda part, kind: lax.all_gather(part.astype(kind), axis),
        array,
        jax.tree.map(lambda a: jnp.bfloat16 if a.dtype == jnp.float32 else a.dtype, array),
    )
    start = jax.tree.map(
        lambda part, zero: jnp.broadcast_to(jnp.asarray(zero, part.dtype), part.shape),
        array,
        identity,
    )

    def lap(k, before):
        at = peers - 1 - k
        reached = at > mine
        new = combine(
            before, jax.tree.map(lambda part, own: part[at].astype(own.dtype), everything, array)
        )
        return jax.tree.map(lambda a, b: jnp.where(reached, a, b), new, before)

    return lax.fori_loop(0, peers, lap, start)


def normed(operand, gain_vec):
    return (
        operand
        * lax.rsqrt(jnp.mean(operand * operand, axis=-1, keepdims=True) + epsilon)
        * gain_vec
    )


def rotate(operand, places, direction):
    half_width = operand.shape[-1] // 2
    frequency = rope_base ** (
        -jnp.arange(half_width, dtype=jnp.float32) * (2.0 / operand.shape[-1])
    )
    angles = places.astype(jnp.float32)[:, None] * frequency[None, :]
    cosine = jnp.cos(angles)[:, None, :]
    sine_part = direction * jnp.sin(angles)[:, None, :]
    first_half = operand[..., :half_width]
    second_half = operand[..., half_width:]
    return jnp.concatenate(
        [
            first_half * cosine - second_half * sine_part,
            second_half * cosine + first_half * sine_part,
        ],
        -1,
    )


def project(left_side, right_side):
    return jnp.dot(left_side, right_side, preferred_element_type=jnp.float32)


def project_back(grad_in, weight):
    return lax.dot_general(
        grad_in, weight, (((1,), (1,)), ((), ())), preferred_element_type=jnp.float32
    )


def convolve(padded, pad_ids, row_ids, kernel_in, bias_in):
    length = row_ids.shape[0]
    total = jnp.zeros((length, padded.shape[1]), jnp.float32) + bias_in[None, :]
    for offset in range(KC):
        same_doc = (pad_ids[offset : offset + length] == row_ids).astype(jnp.float32)
        total = (
            total
            + kernel_in[offset][None, :] * padded[offset : offset + length] * same_doc[:, None]
        )
    return total


def ssm_local(states_x, step_size, log_decay, b_matrix, c_matrix, row_ids):
    length = states_x.shape[0]
    running = jnp.cumsum(log_decay, axis=0)
    places = jnp.arange(length, dtype=jnp.int32)
    allowed = (places[:, None] >= places[None, :]) & (row_ids[:, None] == row_ids[None, :])
    spread = running.T[:, :, None] - running.T[:, None, :]
    decay_matrix = jnp.where(allowed[None], jnp.exp(jnp.where(allowed[None], spread, 0.0)), 0.0)
    intersection = jnp.dot(c_matrix, b_matrix.T, precision=HIGH, preferred_element_type=jnp.float32)
    driven = step_size[:, :, None] * states_x
    y_part = jnp.einsum("hts,shp->thp", decay_matrix * intersection[None], driven, precision=HIGH)
    to_end = jnp.where(
        (row_ids == row_ids[-1])[:, None], jnp.exp(running[-1][None, :] - running), 0.0
    )
    local_state = jnp.einsum("sh,shp,sn->hpn", to_end, driven, b_matrix, precision=HIGH)
    return (y_part, local_state)


def ssm_carry(c_matrix, log_decay, row_ids, prev_id, state_in):
    kept_mask = (row_ids == prev_id).astype(jnp.float32)
    weight = jnp.exp(jnp.cumsum(log_decay, axis=0)) * kept_mask[:, None]
    return weight[:, :, None] * jnp.einsum("hpn,tn->thp", state_in, c_matrix, precision=HIGH)


def block_decay(log_decay, row_ids, prev_id):
    return jnp.exp(jnp.sum(log_decay, axis=0)) * (row_ids[-1] == prev_id).astype(jnp.float32)


def combine(earlier, later):
    return (earlier[0] * later[0], later[0][:, None, None] * earlier[1] + later[1])


def mixer_tail(core_in, states_x, gate_z, skip_in, gain_in):
    length = core_in.shape[0]
    core = core_in + skip_in[None, :, None] * states_x
    gated = core.reshape(length, DS) * jax.nn.silu(gate_z)
    return normed(gated, gain_in)


def swiglu(gate_up_out):
    return jax.nn.silu(gate_up_out[:, :FF]) * gate_up_out[:, FF:]


def body(
    tokens,
    cotangent,
    doc_ids,
    in_proj,
    dt_proj,
    conv_weight,
    conv_bias,
    dt_bias,
    a_log,
    d_skip,
    mixer_gain,
    out_proj,
    qkv_proj,
    o_proj,
    first_gain,
    second_gain,
    gate_up,
    down_proj,
):
    hidden = tokens[0].astype(jnp.float32)
    grad_out = cotangent[0].astype(jnp.float32)
    own_ids = doc_ids[0]
    length = hidden.shape[0]
    my_index = lax.axis_index("ctx")
    all_ids = lax.all_gather(own_ids, "ctx", axis=0, tiled=True)
    first_row = my_index * length
    places = first_row + jnp.arange(length, dtype=jnp.int32)
    before = first_row - (KC - 1) + jnp.arange(KC - 1, dtype=jnp.int32)
    earlier_ids = lax.dynamic_slice_in_dim(all_ids, jnp.maximum(first_row - (KC - 1), 0), KC - 1, 0)
    earlier_ids = jnp.where(before >= 0, earlier_ids, -1)
    pad_ids = jnp.concatenate([earlier_ids, own_ids], 0)
    prev_id = jnp.where(my_index > 0, all_ids[jnp.maximum(first_row - 1, 0)], -1)
    full_in, full_dt, full_out, full_qkv, full_o, full_gu, full_down = (
        lax.all_gather(in_proj, "fsdp", axis=0, tiled=True),
        lax.all_gather(dt_proj, "fsdp", axis=0, tiled=True),
        lax.all_gather(out_proj, "fsdp", axis=0, tiled=True),
        lax.all_gather(qkv_proj, "fsdp", axis=0, tiled=True),
        lax.all_gather(o_proj, "fsdp", axis=0, tiled=True),
        lax.all_gather(gate_up, "fsdp", axis=0, tiled=True),
        lax.all_gather(down_proj, "fsdp", axis=0, tiled=True),
    )
    normed_in, norm_pull = jax.vjp(normed, hidden, first_gain)
    input_low = normed_in.astype(jnp.bfloat16)
    projected = project(input_low, full_in)
    step_raw = project(input_low, full_dt)
    attn_in = project(input_low, full_qkv)
    gate_z = projected[:, :DS]
    conv_low = projected[:, DS:].astype(jnp.bfloat16)
    tail_low = from_behind(conv_low[length - (KC - 1) :], "ctx", 1)

    def front_fn(conv_in, tail_in, shift_in, kernel_in, bias_in, bias_step, log_rate):
        padded = jnp.concatenate([tail_in, conv_in], 0)
        activated = jax.nn.silu(convolve(padded, pad_ids, own_ids, kernel_in, bias_in))
        states_x = activated[:, :DS].reshape(length, NH, HP)
        b_matrix = activated[:, DS : DS + NS]
        c_matrix = activated[:, DS + NS :]
        step_size = jax.nn.softplus(shift_in + bias_step)
        log_decay = -step_size * jnp.exp(log_rate)
        y_part, local_state = ssm_local(states_x, step_size, log_decay, b_matrix, c_matrix, own_ids)
        return (y_part, local_state, states_x, c_matrix, log_decay)

    front_out, front_pull = jax.vjp(
        front_fn,
        conv_low.astype(jnp.float32),
        tail_low.astype(jnp.float32),
        step_raw,
        conv_weight,
        conv_bias,
        dt_bias,
        a_log,
    )
    y_part, local_state, states_x, c_matrix, log_decay = front_out
    decay_now, decay_pull = jax.vjp(lambda log_in: block_decay(log_in, own_ids, prev_id), log_decay)
    identity = (jnp.ones_like(decay_now), jnp.zeros_like(local_state))
    state_in = carried_in((decay_now, local_state), "ctx", combine, identity)[1]
    y_carry, carry_pull = jax.vjp(
        lambda c_in, log_in, state_arg: ssm_carry(c_in, log_in, own_ids, prev_id, state_arg),
        c_matrix,
        log_decay,
        state_in,
    )
    mixer_normed, tail_pull = jax.vjp(
        mixer_tail, y_part + y_carry, states_x, gate_z, d_skip, mixer_gain
    )
    mixer_low = mixer_normed.astype(jnp.bfloat16)
    mixer_out = project(mixer_low, full_out)
    groups = HQ // HK
    scale = HA ** (-0.5)
    query_low = rotate(attn_in[:, : HQ * HA].reshape(length, HQ, HA), places, 1.0).astype(
        jnp.bfloat16
    )
    key_low = rotate(
        attn_in[:, HQ * HA : (HQ + HK) * HA].reshape(length, HK, HA), places, 1.0
    ).astype(jnp.bfloat16)
    value_low = attn_in[:, (HQ + HK) * HA :].reshape(length, HK, HA).astype(jnp.bfloat16)
    query_groups = query_low.reshape(length, HK, groups, HA)
    top_now = jnp.full((HK, groups, length), -1e30, jnp.float32)
    key_piece = lax.all_gather(key_low, "ctx", axis=0, tiled=True)
    value_piece = lax.all_gather(value_low, "ctx", axis=0, tiled=True)
    key_ids = lax.all_gather(own_ids, "ctx", axis=0, tiled=True)
    width = key_piece.shape[0]
    key_places = jnp.arange(width, dtype=jnp.int32)
    score = (
        jnp.einsum("qkgd,rkd->kgqr", query_groups, key_piece, preferred_element_type=jnp.float32)
        * scale
    )
    allowed = (places[:, None] >= key_places[None, :]) & (own_ids[:, None] == key_ids[None, :])
    score = jnp.where(allowed[None, None], score, -1e30)
    new_top = jnp.maximum(top_now, jnp.max(score, axis=-1))
    weight = jnp.where(allowed[None, None], jnp.exp(score - new_top[..., None]), 0.0)
    total = jnp.sum(weight, axis=-1)
    accum = jnp.einsum(
        "kgqr,rkd->qkgd",
        weight.astype(jnp.bfloat16),
        value_piece,
        preferred_element_type=jnp.float32,
    )
    accum, top_now, total = (accum, new_top, total)
    attended = accum / jnp.transpose(total, (2, 0, 1))[..., None]
    log_total = top_now + jnp.log(total)
    attended_low = attended.reshape(length, HQ * HA).astype(jnp.bfloat16)
    attn_out = project(attended_low, full_o)
    middle = hidden + mixer_out + attn_out
    normed_mid, mid_pull = jax.vjp(normed, middle, second_gain)
    mid_low = normed_mid.astype(jnp.bfloat16)
    gate_up_out = project(mid_low, full_gu)
    act_value, act_pull = jax.vjp(swiglu, gate_up_out)
    act_low = act_value.astype(jnp.bfloat16)
    mixed = middle + project(act_low, full_down)
    full_in, full_dt, full_out, full_qkv, full_o, full_gu, full_down = (
        lax.all_gather(in_proj, "fsdp", axis=0, tiled=True),
        lax.all_gather(dt_proj, "fsdp", axis=0, tiled=True),
        lax.all_gather(out_proj, "fsdp", axis=0, tiled=True),
        lax.all_gather(qkv_proj, "fsdp", axis=0, tiled=True),
        lax.all_gather(o_proj, "fsdp", axis=0, tiled=True),
        lax.all_gather(gate_up, "fsdp", axis=0, tiled=True),
        lax.all_gather(down_proj, "fsdp", axis=0, tiled=True),
    )
    grad_low = grad_out.astype(jnp.bfloat16)
    d_act = project_back(grad_low, full_down)
    gu_low = act_pull(d_act)[0].astype(jnp.bfloat16)
    d_mid_norm = project_back(gu_low, full_gu)
    d_middle_part, d_second_gain = mid_pull(d_mid_norm)
    d_middle = grad_out + d_middle_part
    branch_low = d_middle.astype(jnp.bfloat16)
    d_mixer_norm = project_back(branch_low, full_out)
    d_attended = project_back(branch_low, full_o)
    d_out_low = d_attended.reshape(length, HK, groups, HA).astype(jnp.bfloat16)
    delta = jnp.transpose(jnp.sum(d_out_low.astype(jnp.float32) * attended, axis=-1), (1, 2, 0))
    keys_all, values_all = (
        lax.all_gather(key_low, "ctx", axis=0, tiled=True),
        lax.all_gather(value_low, "ctx", axis=0, tiled=True),
    )
    seq_len = keys_all.shape[0]
    block = min(seq_len, 512)

    def key_block(d_query, block_index):
        begin = block_index * block
        key_part = lax.dynamic_slice_in_dim(keys_all, begin, block, 0)
        value_part = lax.dynamic_slice_in_dim(values_all, begin, block, 0)
        key_ids = lax.dynamic_slice_in_dim(all_ids, begin, block, 0)
        key_places = begin + jnp.arange(block, dtype=jnp.int32)
        score = (
            jnp.einsum("qkgd,rkd->kgqr", query_groups, key_part, preferred_element_type=jnp.float32)
            * scale
        )
        allowed = (places[:, None] >= key_places[None, :]) & (own_ids[:, None] == key_ids[None, :])
        prob = jnp.where(
            allowed[None, None],
            jnp.exp(jnp.where(allowed[None, None], score, 0.0) - log_total[..., None]),
            0.0,
        )
        d_prob = jnp.einsum(
            "qkgd,rkd->kgqr", d_out_low, value_part, preferred_element_type=jnp.float32
        )
        score_grad = (prob * (d_prob - delta[..., None])).astype(jnp.bfloat16)
        d_query = (
            d_query
            + jnp.einsum("kgqr,rkd->qkgd", score_grad, key_part, preferred_element_type=jnp.float32)
            * scale
        )
        d_keys = (
            jnp.einsum(
                "kgqr,qkgd->rkd", score_grad, query_groups, preferred_element_type=jnp.float32
            )
            * scale
        )
        d_values = jnp.einsum(
            "kgqr,qkgd->rkd",
            prob.astype(jnp.bfloat16),
            d_out_low,
            preferred_element_type=jnp.float32,
        )
        return (d_query, jnp.concatenate([d_keys, d_values], 1).reshape(block, 2 * HK * HA))

    d_query, kv_terms = lax.scan(
        key_block,
        jnp.zeros((length, HK, groups, HA), jnp.float32),
        jnp.arange(seq_len // block, dtype=jnp.int32),
    )
    d_kv = lax.psum_scatter(
        kv_terms.reshape(seq_len, 2 * HK * HA).astype(jnp.bfloat16),
        "ctx",
        scatter_dimension=0,
        tiled=True,
    ).astype(jnp.float32)
    d_attn_in = jnp.concatenate(
        [
            rotate(d_query.reshape(length, HQ, HA), places, -1.0).reshape(length, HQ * HA),
            rotate(d_kv[:, : HK * HA].reshape(length, HK, HA), places, -1.0).reshape(
                length, HK * HA
            ),
            d_kv[:, HK * HA :],
        ],
        1,
    )
    qkv_low = d_attn_in.astype(jnp.bfloat16)
    d_core, d_states_tail, d_gate_z, d_d_skip, d_mixer_gain = tail_pull(d_mixer_norm)
    d_c_carry, d_log_carry, d_state_in = carry_pull(d_core)
    later_grad = prefix((decay_now, d_state_in), "ctx", combine, identity)[1]
    d_decay = jnp.sum(later_grad * state_in, axis=(1, 2))
    d_log_decay = decay_pull(d_decay)[0]
    d_conv_in, d_tail, d_step_raw, d_conv_weight, d_conv_bias, d_dt_bias, d_a_log = front_pull(
        (d_core, later_grad, d_states_tail, d_c_carry, d_log_carry + d_log_decay)
    )
    from_next = from_behind(d_tail.astype(jnp.bfloat16), "ctx", -1).astype(d_tail.dtype)
    d_conv_in = jnp.concatenate(
        [d_conv_in[: length - (KC - 1)], d_conv_in[length - (KC - 1) :] + from_next], 0
    )
    proj_low = jnp.concatenate([d_gate_z, d_conv_in], 1).astype(jnp.bfloat16)
    step_low = d_step_raw.astype(jnp.bfloat16)
    d_normed_in = (
        project_back(proj_low, full_in)
        + project_back(step_low, full_dt)
        + project_back(qkv_low, full_qkv)
    )
    d_hidden_part, d_first_gain = norm_pull(d_normed_in)
    d_tokens = d_middle + d_hidden_part

    def weight_grad(act_in, grad_in):
        return lax.psum_scatter(
            lax.dot_general(
                act_in, grad_in, (((0,), (0,)), ((), ())), preferred_element_type=jnp.float32
            ).astype(jnp.bfloat16),
            "fsdp",
            scatter_dimension=0,
            tiled=True,
        ).astype(jnp.float32)

    shards = [
        weight_grad(act_in, grad_in)
        for act_in, grad_in in (
            (input_low, proj_low),
            (input_low, step_low),
            (mixer_low, branch_low),
            (input_low, qkv_low),
            (attended_low, branch_low),
            (mid_low, gu_low),
            (act_low, grad_low),
        )
    ]
    summed = (
        lax.psum(shards[0].astype(jnp.bfloat16), "ctx").astype(jnp.float32),
        lax.psum(shards[1].astype(jnp.bfloat16), "ctx").astype(jnp.float32),
        lax.psum(shards[2].astype(jnp.bfloat16), "ctx").astype(jnp.float32),
        lax.psum(shards[3].astype(jnp.bfloat16), "ctx").astype(jnp.float32),
        lax.psum(shards[4].astype(jnp.bfloat16), "ctx").astype(jnp.float32),
        lax.psum(shards[5].astype(jnp.bfloat16), "ctx").astype(jnp.float32),
        lax.psum(shards[6].astype(jnp.bfloat16), "ctx").astype(jnp.float32),
    )
    smalls = lax.psum(
        (
            d_conv_weight,
            d_conv_bias,
            d_dt_bias,
            d_a_log,
            d_d_skip,
            d_mixer_gain,
            d_first_gain,
            d_second_gain,
        ),
        ("ctx", "fsdp"),
    )
    return (
        mixed[None].astype(jnp.bfloat16),
        d_tokens[None],
        summed[0],
        summed[1],
        smalls[0],
        smalls[1],
        smalls[2],
        smalls[3],
        smalls[4],
        smalls[5],
        summed[2],
        summed[3],
        summed[4],
        smalls[6],
        smalls[7],
        summed[5],
        summed[6],
    )


def solution(mesh):
    return jax.shard_map(
        body,
        mesh=mesh,
        in_specs=(
            P("fsdp", "ctx", None),
            P("fsdp", "ctx", None),
            P("fsdp", "ctx"),
            P("fsdp", None),
            P("fsdp", None),
            P(),
            P(),
            P(),
            P(),
            P(),
            P(),
            P("fsdp", None),
            P("fsdp", None),
            P("fsdp", None),
            P(),
            P(),
            P("fsdp", None),
            P("fsdp", None),
        ),
        out_specs=(
            P("fsdp", "ctx", None),
            P("fsdp", "ctx", None),
            P("fsdp", None),
            P("fsdp", None),
            P(),
            P(),
            P(),
            P(),
            P(),
            P(),
            P("fsdp", None),
            P("fsdp", None),
            P("fsdp", None),
            P(),
            P(),
            P("fsdp", None),
            P("fsdp", None),
        ),
        check_vma=False,
    )
```

profile of v0, /device:TPU:0, one launch (start us, length us, event | category | flops | bytes accessed | tf_op | source)
XLA Modules:
  0.0 4185.6 jit_solution(10153307166386498091)
XLA Ops:
  9.4 15.5 all_gather.58
  26.6 8.8 all-gather
  37.8 433.7 %all-gather.13.cloned.1.call-done = bf16[2048,6656]{1,0:T(8,128)(2,1)} async-done(((bf16[512,6656]{1,0:T(8,128)(2,1)}), bf16[2048,6656]{1,0:T(8,128)(2,1)}) %all-gather.13.cloned.1.call-update) | async-done | bytes 27262992 | tf_op jit(solution)/shard_map/all_gather | solution.py:197
  471.5 15.3 fusion.178
  496.7 5.2 convolution_convert_fusion.8
  506.6 15.1 all-reduce.14
  524.5 62.2 %all-gather.17.cloned.1.call-done = bf16[2048,1536]{1,0:T(8,128)(2,1)} async-done(((bf16[512,1536]{1,0:T(8,128)(2,1)}), bf16[2048,1536]{1,0:T(8,128)(2,1)}) %all-gather.17.cloned.1.call-update) | async-done | bytes 6291472 | tf_op jit(solution)/shard_map/all_gather | solution.py:200
  592.6 11.8 all_gather.67
  604.4 12.3 all_gather.66
  622.0 39.6 all-gather.25.cloned.1.call-done
  666.4 7.6 fusion.50
  681.5 199.8 %all-gather.15.cloned.1.call-done = bf16[3072,2048]{1,0:T(8,128)(2,1)} async-done(((bf16[768,2048]{1,0:T(8,128)(2,1)}), bf16[3072,2048]{1,0:T(8,128)(2,1)}) %all-gather.15.cloned.1.call-update) | async-done | bytes 12582928 | tf_op jit(solution)/shard_map/all_gather | solution.py:199
  881.3 7.9 convolution_add_fusion.2
  889.2 72.5 %all-gather.19.cloned.1.call-done = bf16[1024,2048]{1,0:T(8,128)(2,1)} async-done(((bf16[256,2048]{1,0:T(8,128)(2,1)}), bf16[1024,2048]{1,0:T(8,128)(2,1)}) %all-gather.19.cloned.1.call-update) | async-done | bytes 4194320 | tf_op jit(solution)/shard_map/all_gather | solution.py:201
  966.4 556.7 %all-gather.21.cloned.1.call-done = bf16[2048,8192]{1,0:T(8,128)(2,1)} async-done(((bf16[512,8192]{1,0:T(8,128)(2,1)}), bf16[2048,8192]{1,0:T(8,128)(2,1)}) %all-gather.21.cloned.1.call-update) | async-done | bytes 33554448 | tf_op jit(solution)/shard_map/all_gather | solution.py:202
  1523.1 20.2 fusion.158
  1543.3 266.3 %all-gather.23.cloned.1.call-done = bf16[4096,2048]{1,0:T(8,128)(2,1)} async-done(((bf16[1024,2048]{1,0:T(8,128)(2,1)}), bf16[4096,2048]{1,0:T(8,128)(2,1)}) %all-gather.23.cloned.1.call-update) | async-done | bytes 16777232 | tf_op jit(solution)/shard_map/all_gather | solution.py:203
  1809.7 15.6 fusion.116
  1825.2 20.4 multiply_reduce_fusion.13
  1856.3 33.2 while.43
  1890.1 10.5 multiply_reduce_fusion.7
  1908.3 5.2 convolution_convert_fusion.7
  1935.1 5.7 convolution_convert_fusion.4
  1941.5 9.8 convolution_convert_fusion.3
  1951.5 13.5 convolution_convert_fusion.2
  1965.6 16.5 convolution_convert_fusion
  1987.2 7.7 fusion.41
  1998.0 47.9 %while.42 = (s32[]{:T(128)}, f32[48,64,256]{2,1,0:T(8,128)}, s32[]{:T(128)}, bf16[8,48]{1,0:T(8,128)(2,1)}, bf16[8,48,64,256]{3,2,1,0:T(8,128)(2,1)}, /*index=5*/s32[]{:T(128)}, s32[]{:T(128)}, s32[]{:T(128)}, s32[]{:T(128)}) while((s32[]{:T(128)}, f32[48,64,256]{2,1,0:T(8,128)}, s32[]{:T(128)}, bf16[8,48]{1,0:T(8,128)(2,1)}, ...), condition=%wide.region_13.14_spmd.clone, body=%wide.region_12.13_spmd.clone.sunk | while | flops 3932216 | bytes 7864975 | solution.py:69
  2004.3 4.9 fusion.234
  2034.5 4.9 fusion.234
  2040.6 4.9 fusion.234
  2046.0 4.9 fusion.119
  2051.0 6.7 multiply_reduce_fusion.6
  2060.7 5.3 fusion.82
  2076.5 15.2 convolution_convert_fusion.1
  2107.4 84.4 %reduce-scatter.19.cloned.1.call-done = bf16[512,1536]{1,0:T(8,128)(2,1)} async-done(((bf16[2048,1536]{1,0:T(8,128)(2,1)}), bf16[512,1536]{1,0:T(8,128)(2,1)}) %reduce-scatter.19.cloned.1.call-update) | async-done | bytes 1572880 | tf_op jit(solution)/shard_map/reduce_scatter | solution.py:404
  2191.8 215.3 %reduce-scatter.17.cloned.1.call-done = bf16[768,2048]{1,0:T(8,128)(2,1)} async-done(((bf16[3072,2048]{1,0:T(8,128)(2,1)}), bf16[768,2048]{1,0:T(8,128)(2,1)}) %reduce-scatter.17.cloned.1.call-update) | async-done | bytes 3145744 | tf_op jit(solution)/shard_map/reduce_scatter | solution.py:404
  2407.1 284.4 %reduce-scatter.23.cloned.1.call-done = bf16[1024,2048]{1,0:T(8,128)(2,1)} async-done(((bf16[4096,2048]{1,0:T(8,128)(2,1)}), bf16[1024,2048]{1,0:T(8,128)(2,1)}) %reduce-scatter.23.cloned.1.call-update) | async-done | bytes 4194320 | tf_op jit(solution)/shard_map/reduce_scatter | solution.py:404
  2691.6 555.0 %reduce-scatter.25.cloned.1.call-done = bf16[512,8192]{1,0:T(8,128)(2,1)} async-done(((bf16[2048,8192]{1,0:T(8,128)(2,1)}), bf16[512,8192]{1,0:T(8,128)(2,1)}) %reduce-scatter.25.cloned.1.call-update) | async-done | bytes 8388624
  3246.6 451.0 %reduce-scatter.13.cloned.1.call-done = bf16[512,6656]{1,0:T(8,128)(2,1)} async-done(((bf16[2048,6656]{1,0:T(8,128)(2,1)}), bf16[512,6656]{1,0:T(8,128)(2,1)}) %reduce-scatter.13.cloned.1.call-update) | async-done | bytes 6815760 | tf_op jit(solution)/shard_map/reduce_scatter | solution.py:404
  3699.1 8.9 fusion.33
  3708.1 6.0 fusion.118
  3715.5 14.8 fusion.107
  3737.6 27.7 psum.106
  3765.9 271.4 %all-reduce.23.cloned.1.call-done = (bf16[512,6656]{1,0:T(8,128)(2,1)}, bf16[768,2048]{1,0:T(8,128)(2,1)}, bf16[512,1536]{1,0:T(8,128)(2,1)}, bf16[256,2048]{1,0...) async-done(((bf16[512,6656]{1,0:T(8,128)(2,1)}, bf16[768,2048]{1,0:T(8,128)(2,1)}, bf16[512,1536]{1,0:T(8,128)(2,1)}, bf16[256,2048]{1,0:T(8,128)(2,1)}, ...) | async-done | bytes 25165840 | tf_op jit(solution)/shard_map/psum | solution.py:426
  4037.3 10.0 convert_element_type.276
  4054.5 11.9 convert_element_type.286
  4070.9 97.5 %all-reduce.21.cloned.1.call-done = (f32[4,3584]{1,0:T(4,128)}, f32[3584]{0:T(1024)}, f32[48]{0:T(128)}, f32[48]{0:T(128)}, f32[48]{0:T(128)}, /*index=5*/f32[3072]{0:T(1024)}, f32[2048]{0:T(1024)}, f32[2048]{0:T(1024)}) async-done(((f32[4,3584]{1,0:T(4,128)}, f32[3584]{0:T(1024)}, f32[48]{0:T(128)}, f32[48]{0:T(128)}, f32[48]{0:T(128)}, /*index=5*/f32[3072]{0:T(1024)}, f32[2048]{0:T(1024)}, ...) | async-done | bytes 100944 | tf_op jit(solution)/shard_map/psum | solution.py:434
  (517 shorter events, 224.8 us)
Async XLA Ops:
  7.2 464.3 %all-gather.13.cloned.1.call-start = ((), (), s32[]{:S(2)}) async-start(), calls=%async_computation.8 | async-start | bytes 34078720 | tf_op jit(solution)/shard_map/all_gather | solution.py:197
  8.0 28.7 copy-start.92
  8.0 578.7 %all-gather.17.cloned.1.call-start = ((), (), s32[]{:S(2)}) async-start(), calls=%async_computation.10 | async-start | bytes 7864320 | tf_op jit(solution)/shard_map/all_gather | solution.py:200
  8.7 652.9 %all-gather.25.cloned.1.call-start = ((), (), s32[]{:S(2)}) async-start(), calls=%async_computation.21 | async-start | bytes 14155776 | tf_op jit(solution)/shard_map/all_gather | solution.py:31
  9.4 27.2 copy-start.127
  24.9 462.0 %copy-start.44 = (bf16[2048,48]{0,1:T(8,128)(2,1)}, bf16[2048,48]{0,1:T(8,128)(2,1)S(1)}, u32[]{:S(2)}) copy-start(bf16[2048,48]{0,1:T(8,128)(2,1)S(1)} %all_gather.58) | copy-start | bytes 589828
  25.1 561.6 %copy-start.87 = (f32[128]{0:T(128)}, f32[128]{0:T(128)S(1)}, u32[]{:S(2)}) copy-start(f32[128]{0:T(128)S(1)} %fusion.143) | copy-start | bytes 1540
  26.2 470.5 %copy-start.73 = (f32[128,48]{0,1:T(8,128)}, f32[128,48]{0,1:T(8,128)S(1)}, u32[]{:S(2)}) copy-start(f32[128,48]{0,1:T(8,128)S(1)} %get-tuple-element.500) | copy-start | bytes 73732
  26.2 480.1 %copy-start.132 = (f32[48]{0:T(128)}, f32[48]{0:T(128)S(1)}, u32[]{:S(2)}) copy-start(f32[48]{0:T(128)S(1)} %get-tuple-element.469) | copy-start | bytes 580
  26.5 496.0 %copy-start.35 = (f32[128,48]{1,0:T(8,128)}, f32[128,48]{1,0:T(8,128)S(1)}, u32[]{:S(2)}) copy-start(f32[128,48]{1,0:T(8,128)S(1)} %reduce_window_sum.29) | copy-start | bytes 73732
  26.6 460.3 %copy-start.56 = (f32[128,48]{0,1:T(8,128)}, f32[128,48]{0,1:T(8,128)S(1)}, u32[]{:S(2)}) copy-start(f32[128,48]{0,1:T(8,128)S(1)} %copy.156) | copy-start | bytes 73732
  35.3 488.6 %copy-start.79 = (s32[1,1024]{1,0:T(1,128)}, s32[1,1024]{1,0:T(1,128)S(1)}, u32[]{:S(2)}) copy-start(s32[1,1024]{1,0:T(1,128)S(1)} %all-gather) | copy-start | bytes 12292
  36.9 452.8 %copy-start.64 = (f32[3584]{0:T(1024)}, f32[3584]{0:T(1024)S(1)}, u32[]{:S(2)}) copy-start(f32[3584]{0:T(1024)S(1)} %get-tuple-element.396) | copy-start | bytes 43012
  36.9 452.8 %copy-start.66 = (f32[3584]{0:T(1024)}, f32[3584]{0:T(1024)S(1)}, u32[]{:S(2)}) copy-start(f32[3584]{0:T(1024)S(1)} %get-tuple-element.397) | copy-start | bytes 43012
  36.9 452.8 %copy-start.68 = (f32[3584]{0:T(1024)}, f32[3584]{0:T(1024)S(1)}, u32[]{:S(2)}) copy-start(f32[3584]{0:T(1024)S(1)} %get-tuple-element.398) | copy-start | bytes 43012
  36.9 452.8 %copy-start.70 = (f32[3584]{0:T(1024)}, f32[3584]{0:T(1024)S(1)}, u32[]{:S(2)}) copy-start(f32[3584]{0:T(1024)S(1)} %get-tuple-element.399) | copy-start | bytes 43012
  37.7 449.2 %copy-start.111 = (pred[128]{0:T(512)(128)(4,1)}, pred[128]{0:T(512)(128)(4,1)S(1)}, u32[]{:S(2)}) copy-start(pred[128]{0:T(512)(128)(4,1)S(1)} %get-tuple-element.508) | copy-start | bytes 388
  37.7 452.1 %copy-start.113 = (f32[128]{0:T(128)}, f32[128]{0:T(128)S(1)}, u32[]{:S(2)}) copy-start(f32[128]{0:T(128)S(1)} %get-tuple-element.501) | copy-start | bytes 1540
  37.7 452.1 %copy-start.115 = (f32[128]{0:T(128)}, f32[128]{0:T(128)S(1)}, u32[]{:S(2)}) copy-start(f32[128]{0:T(128)S(1)} %get-tuple-element.502) | copy-start | bytes 1540
  37.7 452.1 %copy-start.117 = (f32[128]{0:T(128)}, f32[128]{0:T(128)S(1)}, u32[]{:S(2)}) copy-start(f32[128]{0:T(128)S(1)} %get-tuple-element.503) | copy-start | bytes 1540
  37.7 484.8 %copy-start.121 = (f32[128]{0:T(128)}, f32[128]{0:T(128)S(1)}, u32[]{:S(2)}) copy-start(f32[128]{0:T(128)S(1)} %get-tuple-element.507) | copy-start | bytes 1540
  37.7 449.2 %copy-start.119 = (f32[48]{0:T(128)}, f32[48]{0:T(128)S(1)}, u32[]{:S(2)}) copy-start(f32[48]{0:T(128)S(1)} %slice_bitcast_fusion.1) | copy-start | bytes 580
  37.8 458.9 %copy-start.59 = (f32[128,48]{0,1:T(8,128)}, f32[128,48]{0,1:T(8,128)S(1)}, u32[]{:S(2)}) copy-start(f32[128,48]{0,1:T(8,128)S(1)} %fusion.139) | copy-start | bytes 73732
  486.9 2.7 collective-permute-start
  492.2 128.8 %copy-start.8 = (f32[128,3584]{1,0:T(8,128)}, f32[128,3584]{1,0:T(8,128)S(1)}, u32[]{:S(2)}) copy-start(f32[128,3584]{1,0:T(8,128)S(1)} %get-tuple-element.471) | copy-start | bytes 5505028
  501.9 379.4 %all-gather.15.cloned.1.call-start = ((), (), s32[]{:S(2)}) async-start(), calls=%async_computation.9 | async-start | bytes 15728640 | tf_op jit(solution)/shard_map/all_gather | solution.py:199
  502.4 459.3 %all-gather.19.cloned.1.call-start = ((), (), s32[]{:S(2)}) async-start(), calls=%async_computation.11 | async-start | bytes 5242880 | tf_op jit(solution)/shard_map/all_gather | solution.py:201
  503.0 1020.1 %all-gather.21.cloned.1.call-start = ((), (), s32[]{:S(2)}) async-start(), calls=%async_computation.12 | async-start | bytes 41943040 | tf_op jit(solution)/shard_map/all_gather | solution.py:202
  503.6 1306.0 %all-gather.23.cloned.1.call-start = ((), (), s32[]{:S(2)}) async-start(), calls=%async_computation.13 | async-start | bytes 20971520 | tf_op jit(solution)/shard_map/all_gather | solution.py:203
  504.4 1419.9 %reduce-scatter.11.cloned.1.call-start = ((), (), s32[]{:S(2)}) async-start(), calls=%async_computation.14 | async-start | bytes 1179648 | tf_op jit(solution)/shard_map/reduce_scatter | solution.py:364
  524.5 1398.2 %copy-start.37 = (f32[128,64]{1,0:T(8,128)}, f32[128,64]{1,0:T(8,128)S(1)}, u32[]{:S(2)}) copy-start(f32[128,64]{1,0:T(8,128)S(1)} %get-tuple-element.506) | copy-start | bytes 98308
  524.5 1398.2 %copy-start.50 = (f32[128,64]{1,0:T(8,128)}, f32[128,64]{1,0:T(8,128)S(1)}, u32[]{:S(2)}) copy-start(f32[128,64]{1,0:T(8,128)S(1)} %get-tuple-element.504) | copy-start | bytes 98308
  621.1 340.6 %copy-start.33 = (bf16[128,2,4,128]{0,3,2,1:T(8,128)(2,1)}, bf16[128,2,4,128]{0,3,2,1:T(8,128)(2,1)S(1)}, u32[]{:S(2)}) copy-start(bf16[128,2,4,128]{0,3,2,1:T(8,128)(2,1)S(1)} %get-tuple-element.514) | copy-start | bytes 786436
  681.5 207.7 %copy-start.104 = (f32[128]{0:T(128)}, f32[128]{0:T(128)S(1)}, u32[]{:S(2)}) copy-start(f32[128]{0:T(128)S(1)} %fusion.144) | copy-start | bytes 1540
  961.7 561.4 %copy-start.53 = (f32[2048]{0:T(1024)S(1)}, f32[2048]{0:T(1024)}, u32[]{:S(2)}) copy-start(f32[2048]{0:T(1024)} %param.39) | copy-start | bytes 24580
  966.4 879.3 %copy-start.97 = (f32[128]{0:T(128)}, f32[128]{0:T(128)S(1)}, u32[]{:S(2)}) copy-start(f32[128]{0:T(128)S(1)} %fusion.145) | copy-start | bytes 1540
  1889.6 108.4 %all-gather.27.cloned.1.call-start = ((), (), s32[]{:S(2)}) async-start(), calls=%async_computation.22 | async-start | bytes 14155776 | tf_op jit(solution)/shard_map/all_gather | solution.py:51
  1913.5 193.9 %reduce-scatter.21.cloned.1.call-start = ((), (), s32[]{:S(2)}) async-start(), calls=%async_computation.19 | async-start | bytes 5242880 | tf_op jit(solution)/shard_map/reduce_scatter | solution.py:404
  1917.9 273.9 %reduce-scatter.19.cloned.1.call-start = ((), (), s32[]{:S(2)}) async-start(), calls=%async_computation.18 | async-start | bytes 7864320 | tf_op jit(solution)/shard_map/reduce_scatter | solution.py:404
  1940.9 466.2 %reduce-scatter.17.cloned.1.call-start = ((), (), s32[]{:S(2)}) async-start(), calls=%async_computation.17 | async-start | bytes 15728640 | tf_op jit(solution)/shard_map/reduce_scatter | solution.py:404
  1951.4 740.1 %reduce-scatter.23.cloned.1.call-start = ((), (), s32[]{:S(2)}) async-start(), calls=%async_computation.20 | async-start | bytes 20971520 | tf_op jit(solution)/shard_map/reduce_scatter | solution.py:404
  1965.0 1281.6 %reduce-scatter.25.cloned.1.call-start = ((), (), s32[]{:S(2)}) async-start(), calls=%async_computation.23 | async-start | bytes 41943040
  1982.1 1715.4 %reduce-scatter.13.cloned.1.call-start = ((), (), s32[]{:S(2)}) async-start(), calls=%async_computation.15 | async-start | bytes 34078720 | tf_op jit(solution)/shard_map/reduce_scatter | solution.py:404
  2073.3 3.1 collective-permute-start.1
  2091.7 1645.8 %reduce-scatter.15.cloned.1.call-start = ((), (), s32[]{:S(2)}) async-start(), calls=%async_computation.16 | async-start | bytes 245760 | tf_op jit(solution)/shard_map/reduce_scatter | solution.py:404
  2106.3 1591.3 %copy-start.93 = (bf16[128,48]{0,1:T(8,128)(2,1)}, bf16[128,48]{0,1:T(8,128)(2,1)S(1)}, u32[]{:S(2)}) copy-start(bf16[128,48]{0,1:T(8,128)(2,1)S(1)} %get-tuple-element.463) | copy-start | bytes 36868
  2107.4 1930.0 %all-reduce.23.cloned.1.call-start = ((), (), s32[]{:S(2)}) async-start(), calls=%async_computation.25 | async-start | bytes 50331648 | tf_op jit(solution)/shard_map/psum | solution.py:426
  3697.6 470.9 %all-reduce.21.cloned.1.call-start = ((), (), s32[]{:S(2)}) async-start(), calls=%async_computation.24 | async-start | bytes 207872 | tf_op jit(solution)/shard_map/psum | solution.py:434
  (119 other events, 640.8 us)
Sparse Core Ops, SparseCore 0:
  9.6 461.8 all-gather.12
  473.1 113.5 all-gather.16
  589.1 72.4 all-gather.24
  663.1 218.1 all-gather.14
  882.7 78.9 all-gather.18
  963.1 559.9 all-gather.20
  1524.7 284.9 all-gather.22
  1889.7 34.2 reduce-scatter.10
  1925.9 72.0 all-gather.26
  2000.7 76.7 reduce-scatter.20
  2080.5 111.2 reduce-scatter.18
  2194.7 212.3 reduce-scatter.16
  2410.2 281.3 reduce-scatter.22
  2693.8 552.7 reduce-scatter.24
  3248.9 448.5 reduce-scatter.12
  3700.2 21.4 reduce-scatter.14
  3727.2 310.0 all-reduce.22
  4044.7 123.6 all-reduce.20
where the time goes:
time: 4200 us; the launch traced here: 4190 us
  waiting for transfers between devices  3600 us (86%)
  matrix products  274 us (7%)
  other arithmetic  130 us (3%)
  blocking collectives  91 us (2%)
  local copies, waits for them, and re-layouts  68.2 us (2%)
    reduce_scatter x6, waiting for transfers between devices, weight_grad(): lax.psum_scatter(lax.dot_general(act_in, grad_in, (((0,), (0,)), ((), ())...  1040 us
    unnamed x19, waiting for transfers between devices  559 us
    all_gather x1, waiting for transfers between devices, body(): lax.all_gather(gate_up, 'fsdp', axis=0, tiled=True)  557 us
    all_gather x1, waiting for transfers between devices, body(): lax.all_gather(in_proj, 'fsdp', axis=0, tiled=True)  434 us
    psum x1, waiting for transfers between devices, body(): lax.psum(shards[0].astype(jnp.bfloat16), 'ctx').astype(jnp.float32)  271 us
    all_gather x1, waiting for transfers between devices, body(): lax.all_gather(down_proj, 'fsdp', axis=0, tiled=True)  266 us
    all_gather x1, waiting for transfers between devices, body(): lax.all_gather(out_proj, 'fsdp', axis=0, tiled=True)  200 us
    psum x1, waiting for transfers between devices, body(): lax.psum((d_conv_weight, d_conv_bias, d_dt_bias, d_a_log, d_d_skip, d_mix...  97.5 us
  transfers between devices with their start and end apart: 20, of which 17 were waited for; matrix products, arithmetic and copies ran while one was open for 9% of the time, Pallas kernels for 0%

commit v1 on v0

--- a/solution.py
+++ b/solution.py
@@ -1,8 +1,11 @@
 import jax
 import jax.numpy as jnp
 from jax import lax
+from jax.experimental import pallas as pl
+from jax.experimental.pallas import tpu as pltpu
 from jax.sharding import PartitionSpec as P
 
+D = 2048
 FF = 4096
 NH = 48
 HP = 64
@@ -23,50 +26,6 @@
     devices = range(lax.axis_size(axis))
     route = [(i - distance, i) for i in devices if i - distance in devices]
     return lax.ppermute(block, axis, route)
-
-
-def carried_in(array, axis, join, neutral):
-    place = lax.axis_index(axis)
-    gathered = jax.tree.map(
-        lambda a, kind: lax.all_gather(a.astype(kind), axis), array, (jnp.bfloat16, jnp.bfloat16)
-    )
-    state = jax.tree.map(lambda a, e: jnp.zeros_like(a) + jnp.asarray(e, a.dtype), array, neutral)
-
-    def one(lap, state):
-        return join(
-            state,
-            jax.tree.map(
-                lambda a, own: lax.dynamic_index_in_dim(a, lap, 0, False).astype(own.dtype),
-                gathered,
-                array,
-            ),
-        )
-
-    return lax.fori_loop(0, place, one, state)
-
-
-def prefix(array, axis, combine, identity):
-    peers, mine = (lax.axis_size(axis), lax.axis_index(axis))
-    everything = jax.tree.map(
-        lambda part, kind: lax.all_gather(part.astype(kind), axis),
-        array,
-        jax.tree.map(lambda a: jnp.bfloat16 if a.dtype == jnp.float32 else a.dtype, array),
-    )
-    start = jax.tree.map(
-        lambda part, zero: jnp.broadcast_to(jnp.asarray(zero, part.dtype), part.shape),
-        array,
-        identity,
-    )
-
-    def lap(k, before):
-        at = peers - 1 - k
-        reached = at > mine
-        new = combine(
-            before, jax.tree.map(lambda part, own: part[at].astype(own.dtype), everything, array)
-        )
-        return jax.tree.map(lambda a, b: jnp.where(reached, a, b), new, before)
-
-    return lax.fori_loop(0, peers, lap, start)
 
 
 def normed(operand, gain_vec):
@@ -145,10 +104,6 @@
     return jnp.exp(jnp.sum(log_decay, axis=0)) * (row_ids[-1] == prev_id).astype(jnp.float32)
 
 
-def combine(earlier, later):
-    return (earlier[0] * later[0], later[0][:, None, None] * earlier[1] + later[1])
-
-
 def mixer_tail(core_in, states_x, gate_z, skip_in, gain_in):
     length = core_in.shape[0]
     core = core_in + skip_in[None, :, None] * states_x
@@ -158,6 +113,364 @@
 
 def swiglu(gate_up_out):
     return jax.nn.silu(gate_up_out[:, :FF]) * gate_up_out[:, FF:]
+
+
+def swap(block, distance):
+    peers = lax.axis_size("ctx")
+    return lax.ppermute(block, "ctx", [(i, i ^ distance) for i in range(peers)])
+
+
+def shifted(block, hops):
+    peers = lax.axis_size("fsdp")
+    return lax.ppermute(block, "fsdp", [(i, (i + hops) % peers) for i in range(peers)])
+
+
+def powers(first, limit):
+    found = []
+    while first < limit:
+        found.append(first)
+        first *= 2
+    return found
+
+
+def chip_steps():
+    return powers(2, lax.axis_size("ctx"))
+
+
+def ordered(flag, first, second, axis):
+    return jnp.where(
+        flag,
+        jnp.concatenate([second, first], axis),
+        jnp.concatenate([first, second], axis),
+    )
+
+
+def halves(flag, array, axis):
+    size = array.shape[axis] // 2
+    low = lax.slice_in_dim(array, 0, size, axis=axis)
+    high = lax.slice_in_dim(array, size, 2 * size, axis=axis)
+    return (jnp.where(flag, high, low), jnp.where(flag, low, high))
+
+
+def join(earlier, later):
+    return (earlier[0] * later[0], later[0][:, None, None] * earlier[1] + later[1])
+
+
+def either(flag, when, otherwise):
+    return jax.tree.map(lambda a, b: jnp.where(flag, a, b), when, otherwise)
+
+
+def entering(decay, state, place, backwards):
+    def sent(pair, step):
+        return (swap(pair[0], step), swap(pair[1].astype(jnp.bfloat16), step).astype(jnp.float32))
+
+    def is_later(step):
+        return (jnp.bitwise_and(place, step) != 0) != backwards
+
+    core = jnp.bitwise_and(place, 1) == 1
+    near = sent((decay, state), 1)
+    total = either(is_later(1), join(near, (decay, state)), join((decay, state), near))
+    total = tuple(halves(core, part, 0)[0] for part in total)
+    before = (jnp.ones_like(total[0]), jnp.zeros_like(total[1]))
+    steps = chip_steps()
+    for step in steps:
+        there = sent(total, step)
+        before = either(is_later(step), join(there, before), before)
+        if step != steps[-1]:
+            total = either(is_later(step), join(there, total), join(total, there))
+    across = swap(before[1].astype(jnp.bfloat16), 1).astype(jnp.float32)
+    whole = ordered(core, before[1], across, 0)
+    return jnp.where(is_later(1), near[0][:, None, None] * whole + near[1], whole)
+
+
+def place_kernel(first_col, found, idx_ref, shard_ref, *refs):
+    count = sum(len(side) for side in found)
+    part_refs, whole_ref, sems = refs[:count], refs[count], refs[-1]
+    chip, core, layer = idx_ref[0], idx_ref[1], idx_ref[2]
+    depth, width = shard_ref.shape[0], whole_ref.shape[1]
+    layers, rows = whole_ref.shape[0] // depth, part_refs[0].shape[1]
+    columns = pl.ds(pl.multiple_of(first_col + core * width, 128), width)
+    copies = [
+        pltpu.make_async_copy(
+            shard_ref.at[:, columns],
+            whole_ref.at[pl.ds(pl.multiple_of(layer * depth, depth), depth), :],
+            sems.at[0],
+        )
+    ]
+    at = 0
+    for side, groups in enumerate(found):
+        for group in groups:
+            for number, other in enumerate(group):
+                for hop in range(layers - 1):
+                    owner = lax.rem(layer + 1 + hop, layers)
+                    begin = owner * depth + jnp.bitwise_xor(chip, other) * rows
+                    copies.append(
+                        pltpu.make_async_copy(
+                            part_refs[at].at[number * (layers - 1) + hop],
+                            whole_ref.at[
+                                pl.ds(pl.multiple_of(begin, rows), rows),
+                                pl.ds(side * (width // 2), width // 2),
+                            ],
+                            sems.at[len(copies)],
+                        )
+                    )
+            at += 1
+    for copy in copies:
+        copy.start()
+    for copy in copies:
+        copy.wait()
+
+
+def placed(idx, shard, first_col, found, parts):
+    layers = lax.axis_size("fsdp")
+    rows, width = parts[0][0].shape[1], 2 * parts[0][0].shape[2]
+    depth = shard.shape[0]
+    count = 1 + sum((layers - 1) * len(group) for side in found for group in side)
+    flat = [part for side in parts for part in side]
+    return pl.pallas_call(
+        lambda *refs: place_kernel(first_col, found, *refs),
+        out_shape=jax.ShapeDtypeStruct((layers * depth, width), shard.dtype),
+        in_specs=[pl.BlockSpec(memory_space=pltpu.SMEM)]
+        + [pl.BlockSpec(memory_space=pl.ANY)] * (1 + len(flat)),
+        out_specs=pl.BlockSpec(memory_space=pltpu.VMEM),
+        scratch_shapes=[pltpu.SemaphoreType.DMA((count,))],
+        compiler_params=pltpu.CompilerParams(vmem_limit_bytes=32 * 1024 * 1024),
+        cost_estimate=pl.CostEstimate(
+            flops=0, bytes_accessed=4 * layers * depth * width, transcendentals=0
+        ),
+        name="place",
+    )(idx, shard, *flat)
+
+
+def gathered(chunks, idx, chip, core, layer):
+    steps, layers = chip_steps(), lax.axis_size("fsdp")
+    stages = len(steps) + 1
+    pieces, along = [], {}
+    for shard, first_col, width in chunks:
+        rows = shard.shape[0] // (lax.axis_size("ctx") // 2)
+        cut = lax.dynamic_slice_in_dim(
+            shard[:, first_col : first_col + width], chip * rows, rows, 0
+        )
+        pieces.append(halves(core == 1, cut, 1)[0])
+    along[0] = lax.all_gather(pieces[0], "fsdp")
+
+    def others(block):
+        return jnp.stack(
+            [
+                lax.dynamic_index_in_dim(block, lax.rem(layer + 1 + hop, layers), 0, False)
+                for hop in range(layers - 1)
+            ]
+        )
+
+    state, found, done = {}, {}, [None] * len(chunks)
+    pieces = dict(enumerate(pieces))
+    for turn in range(len(chunks) + stages - 1):
+        live = [at for at in range(len(chunks)) if 0 <= turn - at < stages]
+        held = ([state[at] for at in live if at in state], along, pieces)
+        held, along, pieces = lax.optimization_barrier(held)
+        state.update(zip([at for at in live if at in state], held, strict=True))
+        if turn + 1 < len(chunks):
+            along[turn + 1] = lax.all_gather(pieces[turn + 1], "fsdp")
+        if turn in along:
+            rest, width = others(along.pop(turn)), chunks[turn][2] // 2
+            state[turn] = [[rest[:, :, : width // 2]], [rest[:, :, width // 2 :]]]
+            found[turn] = [[[0]], [[0]]]
+        for at in live:
+            stage = turn - at
+            if stage < len(steps):
+                for side in range(2):
+                    step = (steps[side:] + steps[:side])[stage]
+                    have = state[at][side]
+                    block = jnp.concatenate(have, 0) if len(have) > 1 else have[0]
+                    state[at][side] = have + [swap(block, step)]
+                    reached = [other for group in found[at][side] for other in group]
+                    found[at][side] = found[at][side] + [
+                        [other ^ (step // 2) for other in reached]
+                    ]
+            else:
+                own = placed(idx, chunks[at][0], chunks[at][1], found[at], state[at])
+                done[at] = (own, swap(own, 1))
+    return done
+
+
+def tile_of(width):
+    return max(tile for tile in range(128, 1025, 128) if width % tile == 0)
+
+
+def forth_kernel(idx_ref, left_ref, own_ref, other_ref, out_ref):
+    for side, part_ref in enumerate((own_ref, other_ref)):
+
+        @pl.when(pl.program_id(0) == side)
+        def _():
+            out_ref[...] = jnp.dot(
+                left_ref[...], part_ref[...], preferred_element_type=jnp.float32
+            ).astype(out_ref.dtype)
+
+
+def back_kernel(idx_ref, grad_ref, own_ref, other_ref, out_ref):
+    @pl.when((pl.program_id(0) == 0) & (pl.program_id(1) == 0))
+    def _():
+        out_ref[...] = jnp.zeros_like(out_ref)
+
+    for side, part_ref in enumerate((own_ref, other_ref)):
+
+        @pl.when(pl.program_id(0) == side)
+        def _():
+            out_ref[...] += lax.dot_general(
+                grad_ref[...],
+                part_ref[...],
+                (((1,), (1,)), ((), ())),
+                preferred_element_type=jnp.float32,
+            )
+
+
+def product_specs(depth, width):
+    tile = tile_of(width)
+    count = width // tile
+    return (
+        tile,
+        count,
+        pl.BlockSpec((depth, tile), lambda s, t, idx: (0, jnp.where(s == 0, t, count - 1))),
+        pl.BlockSpec((depth, tile), lambda s, t, idx: (0, jnp.where(s == 0, 0, t))),
+        lambda s, t, idx: (0, jnp.bitwise_xor(idx[1], s) * count + t),
+    )
+
+
+def forth(idx, left_side, chunk, kind=jnp.float32):
+    rows, (depth, width) = left_side.shape[0], chunk[0].shape
+    tile, count, own_spec, other_spec, place = product_specs(depth, width)
+    return pl.pallas_call(
+        forth_kernel,
+        grid_spec=pltpu.PrefetchScalarGridSpec(
+            num_scalar_prefetch=1,
+            grid=(2, count),
+            in_specs=[pl.BlockSpec((rows, depth), lambda s, t, idx: (0, 0)), own_spec, other_spec],
+            out_specs=pl.BlockSpec((rows, tile), place),
+        ),
+        out_shape=jax.ShapeDtypeStruct((rows, 2 * width), kind),
+        compiler_params=pltpu.CompilerParams(vmem_limit_bytes=40 * 1024 * 1024),
+        cost_estimate=pl.CostEstimate(
+            flops=4 * rows * depth * width, bytes_accessed=4 * depth * width, transcendentals=0
+        ),
+        name="forth",
+    )(idx, left_side, *chunk)
+
+
+def back(idx, grad_in, chunk):
+    rows, (depth, width) = grad_in.shape[0], chunk[0].shape
+    tile, count, own_spec, other_spec, place = product_specs(depth, width)
+    return pl.pallas_call(
+        back_kernel,
+        grid_spec=pltpu.PrefetchScalarGridSpec(
+            num_scalar_prefetch=1,
+            grid=(2, count),
+            in_specs=[pl.BlockSpec((rows, tile), place), own_spec, other_spec],
+            out_specs=pl.BlockSpec((rows, depth), lambda s, t, idx: (0, 0)),
+        ),
+        out_shape=jax.ShapeDtypeStruct((rows, depth), jnp.float32),
+        compiler_params=pltpu.CompilerParams(vmem_limit_bytes=40 * 1024 * 1024),
+        cost_estimate=pl.CostEstimate(
+            flops=4 * rows * depth * width, bytes_accessed=4 * depth * width, transcendentals=0
+        ),
+        name="back",
+    )(idx, grad_in, *chunk)
+
+
+def dealt(array, layer):
+    peers = lax.axis_size("fsdp")
+    width = array.shape[1] // peers
+
+    def cut(hops):
+        return lax.dynamic_slice_in_dim(array, lax.rem(layer + hops, peers) * width, width, 1)
+
+    ahead = [cut(0)] + [shifted(cut(peers - hops), peers - hops) for hops in range(1, peers)]
+    twice = jnp.concatenate(ahead + ahead, 0)
+    length = array.shape[0]
+    return lax.dynamic_slice_in_dim(
+        twice, lax.rem(peers - layer, peers) * length, peers * length, 0
+    )
+
+
+def every(block):
+    return lax.all_gather(block, "fsdp", axis=0, tiled=True)
+
+
+def added(left_side, right_side):
+    return (left_side.astype(jnp.float32) + right_side.astype(jnp.float32)).astype(jnp.bfloat16)
+
+
+def plane_sum(part, place, core):
+    steps = chip_steps()
+    own, other = halves(core == 1, part, 1)
+    own = added(own, swap(other, 1))
+    size = own.shape[0] // 2
+    sides = []
+    for side in range(2):
+        order = steps[side:] + steps[:side]
+        block = own[side * size : (side + 1) * size]
+        for step in order:
+            keep, send = halves(jnp.bitwise_and(place, step) != 0, block, 0)
+            block = added(keep, swap(send, step))
+        for step in order[::-1]:
+            block = ordered(jnp.bitwise_and(place, step) != 0, block, swap(block, step), 0)
+        sides.append(block)
+    own = jnp.concatenate(sides, 0)
+    return (own, swap(own, 1))
+
+
+def finish_kernel(widths, idx_ref, *refs):
+    out_ref = refs[-1]
+    for flag in (0, 1):
+
+        @pl.when(idx_ref[1] == flag)
+        def _():
+            at = 0
+            for number, width in enumerate(widths):
+                pair = refs[2 * number : 2 * number + 2]
+                low, high = pair[flag], pair[1 - flag]
+                half = low.shape[1]
+                out_ref[:, at : at + half] = low[...].astype(jnp.float32)
+                out_ref[:, at + half : at + width] = high[:, : width - half].astype(jnp.float32)
+                at += width
+
+
+def finished(idx, pairs, widths, first_row=0, rows=None):
+    rows = rows or pairs[0][0].shape[0]
+    block = 32
+    while block < 256 and rows % (2 * block) == 0 and first_row % (2 * block) == 0:
+        block *= 2
+    while block > 32 and block * sum(widths) > 1024 * 1024:
+        block //= 2
+    skip = first_row // block
+    flat = [part for pair in pairs for part in pair]
+    return pl.pallas_call(
+        lambda *refs: finish_kernel(widths, *refs),
+        grid=(rows // block,),
+        out_shape=jax.ShapeDtypeStruct((rows, sum(widths)), jnp.float32),
+        in_specs=[pl.BlockSpec(memory_space=pltpu.SMEM)]
+        + [pl.BlockSpec((block, part.shape[1]), lambda i: (i + skip, 0)) for part in flat],
+        out_specs=pl.BlockSpec((block, sum(widths)), lambda i: (i, 0)),
+        compiler_params=pltpu.CompilerParams(vmem_limit_bytes=32 * 1024 * 1024),
+        cost_estimate=pl.CostEstimate(
+            flops=0, bytes_accessed=6 * rows * sum(widths), transcendentals=0
+        ),
+        name="finish",
+    )(idx, *flat)
+
+
+def sum_of_all(arrays):
+    flat = jnp.concatenate([array.reshape(-1) for array in arrays])
+    size = flat.shape[0]
+    flat = jnp.pad(flat, (0, -size % 1024)).reshape(-1, 128)
+    for axis in ("ctx", "fsdp"):
+        peers = lax.axis_size(axis)
+        for step in powers(1, peers):
+            flat = flat + lax.ppermute(flat, axis, [(i, i ^ step) for i in range(peers)])
+    flat, found, at = flat.reshape(-1), [], 0
+    for array in arrays:
+        found.append(flat[at : at + array.size].reshape(array.shape))
+        at += array.size
+    return found
 
 
 def body(
@@ -185,7 +498,12 @@
     own_ids = doc_ids[0]
     length = hidden.shape[0]
     my_index = lax.axis_index("ctx")
-    all_ids = lax.all_gather(own_ids, "ctx", axis=0, tiled=True)
+    all_ids = own_ids.reshape(1, length)
+    for step in powers(1, lax.axis_size("ctx")):
+        all_ids = ordered(
+            jnp.bitwise_and(my_index, step) != 0, all_ids, swap(all_ids, step), 0
+        )
+    all_ids = all_ids.reshape(-1)
     first_row = my_index * length
     places = first_row + jnp.arange(length, dtype=jnp.int32)
     before = first_row - (KC - 1) + jnp.arange(KC - 1, dtype=jnp.int32)
@@ -193,22 +511,59 @@
     earlier_ids = jnp.where(before >= 0, earlier_ids, -1)
     pad_ids = jnp.concatenate([earlier_ids, own_ids], 0)
     prev_id = jnp.where(my_index > 0, all_ids[jnp.maximum(first_row - 1, 0)], -1)
-    full_in, full_dt, full_out, full_qkv, full_o, full_gu, full_down = (
-        lax.all_gather(in_proj, "fsdp", axis=0, tiled=True),
-        lax.all_gather(dt_proj, "fsdp", axis=0, tiled=True),
-        lax.all_gather(out_proj, "fsdp", axis=0, tiled=True),
-        lax.all_gather(qkv_proj, "fsdp", axis=0, tiled=True),
-        lax.all_gather(o_proj, "fsdp", axis=0, tiled=True),
-        lax.all_gather(gate_up, "fsdp", axis=0, tiled=True),
-        lax.all_gather(down_proj, "fsdp", axis=0, tiled=True),
-    )
+    core = jnp.bitwise_and(my_index, 1)
+    layer = lax.axis_index("fsdp")
+    layers = lax.axis_size("fsdp")
+    idx = jnp.stack([my_index // 2, core, layer]).astype(jnp.int32)
+    z_qkv_dt = jnp.concatenate(
+        [
+            in_proj[:, :DS],
+            qkv_proj,
+            dt_proj,
+            jnp.zeros((qkv_proj.shape[0], 512 - NH), jnp.bfloat16),
+        ],
+        1,
+    )
+    out_o = jnp.concatenate([out_proj, o_proj], 0)
+    conv_w, zqd_w, oo_w, gate_w, up_w, down_w = gathered(
+        [
+            (in_proj, DS, DS + 2 * NS),
+            (z_qkv_dt, 0, z_qkv_dt.shape[1]),
+            (out_o, 0, D),
+            (gate_up, 0, FF),
+            (gate_up, FF, FF),
+            (down_proj, 0, D),
+        ],
+        idx,
+        my_index // 2,
+        core,
+        layer,
+    )
+    qkv_end = DS + (HQ + 2 * HK) * HA
+
+    def interleaved(mixed_in, attended_in):
+        return jnp.concatenate(
+            [
+                mixed_in.reshape(length, layers, DS // layers),
+                attended_in.reshape(length, layers, HQ * HA // layers),
+            ],
+            2,
+        ).reshape(length, DS + HQ * HA)
+
+    def parted(both):
+        both = both.reshape(length, layers, (DS + HQ * HA) // layers)
+        return (
+            both[:, :, : DS // layers].reshape(length, DS),
+            both[:, :, DS // layers :].reshape(length, HQ * HA),
+        )
+
     normed_in, norm_pull = jax.vjp(normed, hidden, first_gain)
     input_low = normed_in.astype(jnp.bfloat16)
-    projected = project(input_low, full_in)
-    step_raw = project(input_low, full_dt)
-    attn_in = project(input_low, full_qkv)
-    gate_z = projected[:, :DS]
-    conv_low = projected[:, DS:].astype(jnp.bfloat16)
+    conv_low = forth(idx, input_low, conv_w, jnp.bfloat16)
+    zqd_out = forth(idx, input_low, zqd_w)
+    gate_z = zqd_out[:, :DS]
+    attn_in = zqd_out[:, DS:qkv_end]
+    step_raw = zqd_out[:, qkv_end : qkv_end + NH]
     tail_low = from_behind(conv_low[length - (KC - 1) :], "ctx", 1)
 
     def front_fn(conv_in, tail_in, shift_in, kernel_in, bias_in, bias_step, log_rate):
@@ -234,8 +589,7 @@
     )
     y_part, local_state, states_x, c_matrix, log_decay = front_out
     decay_now, decay_pull = jax.vjp(lambda log_in: block_decay(log_in, own_ids, prev_id), log_decay)
-    identity = (jnp.ones_like(decay_now), jnp.zeros_like(local_state))
-    state_in = carried_in((decay_now, local_state), "ctx", combine, identity)[1]
+    state_in = entering(decay_now, local_state, my_index, False)
     y_carry, carry_pull = jax.vjp(
         lambda c_in, log_in, state_arg: ssm_carry(c_in, log_in, own_ids, prev_id, state_arg),
         c_matrix,
@@ -246,7 +600,6 @@
         mixer_tail, y_part + y_carry, states_x, gate_z, d_skip, mixer_gain
     )
     mixer_low = mixer_normed.astype(jnp.bfloat16)
-    mixer_out = project(mixer_low, full_out)
     groups = HQ // HK
     scale = HA ** (-0.5)
     query_low = rotate(attn_in[:, : HQ * HA].reshape(length, HQ, HA), places, 1.0).astype(
@@ -258,9 +611,11 @@
     value_low = attn_in[:, (HQ + HK) * HA :].reshape(length, HK, HA).astype(jnp.bfloat16)
     query_groups = query_low.reshape(length, HK, groups, HA)
     top_now = jnp.full((HK, groups, length), -1e30, jnp.float32)
-    key_piece = lax.all_gather(key_low, "ctx", axis=0, tiled=True)
-    value_piece = lax.all_gather(value_low, "ctx", axis=0, tiled=True)
-    key_ids = lax.all_gather(own_ids, "ctx", axis=0, tiled=True)
+    both_all = lax.all_gather(
+        jnp.concatenate([key_low, value_low], 1), "ctx", axis=0, tiled=True
+    )
+    key_piece, value_piece = both_all[:, :HK], both_all[:, HK:]
+    key_ids = all_ids
     width = key_piece.shape[0]
     key_places = jnp.arange(width, dtype=jnp.int32)
     score = (
@@ -282,38 +637,25 @@
     attended = accum / jnp.transpose(total, (2, 0, 1))[..., None]
     log_total = top_now + jnp.log(total)
     attended_low = attended.reshape(length, HQ * HA).astype(jnp.bfloat16)
-    attn_out = project(attended_low, full_o)
-    middle = hidden + mixer_out + attn_out
+    branches_low = interleaved(mixer_low, attended_low)
+    middle = hidden + forth(idx, branches_low, oo_w)
     normed_mid, mid_pull = jax.vjp(normed, middle, second_gain)
     mid_low = normed_mid.astype(jnp.bfloat16)
-    gate_up_out = project(mid_low, full_gu)
+    gate_up_out = jnp.concatenate([forth(idx, mid_low, gate_w), forth(idx, mid_low, up_w)], 1)
     act_value, act_pull = jax.vjp(swiglu, gate_up_out)
     act_low = act_value.astype(jnp.bfloat16)
-    mixed = middle + project(act_low, full_down)
-    full_in, full_dt, full_out, full_qkv, full_o, full_gu, full_down = (
-        lax.all_gather(in_proj, "fsdp", axis=0, tiled=True),
-        lax.all_gather(dt_proj, "fsdp", axis=0, tiled=True),
-        lax.all_gather(out_proj, "fsdp", axis=0, tiled=True),
-        lax.all_gather(qkv_proj, "fsdp", axis=0, tiled=True),
-        lax.all_gather(o_proj, "fsdp", axis=0, tiled=True),
-        lax.all_gather(gate_up, "fsdp", axis=0, tiled=True),
-        lax.all_gather(down_proj, "fsdp", axis=0, tiled=True),
-    )
+    mixed = middle + forth(idx, act_low, down_w)
     grad_low = grad_out.astype(jnp.bfloat16)
-    d_act = project_back(grad_low, full_down)
+    d_act = back(idx, grad_low, down_w)
     gu_low = act_pull(d_act)[0].astype(jnp.bfloat16)
-    d_mid_norm = project_back(gu_low, full_gu)
+    d_mid_norm = back(idx, gu_low[:, :FF], gate_w) + back(idx, gu_low[:, FF:], up_w)
     d_middle_part, d_second_gain = mid_pull(d_mid_norm)
     d_middle = grad_out + d_middle_part
     branch_low = d_middle.astype(jnp.bfloat16)
-    d_mixer_norm = project_back(branch_low, full_out)
-    d_attended = project_back(branch_low, full_o)
+    d_mixer_norm, d_attended = parted(back(idx, branch_low, oo_w))
     d_out_low = d_attended.reshape(length, HK, groups, HA).astype(jnp.bfloat16)
     delta = jnp.transpose(jnp.sum(d_out_low.astype(jnp.float32) * attended, axis=-1), (1, 2, 0))
-    keys_all, values_all = (
-        lax.all_gather(key_low, "ctx", axis=0, tiled=True),
-        lax.all_gather(value_low, "ctx", axis=0, tiled=True),
-    )
+    keys_all, values_all = key_piece, value_piece
     seq_len = keys_all.shape[0]
     block = min(seq_len, 512)
 
@@ -380,7 +722,7 @@
     qkv_low = d_attn_in.astype(jnp.bfloat16)
     d_core, d_states_tail, d_gate_z, d_d_skip, d_mixer_gain = tail_pull(d_mixer_norm)
     d_c_carry, d_log_carry, d_state_in = carry_pull(d_core)
-    later_grad = prefix((decay_now, d_state_in), "ctx", combine, identity)[1]
+    later_grad = entering(decay_now, d_state_in, my_index, True)
     d_decay = jnp.sum(later_grad * state_in, axis=(1, 2))
     d_log_decay = decay_pull(d_decay)[0]
     d_conv_in, d_tail, d_step_raw, d_conv_weight, d_conv_bias, d_dt_bias, d_a_log = front_pull(
@@ -390,48 +732,45 @@
     d_conv_in = jnp.concatenate(
         [d_conv_in[: length - (KC - 1)], d_conv_in[length - (KC - 1) :] + from_next], 0
     )
-    proj_low = jnp.concatenate([d_gate_z, d_conv_in], 1).astype(jnp.bfloat16)
+    z_low = d_gate_z.astype(jnp.bfloat16)
+    blank = jnp.zeros((length, 512 - NH), jnp.bfloat16)
+    conv_grad_low = d_conv_in.astype(jnp.bfloat16)
     step_low = d_step_raw.astype(jnp.bfloat16)
-    d_normed_in = (
-        project_back(proj_low, full_in)
-        + project_back(step_low, full_dt)
-        + project_back(qkv_low, full_qkv)
+    d_normed_in = back(idx, conv_grad_low, conv_w) + back(
+        idx, jnp.concatenate([z_low, qkv_low, step_low, blank], 1), zqd_w
     )
     d_hidden_part, d_first_gain = norm_pull(d_normed_in)
     d_tokens = d_middle + d_hidden_part
 
     def weight_grad(act_in, grad_in):
-        return lax.psum_scatter(
-            lax.dot_general(
-                act_in, grad_in, (((0,), (0,)), ((), ())), preferred_element_type=jnp.float32
-            ).astype(jnp.bfloat16),
-            "fsdp",
-            scatter_dimension=0,
-            tiled=True,
-        ).astype(jnp.float32)
-
-    shards = [
-        weight_grad(act_in, grad_in)
-        for act_in, grad_in in (
-            (input_low, proj_low),
-            (input_low, step_low),
-            (mixer_low, branch_low),
-            (input_low, qkv_low),
-            (attended_low, branch_low),
-            (mid_low, gu_low),
-            (act_low, grad_low),
-        )
-    ]
+        part = lax.dot_general(
+            act_in, grad_in, (((0,), (0,)), ((), ())), preferred_element_type=jnp.float32
+        ).astype(jnp.bfloat16)
+        return plane_sum(part, my_index, core)
+
+    input_mine = dealt(input_low, layer)
+    down_pair = weight_grad(dealt(act_low, layer), every(grad_low))
+    gate_up_pair = weight_grad(dealt(mid_low, layer), every(gu_low))
+    oo_pair = weight_grad(dealt(branches_low, layer), every(branch_low))
+    z_pair = weight_grad(input_mine, every(z_low))
+    qkv_pair = weight_grad(input_mine, every(qkv_low))
+    tail_cols = DS + 2 * NS
+    tail_pair = weight_grad(
+        input_mine, every(jnp.concatenate([conv_grad_low, step_low, blank[:, : 256 - NH]], 1))
+    )
+    tail_half = tail_pair[0].shape[1]
     summed = (
-        lax.psum(shards[0].astype(jnp.bfloat16), "ctx").astype(jnp.float32),
-        lax.psum(shards[1].astype(jnp.bfloat16), "ctx").astype(jnp.float32),
-        lax.psum(shards[2].astype(jnp.bfloat16), "ctx").astype(jnp.float32),
-        lax.psum(shards[3].astype(jnp.bfloat16), "ctx").astype(jnp.float32),
-        lax.psum(shards[4].astype(jnp.bfloat16), "ctx").astype(jnp.float32),
-        lax.psum(shards[5].astype(jnp.bfloat16), "ctx").astype(jnp.float32),
-        lax.psum(shards[6].astype(jnp.bfloat16), "ctx").astype(jnp.float32),
-    )
-    smalls = lax.psum(
+        finished(idx, [z_pair, tail_pair], [DS, tail_cols]),
+        jnp.where(core == 1, tail_pair[0], tail_pair[1])[
+            :, tail_cols - tail_half : tail_cols - tail_half + NH
+        ].astype(jnp.float32),
+        finished(idx, [oo_pair], [D], 0, DS // layers),
+        finished(idx, [qkv_pair], [(HQ + 2 * HK) * HA]),
+        finished(idx, [oo_pair], [D], DS // layers, HQ * HA // layers),
+        finished(idx, [gate_up_pair], [2 * FF]),
+        finished(idx, [down_pair], [D]),
+    )
+    smalls = sum_of_all(
         (
             d_conv_weight,
             d_conv_bias,
@@ -441,8 +780,7 @@
             d_mixer_gain,
             d_first_gain,
             d_second_gain,
-        ),
-        ("ctx", "fsdp"),
+        )
     )
     return (
         mixed[None].astype(jnp.bfloat16),

time: 4200 us -> 1460 us (0.35)
  waiting for transfers between devices: 3600 us -> 675 us
  Pallas kernels: 0 us -> 188 us
  matrix products: 274 us -> 109 us
  starting transfers between devices: 4.9 us -> 132 us
  local copies, waits for them, and re-layouts: 68.2 us -> 177 us
  blocking collectives: 91 us -> 0 us
    all_gather x8 -> x13, waiting for transfers between devices: 1630 us -> 117 us  [the longest x6 62.3 us: every(): return lax.all_gather(block, 'fsdp', axis=0, tiled=True)]
    reduce_scatter x6 -> x0, waiting for transfers between devices: 1040 us -> none  [weight_grad(): lax.psum_scatter(lax.dot_general(act_in, grad_in, (((0,), (0,)), ((), ())...]
    unnamed x19 -> x14, waiting for transfers between devices: 559 us -> 1.42 us
    ppermute x0 -> x120, waiting for transfers between devices: none -> 550 us  [the longest x103 435 us: swap(): return lax.ppermute(block, 'ctx', [(i, i ^ distance) for i in range(peers)])]
    psum x2 -> x0, waiting for transfers between devices: 369 us -> none  [the longest x1 271 us: body(): lax.psum(shards[0].astype(jnp.bfloat16), 'ctx').astype(jnp.float32)]
    pallas_call x0 -> x24, Pallas kernels: none -> 188 us  [the longest x6 67.6 us: back(): pl.pallas_call(back_kernel, grid_spec=pltpu.PrefetchScalarGridSpec(num_sc...]
    dot_general x14 -> x0, matrix products: 138 us -> none  [the longest x7 76.1 us: project_back(): lax.dot_general(grad_in, weight, (((1,), (1,)), ((), ())), preferred_elem...]
    ppermute x0 -> x120, starting transfers between devices: none -> 128 us  [the longest x103 96.5 us: swap(): return lax.ppermute(block, 'ctx', [(i, i ^ distance) for i in range(peers)])]
  transfers between devices with their start and end apart: 20 -> 136, of which waited for: 17 -> 52; matrix products, arithmetic and copies ran while one was open for 9% -> 23% of each run, Pallas kernels for 0% -> 8%
where the time goes in v1:
time: 1460 us; the launch traced here: 1450 us
  waiting for transfers between devices  675 us (46%)
  Pallas kernels  188 us (13%)
  local copies, waits for them, and re-layouts  177 us (12%)
  other arithmetic  151 us (10%)
  starting transfers between devices  132 us (9%)
  matrix products  109 us (7%)
  between operations  19.4 us (1%)
    ppermute x103, waiting for transfers between devices, swap(): return lax.ppermute(block, 'ctx', [(i, i ^ distance) for i in range(peers)])  435 us
    ppermute x103, starting transfers between devices, swap(): return lax.ppermute(block, 'ctx', [(i, i ^ distance) for i in range(peers)])  96.5 us
    ppermute x12, waiting for transfers between devices, shifted(): lax.ppermute(block, 'fsdp', [(i, (i + hops) % peers) for i in range(peers)])  94.3 us
    unnamed x539, local copies, waits for them, and re-layouts  93 us
    pallas_call x6, Pallas kernels, back(): pl.pallas_call(back_kernel, grid_spec=pltpu.PrefetchScalarGridSpec(num_sc...  67.6 us
    all_gather x6, waiting for transfers between devices, every(): return lax.all_gather(block, 'fsdp', axis=0, tiled=True)  62.3 us
    pallas_call x6, Pallas kernels, forth(): pl.pallas_call(forth_kernel, grid_spec=pltpu.PrefetchScalarGridSpec(num_s...  52.9 us
    all_gather x5, waiting for transfers between devices, gathered(): along[turn + 1] = lax.all_gather(pieces[turn + 1], 'fsdp')  35.6 us
  transfers between devices with their start and end apart: 136, of which 52 were waited for; matrix products, arithmetic and copies ran while one was open for 23% of the time, Pallas kernels for 8%

profile of v1, /device:TPU:0, one launch (start us, length us, event | category | flops | bytes accessed | tf_op | source)
XLA Modules:
  0.0 1452.8 jit_solution(16466728884814995751)
XLA Ops:
  15.3 7.9 concatenate.300.refs_1_
  38.2 19.4 %all-gather.33.cloned.1.call-done = bf16[512,1792]{1,0:T(8,128)(2,1)} async-done(((bf16[128,1792]{1,0:T(8,128)(2,1)}), bf16[512,1792]{1,0:T(8,128)(2,1)}) %all-gather.33.cloned.1.call-update) | async-done | bytes 1835024 | tf_op jit(solution)/shard_map/all_gather | solution.py:255
  62.5 14.2 collective-permute-done.refs_3_
  77.9 35.6 %all-gather.35.cloned.1.call-done = bf16[512,2560]{1,0:T(8,128)(2,1)} async-done(((bf16[128,2560]{1,0:T(8,128)(2,1)}), bf16[512,2560]{1,0:T(8,128)(2,1)}) %all-gather.35.cloned.1.call-update) | async-done | bytes 2621456 | tf_op jit(solution)/shard_map/all_gather | solution.py:273
  118.9 49.3 %collective-permute-done.4.refs_3_ = bf16[3,128,1280]{2,1,0:T(8,128)(2,1)S(1)} collective-permute-done((bf16[3,128,1280]{2,1,0:T(8,128)(2,1)S(1)}, bf16[3,128,1280]{2,1,0:T(8,128)(2,1)S(1)}, u32[]{:S(2)}, u32[]{:S(2)}) %collective-permute-start.4) | collective-permute-done | bytes 983072 | tf_op jit(solution)/shard_map/ppermute | solution.py:120
  176.6 56.4 %collective-permute-done.8.refs_3_ = bf16[3,256,512]{2,1,0:T(8,128)(2,1)S(1)} collective-permute-done((bf16[3,256,512]{2,1,0:T(8,128)(2,1)S(1)}, bf16[3,256,512]{2,1,0:T(8,128)(2,1)S(1)}, u32[]{:S(2)}, u32[]{:S(2)}) %collective-permute-start.8) | collective-permute-done | bytes 786464 | tf_op jit(solution)/shard_map/ppermute | solution.py:120
  264.9 17.7 %collective-permute-done.24.refs_3_ = bf16[3,128,1024]{2,1,0:T(8,128)(2,1)S(1)} collective-permute-done((bf16[3,128,1024]{2,1,0:T(8,128)(2,1)S(1)}, bf16[3,128,1024]{2,1,0:T(8,128)(2,1)S(1)}, u32[]{:S(2)}, u32[]{:S(2)}) %collective-permute-start.24) | collective-permute-done | bytes 786464 | tf_op jit(solution)/shard_map/ppermute | solution.py:120
  283.9 30.2 %collective-permute-done.25.refs_6_ = bf16[3,128,1024]{2,1,0:T(8,128)(2,1)S(1)} collective-permute-done((bf16[3,128,1024]{2,1,0:T(8,128)(2,1)S(1)}, bf16[3,128,1024]{2,1,0:T(8,128)(2,1)S(1)}, u32[]{:S(2)}, u32[]{:S(2)}) %collective-permute-start.25) | collective-permute-done | bytes 786464 | tf_op jit(solution)/shard_map/ppermute | solution.py:120
  327.5 47.7 %collective-permute-done.29.refs_3_ = bf16[3,128,1024]{2,1,0:T(8,128)(2,1)S(1)} collective-permute-done((bf16[3,128,1024]{2,1,0:T(8,128)(2,1)S(1)}, bf16[3,128,1024]{2,1,0:T(8,128)(2,1)S(1)}, u32[]{:S(2)}, u32[]{:S(2)}) %collective-permute-start.29) | collective-permute-done | bytes 786464 | tf_op jit(solution)/shard_map/ppermute | solution.py:120
  377.4 16.6 %collective-permute-done.30.refs_6_ = bf16[3,128,1024]{2,1,0:T(8,128)(2,1)S(1)} collective-permute-done((bf16[3,128,1024]{2,1,0:T(8,128)(2,1)S(1)}, bf16[3,128,1024]{2,1,0:T(8,128)(2,1)S(1)}, u32[]{:S(2)}, u32[]{:S(2)}) %collective-permute-start.30) | collective-permute-done | bytes 786464 | tf_op jit(solution)/shard_map/ppermute | solution.py:120
  401.7 8.4 forth.7
  413.1 19.5 %collective-permute-done.15 = s32[4,128]{1,0:T(4,128)S(1)} collective-permute-done((s32[4,128]{1,0:T(4,128)S(1)}, s32[4,128]{1,0:T(4,128)S(1)}, u32[]{:S(2)}, u32[]{:S(2)}) %collective-permute-start.15) | collective-permute-done | bytes 2080 | tf_op jit(solution)/shard_map/ppermute | solution.py:120
  468.1 10.5 forth.6
  511.8 8.5 collective-permute-done.16
  531.0 17.7 %collective-permute-done.19 = bf16[24,64,256]{2,1,0:T(8,128)(2,1)} collective-permute-done((bf16[24,64,256]{2,1,0:T(8,128)(2,1)}, bf16[24,64,256]{2,1,0:T(8,128)(2,1)}, u32[]{:S(2)}, u32[]{:S(2)}) %collective-permute-start.19) | collective-permute-done | bytes 786464 | tf_op jit(solution)/shard_map/ppermute | solution.py:120
  556.2 15.4 %collective-permute-done.20 = bf16[24,64,256]{2,1,0:T(8,128)(2,1)} collective-permute-done((bf16[24,64,256]{2,1,0:T(8,128)(2,1)}, bf16[24,64,256]{2,1,0:T(8,128)(2,1)}, u32[]{:S(2)}, u32[]{:S(2)}) %collective-permute-start.20) | collective-permute-done | bytes 786464 | tf_op jit(solution)/shard_map/ppermute | solution.py:120
  586.3 7.6 fusion.59
  605.2 9.0 forth.8
  615.4 9.3 forth.9
  624.7 9.3 forth.10
  634.0 10.0 back.6
  649.7 11.1 back.7
  660.7 11.3 back.8
  682.7 12.6 back.9
  704.4 24.8 %while.13 = (s32[]{:T(128)}, f32[128,2,4,128]{0,3,2,1:T(8,128)}, bf16[2,512,512]{1,2,0:T(8,128)(2,1)}, s32[2]{0:T(128)S(1)}, bf16[1024,2,128]{2,0,1:T(8,128)(2,1...) while((s32[]{:T(128)}, f32[128,2,4,128]{0,3,2,1:T(8,128)}, ...), condition=%wide.region_12.13_spmd.clone, body=%wide.region_11.12_spmd.clone.sunk | while | flops 676397696 | bytes 39210924 | solution.py:701
  800.4 31.9 %collective-permute-done.98 = bf16[128,512]{1,0:T(8,128)(2,1)S(1)} collective-permute-done((bf16[128,512]{1,0:T(8,128)(2,1)S(1)}, bf16[128,512]{1,0:T(8,128)(2,1)S(1)}, u32[]{:S(2)}, u32[]{:S(2)}) %collective-permute-start.98) | collective-permute-done | bytes 131104 | tf_op jit(solution)/shard_map/ppermute | solution.py:125
  854.4 9.9 collective-permute-start.110
  871.5 8.7 collective-permute-done.109
  881.0 30.9 %collective-permute-done.110 = bf16[128,1024]{1,0:T(8,128)(2,1)S(1)} collective-permute-done((bf16[128,1024]{1,0:T(8,128)(2,1)S(1)}, bf16[128,1024]{1,0:T(8,128)(2,1)S(1)}, u32[]{:S(2)}, u32[]{:S(2)}) %collective-permute-start.110) | collective-permute-done | bytes 262176 | tf_op jit(solution)/shard_map/ppermute | solution.py:125
  930.1 7.7 fusion.44
  958.2 7.0 collective-permute-done.41
  980.0 8.3 collective-permute-done.42
  1023.4 8.2 fusion.99
  1062.9 12.7 back.11
  1076.9 10.0 back.10
  1102.6 12.5 collective-permute-done.71
  1144.8 8.6 collective-permute-done.77
  1167.2 8.1 convolution_convert_fusion
  1181.9 62.3 %all-gather.25.cloned.1.call-done = bf16[512,3840]{1,0:T(8,128)(2,1)} async-done(((bf16[128,3840]{1,0:T(8,128)(2,1)}), bf16[512,3840]{1,0:T(8,128)(2,1)}) %all-gather.25.cloned.1.call-update) | async-done | bytes 3932176 | tf_op jit(solution)/shard_map/all_gather | solution.py:395
  1254.8 9.9 collective-permute-done.84
  1286.4 18.6 %collective-permute-done.100 = bf16[128,4096]{1,0:T(8,128)(2,1)S(1)} collective-permute-done((bf16[128,4096]{1,0:T(8,128)(2,1)S(1)}, bf16[128,4096]{1,0:T(8,128)(2,1)S(1)}, u32[]{:S(2)}, u32[]{:S(2)}) %collective-permute-start.100) | collective-permute-done | bytes 1048608 | tf_op jit(solution)/shard_map/ppermute | solution.py:120
  1309.8 10.9 collective-permute-done.105
  1324.2 9.7 collective-permute-done.106
  1344.1 18.7 %collective-permute-done.107 = bf16[128,4096]{1,0:T(8,128)(2,1)S(1)} collective-permute-done((bf16[128,4096]{1,0:T(8,128)(2,1)S(1)}, bf16[128,4096]{1,0:T(8,128)(2,1)S(1)}, u32[]{:S(2)}, u32[]{:S(2)}) %collective-permute-start.107) | collective-permute-done | bytes 1048608 | tf_op jit(solution)/shard_map/ppermute | solution.py:120
  1376.9 10.1 collective-permute-done.66
  1390.6 7.1 collective-permute-done.56
  1428.3 8.3 finish.6
  1436.6 9.4 finish.10
  (1153 shorter events, 647.1 us)
Async XLA Ops:
  13.4 100.1 %all-gather.35.cloned.1.call-start = ((), (), s32[]{:S(2)}) async-start(), calls=%async_computation.9 | async-start | bytes 3276800 | tf_op jit(solution)/shard_map/all_gather | solution.py:273
  57.7 113.7 %all-gather.37.cloned.1.call-start = ((), (), s32[]{:S(2)}) async-start(), calls=%async_computation.10 | async-start | bytes 2621440 | tf_op jit(solution)/shard_map/all_gather | solution.py:273
  113.5 123.2 %all-gather.39.cloned.1.call-start = ((), (), s32[]{:S(2)}) async-start(), calls=%async_computation.11 | async-start | bytes 2621440 | tf_op jit(solution)/shard_map/all_gather | solution.py:273
  113.8 55.5 %collective-permute-start.2 = (bf16[6,128,896]{2,1,0:T(8,128)(2,1)S(1)}, bf16[6,128,896]{2,1,0:T(8,128)(2,1)S(1)}, u32[]{:S(2)}, u32[]{:S(2)}) collective-permute-start(bf16[6,128,896]{2,1,0:T(8,128)(2,1)S(1)} %pad_maximum_fusion.23), channel_id=1, source_target_pairs={{0,16},{4,20},{8,24},{12,28},{16,0},{20,4},{24,8},{28,12},{1,17},{... | collective-permute-start | bytes 4128776 | tf_op jit(solution)/shard_map/ppermute | solution.py:120
  115.5 54.8 %collective-permute-start.3 = (bf16[6,128,896]{2,1,0:T(8,128)(2,1)S(1)}, bf16[6,128,896]{2,1,0:T(8,128)(2,1)S(1)}, u32[]{:S(2)}, u32[]{:S(2)}) collective-permute-start(bf16[6,128,896]{2,1,0:T(8,128)(2,1)S(1)} %pad_maximum_fusion.24), channel_id=1, source_target_pairs={{0,8},{4,12},{8,0},{12,4},{16,24},{20,28},{24,16},{28,20},{1,9},{5... | collective-permute-start | bytes 4128776 | tf_op jit(solution)/shard_map/ppermute | solution.py:120
  171.4 145.0 %all-gather.41.cloned.1.call-start = ((), (), s32[]{:S(2)}) async-start(), calls=%async_computation.12 | async-start | bytes 2621440 | tf_op jit(solution)/shard_map/all_gather | solution.py:273
  171.7 61.4 %collective-permute-start.6 = (bf16[6,128,1280]{2,1,0:T(8,128)(2,1)S(1)}, bf16[6,128,1280]{2,1,0:T(8,128)(2,1)S(1)}, u32[]{:S(2)}, u32[]{:S(2)}) collective-permute-start(bf16[6,128,1280]{2,1,0:T(8,128)(2,1)S(1)} %pad_maximum_fusion.6), channel_id=1, source_target_pairs={{0,16},{4,20},{8,24},{12,28},{16,0},{20,4},{24,8},{28,12},{1,17},{... | collective-permute-start | bytes 5898248 | tf_op jit(solution)/shard_map/ppermute | solution.py:120
  172.8 62.7 %collective-permute-start.7 = (bf16[6,128,1280]{2,1,0:T(8,128)(2,1)S(1)}, bf16[6,128,1280]{2,1,0:T(8,128)(2,1)S(1)}, u32[]{:S(2)}, u32[]{:S(2)}) collective-permute-start(bf16[6,128,1280]{2,1,0:T(8,128)(2,1)S(1)} %pad_maximum_fusion.7), channel_id=1, source_target_pairs={{0,8},{4,12},{8,0},{12,4},{16,24},{20,28},{24,16},{28,20},{1,9},{5... | collective-permute-start | bytes 5898248 | tf_op jit(solution)/shard_map/ppermute | solution.py:120
  174.8 58.3 %collective-permute-start.8 = (bf16[3,256,512]{2,1,0:T(8,128)(2,1)S(1)}, bf16[3,256,512]{2,1,0:T(8,128)(2,1)S(1)}, u32[]{:S(2)}, u32[]{:S(2)}) collective-permute-start(bf16[3,256,512]{2,1,0:T(8,128)(2,1)S(1)} %get-tuple-element.208.refs_2_), channel_id=1, source_target_pairs={{0,8},{4,12},{8,0},{12,4},{16,24},{20,28},{24,16},{28,20},{1,9},{5... | collective-permute-start | bytes 2359304 | tf_op jit(solution)/shard_map/ppermute | solution.py:120
  175.5 57.6 %collective-permute-start.9 = (bf16[3,256,512]{2,1,0:T(8,128)(2,1)S(1)}, bf16[3,256,512]{2,1,0:T(8,128)(2,1)S(1)}, u32[]{:S(2)}, u32[]{:S(2)}) collective-permute-start(bf16[3,256,512]{2,1,0:T(8,128)(2,1)S(1)} %get-tuple-element.211.refs_5_), channel_id=1, source_target_pairs={{0,16},{4,20},{8,24},{12,28},{16,0},{20,4},{24,8},{28,12},{1,17},{... | collective-permute-start | bytes 2359304 | tf_op jit(solution)/shard_map/ppermute | solution.py:120
  254.0 210.2 %collective-permute-start.10 = (bf16[2048,2560]{1,0:T(8,128)(2,1)}, bf16[2048,2560]{1,0:T(8,128)(2,1)}, u32[]{:S(2)}, u32[]{:S(2)}) collective-permute-start(bf16[2048,2560]{1,0:T(8,128)(2,1)} %place.6.own_ref), channel_id=1, source_target_pairs={{0,4},{4,0},{8,12},{12,8},{16,20},{20,16},{24,28},{28,24},{1,5},{5... | collective-permute-start | bytes 31457288 | tf_op jit(solution)/shard_map/ppermute | solution.py:120
  258.6 143.1 %collective-permute-start.11 = (bf16[2048,1792]{1,0:T(8,128)(2,1)}, bf16[2048,1792]{1,0:T(8,128)(2,1)}, u32[]{:S(2)}, u32[]{:S(2)}) collective-permute-start(bf16[2048,1792]{1,0:T(8,128)(2,1)} %place.7.own_ref), channel_id=1, source_target_pairs={{0,4},{4,0},{8,12},{12,8},{16,20},{20,16},{24,28},{28,24},{1,5},{5... | collective-permute-start | bytes 22020104 | tf_op jit(solution)/shard_map/ppermute | solution.py:120
  259.2 137.2 %all-gather.43.cloned.1.call-start = ((), (), s32[]{:S(2)}) async-start(), calls=%async_computation.13 | async-start | bytes 2621440 | tf_op jit(solution)/shard_map/all_gather | solution.py:273
  260.8 53.3 %collective-permute-start.22 = (bf16[6,256,512]{2,1,0:T(8,128)(2,1)S(1)}, bf16[6,256,512]{2,1,0:T(8,128)(2,1)S(1)}, u32[]{:S(2)}, u32[]{:S(2)}) collective-permute-start(bf16[6,256,512]{2,1,0:T(8,128)(2,1)S(1)} %pad_maximum_fusion.10), channel_id=1, source_target_pairs={{0,16},{4,20},{8,24},{12,28},{16,0},{20,4},{24,8},{28,12},{1,17},{... | collective-permute-start | bytes 4718600 | tf_op jit(solution)/shard_map/ppermute | solution.py:120
  316.5 236.9 %all-gather.21.cloned.1.call-start = ((), (), s32[]{:S(2)}) async-start(), calls=%async_computation.1 | async-start | bytes 1179648 | tf_op jit(solution)/shard_map/all_gather | solution.py:614
  319.2 77.2 %collective-permute-start.27 = (bf16[6,128,1024]{2,1,0:T(8,128)(2,1)}, bf16[6,128,1024]{2,1,0:T(8,128)(2,1)}, u32[]{:S(2)}, u32[]{:S(2)}) collective-permute-start(bf16[6,128,1024]{2,1,0:T(8,128)(2,1)} %pad_maximum_fusion.13), channel_id=1, source_target_pairs={{0,16},{4,20},{8,24},{12,28},{16,0},{20,4},{24,8},{28,12},{1,17},{... | collective-permute-start | bytes 4718600 | tf_op jit(solution)/shard_map/ppermute | solution.py:120
  321.6 74.8 %collective-permute-start.28 = (bf16[6,128,1024]{2,1,0:T(8,128)(2,1)}, bf16[6,128,1024]{2,1,0:T(8,128)(2,1)}, u32[]{:S(2)}, u32[]{:S(2)}) collective-permute-start(bf16[6,128,1024]{2,1,0:T(8,128)(2,1)} %pad_maximum_fusion.14), channel_id=1, source_target_pairs={{0,8},{4,12},{8,0},{12,4},{16,24},{20,28},{24,16},{28,20},{1,9},{5... | collective-permute-start | bytes 4718600 | tf_op jit(solution)/shard_map/ppermute | solution.py:120
  323.7 51.5 %collective-permute-start.29 = (bf16[3,128,1024]{2,1,0:T(8,128)(2,1)S(1)}, bf16[3,128,1024]{2,1,0:T(8,128)(2,1)S(1)}, u32[]{:S(2)}, u32[]{:S(2)}) collective-permute-start(bf16[3,128,1024]{2,1,0:T(8,128)(2,1)S(1)} %get-tuple-element.231.refs_2_), channel_id=1, source_target_pairs={{0,8},{4,12},{8,0},{12,4},{16,24},{20,28},{24,16},{28,20},{1,9},{5... | collective-permute-start | bytes 2359304 | tf_op jit(solution)/shard_map/ppermute | solution.py:120
  397.7 53.9 %collective-permute-start.32 = (bf16[6,128,1024]{2,1,0:T(8,128)(2,1)}, bf16[6,128,1024]{2,1,0:T(8,128)(2,1)}, u32[]{:S(2)}, u32[]{:S(2)}) collective-permute-start(bf16[6,128,1024]{2,1,0:T(8,128)(2,1)} %pad_maximum_fusion.16), channel_id=1, source_target_pairs={{0,16},{4,20},{8,24},{12,28},{16,0},{20,4},{24,8},{28,12},{1,17},{... | collective-permute-start | bytes 4718600 | tf_op jit(solution)/shard_map/ppermute | solution.py:120
  399.9 51.7 %collective-permute-start.33 = (bf16[6,128,1024]{2,1,0:T(8,128)(2,1)}, bf16[6,128,1024]{2,1,0:T(8,128)(2,1)}, u32[]{:S(2)}, u32[]{:S(2)}) collective-permute-start(bf16[6,128,1024]{2,1,0:T(8,128)(2,1)} %pad_maximum_fusion.17), channel_id=1, source_target_pairs={{0,8},{4,12},{8,0},{12,4},{16,24},{20,28},{24,16},{28,20},{1,9},{5... | collective-permute-start | bytes 4718600 | tf_op jit(solution)/shard_map/ppermute | solution.py:120
  451.6 153.6 %collective-permute-start.26 = (bf16[4096,1024]{1,0:T(8,128)(2,1)}, bf16[4096,1024]{1,0:T(8,128)(2,1)}, u32[]{:S(2)}, u32[]{:S(2)}) collective-permute-start(bf16[4096,1024]{1,0:T(8,128)(2,1)} %place.8.own_ref), channel_id=1, source_target_pairs={{0,4},{4,0},{8,12},{12,8},{16,20},{20,16},{24,28},{28,24},{1,5},{5... | collective-permute-start | bytes 25165832 | tf_op jit(solution)/shard_map/ppermute | solution.py:120
  495.0 120.4 %collective-permute-start.31 = (bf16[2048,2048]{1,0:T(8,128)(2,1)}, bf16[2048,2048]{1,0:T(8,128)(2,1)}, u32[]{:S(2)}, u32[]{:S(2)}) collective-permute-start(bf16[2048,2048]{1,0:T(8,128)(2,1)} %place.9.own_ref), channel_id=1, source_target_pairs={{0,4},{4,0},{8,12},{12,8},{16,20},{20,16},{24,28},{28,24},{1,5},{5... | collective-permute-start | bytes 25165832 | tf_op jit(solution)/shard_map/ppermute | solution.py:120
  502.3 122.4 %collective-permute-start.36 = (bf16[2048,2048]{1,0:T(8,128)(2,1)}, bf16[2048,2048]{1,0:T(8,128)(2,1)}, u32[]{:S(2)}, u32[]{:S(2)}) collective-permute-start(bf16[2048,2048]{1,0:T(8,128)(2,1)} %place.10.own_ref), channel_id=1, source_target_pairs={{0,4},{4,0},{8,12},{12,8},{16,20},{20,16},{24,28},{28,24},{1,5},{5... | collective-permute-start | bytes 25165832 | tf_op jit(solution)/shard_map/ppermute | solution.py:120
  511.4 253.8 %reduce-scatter.2.cloned.1.call-start = ((), (), s32[]{:S(2)}) async-start(), calls=%async_computation.2 | async-start | bytes 1179648 | tf_op jit(solution)/shard_map/reduce_scatter | solution.py:706
  520.4 113.6 %collective-permute-start.39 = (bf16[4096,1024]{1,0:T(8,128)(2,1)}, bf16[4096,1024]{1,0:T(8,128)(2,1)}, u32[]{:S(2)}, u32[]{:S(2)}) collective-permute-start(bf16[4096,1024]{1,0:T(8,128)(2,1)} %copy-done.2), channel_id=1, source_target_pairs={{0,4},{4,0},{8,12},{12,8},{16,20},{20,16},{24,28},{28,24},{1,5},{5... | collective-permute-start | bytes 25165832 | tf_op jit(solution)/shard_map/ppermute | solution.py:120
  731.5 185.7 %all-gather.45.cloned.1.call-start = ((), (), s32[]{:S(2)}) async-start(), calls=%async_computation.14 | async-start | bytes 2621440 | tf_op jit(solution)/shard_map/all_gather | solution.py:395
  732.2 263.0 %all-gather.27.cloned.1.call-start = ((), (), s32[]{:S(2)}) async-start(), calls=%async_computation.5 | async-start | bytes 2621440 | tf_op jit(solution)/shard_map/all_gather | solution.py:395
  732.8 313.3 %all-gather.29.cloned.1.call-start = ((), (), s32[]{:S(2)}) async-start(), calls=%async_computation.6 | async-start | bytes 1966080 | tf_op jit(solution)/shard_map/all_gather | solution.py:395
  771.3 349.5 %all-gather.23.cloned.1.call-start = ((), (), s32[]{:S(2)}) async-start(), calls=%async_computation.3 | async-start | bytes 3932160 | tf_op jit(solution)/shard_map/all_gather | solution.py:395
  781.1 60.5 %collective-permute-start.73 = (bf16[128,1024]{1,0:T(8,128)(2,1)}, bf16[128,1024]{1,0:T(8,128)(2,1)S(1)}, u32[]{:S(2)}, u32[]{:S(2)}) collective-permute-start(bf16[128,1024]{1,0:T(8,128)(2,1)} %get-tuple-element.585), channel_id=1, source_target_pairs={{0,3},{1,0},{2,1},{3,2},{4,7},{5,4},{6,5},{7,6},{8,11},{9,8},{10,9... | collective-permute-start | bytes 786440 | tf_op jit(solution)/shard_map/ppermute | solution.py:125
  782.2 63.7 %collective-permute-start.74 = (bf16[128,1024]{1,0:T(8,128)(2,1)}, bf16[128,1024]{1,0:T(8,128)(2,1)}, u32[]{:S(2)}, u32[]{:S(2)}) collective-permute-start(bf16[128,1024]{1,0:T(8,128)(2,1)} %get-tuple-element.584), channel_id=1, source_target_pairs={{0,2},{1,3},{2,0},{3,1},{4,6},{5,7},{6,4},{7,5},{8,10},{9,11},{10,... | collective-permute-start | bytes 786440 | tf_op jit(solution)/shard_map/ppermute | solution.py:125
  784.0 63.5 %collective-permute-start.75 = (bf16[128,1024]{1,0:T(8,128)(2,1)}, bf16[128,1024]{1,0:T(8,128)(2,1)}, u32[]{:S(2)}, u32[]{:S(2)}) collective-permute-start(bf16[128,1024]{1,0:T(8,128)(2,1)} %get-tuple-element.582), channel_id=1, source_target_pairs={{0,1},{1,2},{2,3},{3,0},{4,5},{5,6},{6,7},{7,4},{8,9},{9,10},{10,1... | collective-permute-start | bytes 786440 | tf_op jit(solution)/shard_map/ppermute | solution.py:125
  840.9 326.3 %all-gather.31.cloned.1.call-start = ((), (), s32[]{:S(2)}) async-start(), calls=%async_computation.7 | async-start | bytes 10485760 | tf_op jit(solution)/shard_map/all_gather | solution.py:395
  854.4 57.4 %collective-permute-start.110 = (bf16[128,1024]{1,0:T(8,128)(2,1)S(1)}, bf16[128,1024]{1,0:T(8,128)(2,1)S(1)}, u32[]{:S(2)}, u32[]{:S(2)}) collective-permute-start(bf16[128,1024]{1,0:T(8,128)(2,1)S(1)} %get-tuple-element.580), channel_id=1, source_target_pairs={{0,2},{1,3},{2,0},{3,1},{4,6},{5,7},{6,4},{7,5},{8,10},{9,11},{10,... | collective-permute-start | bytes 786440 | tf_op jit(solution)/shard_map/ppermute | solution.py:125
  871.5 68.2 %collective-permute-start.40 = (bf16[48,64,256]{2,1,0:T(8,128)(2,1)}, bf16[48,64,256]{2,1,0:T(8,128)(2,1)}, u32[]{:S(2)}, u32[]{:S(2)}) collective-permute-start(bf16[48,64,256]{2,1,0:T(8,128)(2,1)} %get-tuple-element.641), channel_id=1, source_target_pairs={{0,4},{4,0},{8,12},{12,8},{16,20},{20,16},{24,28},{28,24},{1,5},{5... | collective-permute-start | bytes 4718600 | tf_op jit(solution)/shard_map/ppermute | solution.py:120
  951.3 292.9 %all-gather.25.cloned.1.call-start = ((), (), s32[]{:S(2)}) async-start(), calls=%async_computation.4 | async-start | bytes 4915200 | tf_op jit(solution)/shard_map/all_gather | solution.py:395
  1002.2 135.4 %collective-permute-start.76 = (bf16[1024,1024]{1,0:T(8,128)(2,1)}, bf16[1024,1024]{1,0:T(8,128)(2,1)}, u32[]{:S(2)}, u32[]{:S(2)}) collective-permute-start(bf16[1024,1024]{1,0:T(8,128)(2,1)} %broadcast_select_fusion.2), channel_id=1, source_target_pairs={{0,4},{4,0},{8,12},{12,8},{16,20},{20,16},{24,28},{28,24},{1,5},{5... | collective-permute-start | bytes 6291464 | tf_op jit(solution)/shard_map/ppermute | solution.py:120
  1004.3 85.1 %collective-permute-start.120 = (bf16[256,1024]{1,0:T(8,128)(2,1)}, bf16[256,1024]{1,0:T(8,128)(2,1)}, u32[]{:S(2)}, u32[]{:S(2)}) collective-permute-start(bf16[256,1024]{1,0:T(8,128)(2,1)} %maximum_select_fusion.17), channel_id=1, source_target_pairs={{0,16},{4,20},{8,24},{12,28},{16,0},{20,4},{24,8},{28,12},{1,17},{... | collective-permute-start | bytes 1572872 | tf_op jit(solution)/shard_map/ppermute | solution.py:120
  1006.8 85.7 %collective-permute-start.116 = (bf16[256,1024]{1,0:T(8,128)(2,1)}, bf16[256,1024]{1,0:T(8,128)(2,1)}, u32[]{:S(2)}, u32[]{:S(2)}) collective-permute-start(bf16[256,1024]{1,0:T(8,128)(2,1)} %maximum_select_fusion.16), channel_id=1, source_target_pairs={{0,8},{4,12},{8,0},{12,4},{16,24},{20,28},{24,16},{28,20},{1,9},{5... | collective-permute-start | bytes 1572872 | tf_op jit(solution)/shard_map/ppermute | solution.py:120
  1051.0 64.1 %collective-permute-start.86 = (bf16[512,768]{1,0:T(8,128)(2,1)}, bf16[512,768]{1,0:T(8,128)(2,1)}, u32[]{:S(2)}, u32[]{:S(2)}) collective-permute-start(bf16[512,768]{1,0:T(8,128)(2,1)} %broadcast_select_fusion.7), channel_id=1, source_target_pairs={{0,4},{4,0},{8,12},{12,8},{16,20},{20,16},{24,28},{28,24},{1,5},{5... | collective-permute-start | bytes 2359304 | tf_op jit(solution)/shard_map/ppermute | solution.py:120
  1099.5 306.4 %collective-permute-start.121 = (bf16[1024,1024]{1,0:T(8,128)(2,1)}, bf16[1024,1024]{1,0:T(8,128)(2,1)}, u32[]{:S(2)}, u32[]{:S(2)}) collective-permute-start(bf16[1024,1024]{1,0:T(8,128)(2,1)} %pad_maximum_fusion.4.refs_1_), channel_id=1, source_target_pairs={{0,4},{4,0},{8,12},{12,8},{16,20},{20,16},{24,28},{28,24},{1,5},{5... | collective-permute-start | bytes 6291464 | tf_op jit(solution)/shard_map/ppermute | solution.py:120
  1162.2 86.7 %collective-permute-start.79 = (bf16[128,1024]{1,0:T(8,128)(2,1)S(1)}, bf16[128,1024]{1,0:T(8,128)(2,1)}, u32[]{:S(2)}, u32[]{:S(2)}) collective-permute-start(bf16[128,1024]{1,0:T(8,128)(2,1)S(1)} %add_convert_fusion.23), channel_id=1, source_target_pairs={{0,16},{4,20},{8,24},{12,28},{16,0},{20,4},{24,8},{28,12},{1,17},{... | collective-permute-start | bytes 786440 | tf_op jit(solution)/shard_map/ppermute | solution.py:120
  1164.7 85.5 %collective-permute-start.49 = (bf16[128,1536]{1,0:T(8,128)(2,1)}, bf16[128,1536]{1,0:T(8,128)(2,1)}, u32[]{:S(2)}, u32[]{:S(2)}) collective-permute-start(bf16[128,1536]{1,0:T(8,128)(2,1)} %get-tuple-element.564), channel_id=1, source_target_pairs={{0,8},{4,12},{8,0},{12,4},{16,24},{20,28},{24,16},{28,20},{1,9},{5... | collective-permute-start | bytes 1179656 | tf_op jit(solution)/shard_map/ppermute | solution.py:120
  1166.0 85.9 %collective-permute-start.53 = (bf16[128,1536]{1,0:T(8,128)(2,1)}, bf16[128,1536]{1,0:T(8,128)(2,1)}, u32[]{:S(2)}, u32[]{:S(2)}) collective-permute-start(bf16[128,1536]{1,0:T(8,128)(2,1)} %get-tuple-element.565), channel_id=1, source_target_pairs={{0,16},{4,20},{8,24},{12,28},{16,0},{20,4},{24,8},{28,12},{1,17},{... | collective-permute-start | bytes 1179656 | tf_op jit(solution)/shard_map/ppermute | solution.py:120
  1180.7 89.6 %collective-permute-start.99 = (bf16[512,4096]{1,0:T(8,128)(2,1)}, bf16[512,4096]{1,0:T(8,128)(2,1)}, u32[]{:S(2)}, u32[]{:S(2)}) collective-permute-start(bf16[512,4096]{1,0:T(8,128)(2,1)} %broadcast_select_fusion), channel_id=1, source_target_pairs={{0,4},{4,0},{8,12},{12,8},{16,20},{20,16},{24,28},{28,24},{1,5},{5... | collective-permute-start | bytes 12582920 | tf_op jit(solution)/shard_map/ppermute | solution.py:120
  1282.5 86.4 %collective-permute-start.50 = (bf16[64,1536]{1,0:T(8,128)(2,1)S(1)}, bf16[64,1536]{1,0:T(8,128)(2,1)S(1)}, u32[]{:S(2)}, u32[]{:S(2)}) collective-permute-start(bf16[64,1536]{1,0:T(8,128)(2,1)S(1)} %broadcast_select_fusion.27), channel_id=1, source_target_pairs={{0,16},{4,20},{8,24},{12,28},{16,0},{20,4},{24,8},{28,12},{1,17},{... | collective-permute-start | bytes 589832 | tf_op jit(solution)/shard_map/ppermute | solution.py:120
  1284.5 52.3 %collective-permute-start.64 = (bf16[64,1920]{1,0:T(8,128)(2,1)S(1)}, bf16[64,1920]{1,0:T(8,128)(2,1)S(1)}, u32[]{:S(2)}, u32[]{:S(2)}) collective-permute-start(bf16[64,1920]{1,0:T(8,128)(2,1)S(1)} %broadcast_select_fusion.22), channel_id=1, source_target_pairs={{0,8},{4,12},{8,0},{12,4},{16,24},{20,28},{24,16},{28,20},{1,9},{5... | collective-permute-start | bytes 737288 | tf_op jit(solution)/shard_map/ppermute | solution.py:120
  1369.0 67.7 %collective-permute-start.108 = (bf16[512,4096]{1,0:T(8,128)(2,1)}, bf16[512,4096]{1,0:T(8,128)(2,1)}, u32[]{:S(2)}, u32[]{:S(2)}) collective-permute-start(bf16[512,4096]{1,0:T(8,128)(2,1)} %pad_maximum_fusion.1.refs_1_), channel_id=1, source_target_pairs={{0,4},{4,0},{8,12},{12,8},{16,20},{20,16},{24,28},{28,24},{1,5},{5... | collective-permute-start | bytes 12582920 | tf_op jit(solution)/shard_map/ppermute | solution.py:120
  (354 other events, 5169.6 us)
Sparse Core Ops, SparseCore 0:
  13.5 44.0 all-gather.32
  59.8 53.6 all-gather.34
  115.7 44.6 all-gather.36
  171.5 43.9 all-gather.38
  259.3 44.4 all-gather.40
  316.6 44.7 all-gather.42
  511.5 24.8 all-gather.20
  731.6 33.4 reduce-scatter.1
  766.7 78.6 all-gather.44
  846.8 66.7 all-gather.26
  915.2 35.7 all-gather.28
  952.4 62.3 all-gather.22
  1017.0 148.2 all-gather.30
  1167.3 76.8 all-gather.24

commit v2 on v0

v2 whole, which is shorter than its diff:
```python
import jax
import jax.numpy as jnp
from jax import lax
from jax.experimental import pallas as pl
from jax.experimental.pallas import tpu as pltpu
from jax.sharding import PartitionSpec as P

D = 2048
FF = 4096
NH = 48
HP = 64
NS = 256
KC = 4
HQ = 8
HK = 2
HA = 128
DS = 3072


HIGH = lax.Precision.HIGHEST
epsilon = 1e-05
rope_base = 100000000000.0


def from_behind(block, axis, distance):
    devices = range(lax.axis_size(axis))
    route = [(i - distance, i) for i in devices if i - distance in devices]
    return lax.ppermute(block, axis, route)


def normed(operand, gain_vec):
    return (
        operand
        * lax.rsqrt(jnp.mean(operand * operand, axis=-1, keepdims=True) + epsilon)
        * gain_vec
    )


def rotate(operand, places, direction):
    half_width = operand.shape[-1] // 2
    frequency = rope_base ** (
        -jnp.arange(half_width, dtype=jnp.float32) * (2.0 / operand.shape[-1])
    )
    angles = places.astype(jnp.float32)[:, None] * frequency[None, :]
    cosine = jnp.cos(angles)[:, None, :]
    sine_part = direction * jnp.sin(angles)[:, None, :]
    first_half = operand[..., :half_width]
    second_half = operand[..., half_width:]
    return jnp.concatenate(
        [
            first_half * cosine - second_half * sine_part,
            second_half * cosine + first_half * sine_part,
        ],
        -1,
    )


def project(left_side, right_side):
    return jnp.dot(left_side, right_side, preferred_element_type=jnp.float32)


def project_back(grad_in, weight):
    return lax.dot_general(
        grad_in, weight, (((1,), (1,)), ((), ())), preferred_element_type=jnp.float32
    )


def convolve(padded, pad_ids, row_ids, kernel_in, bias_in):
    length = row_ids.shape[0]
    total = jnp.zeros((length, padded.shape[1]), jnp.float32) + bias_in[None, :]
    for offset in range(KC):
        same_doc = (pad_ids[offset : offset + length] == row_ids).astype(jnp.float32)
        total = (
            total
            + kernel_in[offset][None, :] * padded[offset : offset + length] * same_doc[:, None]
        )
    return total


def ssm_local(states_x, step_size, log_decay, b_matrix, c_matrix, row_ids):
    length = states_x.shape[0]
    running = jnp.cumsum(log_decay, axis=0)
    places = jnp.arange(length, dtype=jnp.int32)
    allowed = (places[:, None] >= places[None, :]) & (row_ids[:, None] == row_ids[None, :])
    spread = running.T[:, :, None] - running.T[:, None, :]
    decay_matrix = jnp.where(allowed[None], jnp.exp(jnp.where(allowed[None], spread, 0.0)), 0.0)
    intersection = jnp.dot(c_matrix, b_matrix.T, precision=HIGH, preferred_element_type=jnp.float32)
    driven = step_size[:, :, None] * states_x
    y_part = jnp.einsum("hts,shp->thp", decay_matrix * intersection[None], driven, precision=HIGH)
    to_end = jnp.where(
        (row_ids == row_ids[-1])[:, None], jnp.exp(running[-1][None, :] - running), 0.0
    )
    local_state = jnp.einsum("sh,shp,sn->hpn", to_end, driven, b_matrix, precision=HIGH)
    return (y_part, local_state)


def ssm_carry(c_matrix, log_decay, row_ids, prev_id, state_in):
    kept_mask = (row_ids == prev_id).astype(jnp.float32)
    weight = jnp.exp(jnp.cumsum(log_decay, axis=0)) * kept_mask[:, None]
    return weight[:, :, None] * jnp.einsum("hpn,tn->thp", state_in, c_matrix, precision=HIGH)


def block_decay(log_decay, row_ids, prev_id):
    return jnp.exp(jnp.sum(log_decay, axis=0)) * (row_ids[-1] == prev_id).astype(jnp.float32)


def mixer_tail(core_in, states_x, gate_z, skip_in, gain_in):
    length = core_in.shape[0]
    core = core_in + skip_in[None, :, None] * states_x
    gated = core.reshape(length, DS) * jax.nn.silu(gate_z)
    return normed(gated, gain_in)


def swiglu(gate_up_out):
    return jax.nn.silu(gate_up_out[:, :FF]) * gate_up_out[:, FF:]


def swap(block, distance):
    peers = lax.axis_size("ctx")
    return lax.ppermute(block, "ctx", [(i, i ^ distance) for i in range(peers)])


def shifted(block, hops):
    peers = lax.axis_size("fsdp")
    return lax.ppermute(block, "fsdp", [(i, (i + hops) % peers) for i in range(peers)])


def powers(first, limit):
    found = []
    while first < limit:
        found.append(first)
        first *= 2
    return found


def chip_steps():
    return powers(2, lax.axis_size("ctx"))


def ordered(flag, first, second, axis):
    return jnp.where(
        flag,
        jnp.concatenate([second, first], axis),
        jnp.concatenate([first, second], axis),
    )


def halves(flag, array, axis):
    size = array.shape[axis] // 2
    low = lax.slice_in_dim(array, 0, size, axis=axis)
    high = lax.slice_in_dim(array, size, 2 * size, axis=axis)
    return (jnp.where(flag, high, low), jnp.where(flag, low, high))


def join(earlier, later):
    return (earlier[0] * later[0], later[0][:, None, None] * earlier[1] + later[1])


def either(flag, when, otherwise):
    return jax.tree.map(lambda a, b: jnp.where(flag, a, b), when, otherwise)


class Last:
    def __init__(self, value):
        self.value = value


class Task:
    def __init__(self, steps):
        self.steps, self.ready, self.result = steps, None, None


class Rounds:
    def __init__(self):
        self.tasks = []

    def start(self, steps):
        self.tasks.append(Task(steps))
        return self.tasks[-1]

    def turn(self, values=()):
        found = []
        for task in self.tasks:
            try:
                found.append(task.steps.send(task.ready))
            except StopIteration:
                found.append(Last(()))
        held = [step.value if isinstance(step, Last) else step for step in found]
        values, held = lax.optimization_barrier((values, held))
        going = []
        for task, step, ready in zip(self.tasks, found, held, strict=True):
            task.ready = ready
            if isinstance(step, Last):
                task.result = ready
            else:
                going.append(task)
        self.tasks = going
        return values

    def until(self, *tasks):
        while any(task.result is None for task in tasks):
            self.turn()

    def until_ready(self, *weights):
        while any(weight.ready is None for weight in weights):
            self.turn()


def entering_steps(decay, state, place, backwards):
    def sent(pair, step):
        return (swap(pair[0], step), swap(pair[1].astype(jnp.bfloat16), step))

    def read(pair):
        return (pair[0], pair[1].astype(jnp.float32))

    def is_later(step):
        return (jnp.bitwise_and(place, step) != 0) != backwards

    core = jnp.bitwise_and(place, 1) == 1
    near = read(sent((decay, state), 1))
    total = either(is_later(1), join(near, (decay, state)), join((decay, state), near))
    total = tuple(halves(core, part, 0)[0] for part in total)
    before = (jnp.ones_like(total[0]), jnp.zeros_like(total[1]))
    steps = chip_steps()
    for step in steps:
        there = read(sent(total, step))
        before = either(is_later(step), join(there, before), before)
        if step != steps[-1]:
            total = either(is_later(step), join(there, total), join(total, there))
            total, before, near = yield total, before, near
    across = swap(before[1].astype(jnp.bfloat16), 1).astype(jnp.float32)
    whole = ordered(core, before[1], across, 0)
    yield Last(jnp.where(is_later(1), near[0][:, None, None] * whole + near[1], whole))


class Weight:
    def __init__(self, shard, width):
        self.shard, self.width, self.chunks, self.ready = shard, width, [], None

    def cuts(self, idx, rows, columns):
        chip, core = idx[0], idx[1]
        per = rows * (lax.axis_size("ctx") // 2)
        for first_row in range(0, self.shard.shape[0], per):
            for first_col in range(0, self.width // 2, columns):
                piece = lax.dynamic_slice(
                    self.shard,
                    (first_row + chip * rows, first_col + core * (self.width // 2)),
                    (rows, columns),
                )
                self.chunks.append((first_row, first_col, []))
                yield piece, self.chunks[-1][2]


class Box:
    def __init__(self, value):
        self.value = value


def copy_all(copies):
    for copy in copies:
        copy.start()
    for copy in copies:
        copy.wait()


def place_kernel(chunks, idx_ref, shard_ref, *refs):
    whole_ref, sems = refs[-2], refs[-1]
    chip, core, layer = idx_ref[0], idx_ref[1], idx_ref[2]
    depth, width = shard_ref.shape[0], whole_ref.shape[1]
    layers = whole_ref.shape[0] // depth
    copies = [
        pltpu.make_async_copy(
            shard_ref.at[:, pl.ds(pl.multiple_of(core * width, 128), width)],
            whole_ref.at[pl.ds(pl.multiple_of(layer * depth, depth), depth), :],
            sems.at[0],
        )
    ]
    for first_row, first_col, found in chunks:
        for side, others, source, first in found:
            rows, columns = refs[source].shape[1:]
            for number, other in enumerate(others):
                for hop in range(layers - 1):
                    owner = lax.rem(layer + 1 + hop, layers)
                    begin = owner * depth + first_row + jnp.bitwise_xor(chip, other) * rows
                    copies.append(
                        pltpu.make_async_copy(
                            refs[source].at[first + number * (layers - 1) + hop],
                            whole_ref.at[
                                pl.ds(pl.multiple_of(begin, rows), rows),
                                pl.ds(first_col + side * columns, columns),
                            ],
                            sems.at[len(copies)],
                        )
                    )
    copy_all(copies)


def placed(idx, weight):
    layers = lax.axis_size("fsdp")
    depth, width = weight.shard.shape[0], weight.width // 2
    boxes = list({id(box): box for _, _, found in weight.chunks for _, _, box, _ in found}.values())
    chunks = [
        (
            first_row,
            first_col,
            [(side, others, boxes.index(box), first) for side, others, box, first in found],
        )
        for first_row, first_col, found in weight.chunks
    ]
    count = 1 + sum(
        (layers - 1) * len(others) for _, _, found in chunks for _, others, _, _ in found
    )
    return pl.pallas_call(
        lambda *refs: place_kernel(chunks, *refs),
        out_shape=jax.ShapeDtypeStruct((layers * depth, width), weight.shard.dtype),
        in_specs=[pl.BlockSpec(memory_space=pltpu.SMEM)]
        + [pl.BlockSpec(memory_space=pl.ANY)] * (1 + len(boxes)),
        out_specs=pl.BlockSpec(memory_space=pltpu.VMEM),
        scratch_shapes=[pltpu.SemaphoreType.DMA((count,))],
        compiler_params=pltpu.CompilerParams(vmem_limit_bytes=32 * 1024 * 1024),
        cost_estimate=pl.CostEstimate(
            flops=0, bytes_accessed=4 * layers * depth * width, transcendentals=0
        ),
        name="place",
    )(idx, weight.shard, *[box.value for box in boxes])


def pack_kernel(fresh, plan, inputs, idx_ref, *refs):
    layer = idx_ref[2]
    outs, sems = refs[inputs:-1], refs[-1]
    copies = []
    for out, first, side in fresh:
        layers, columns = refs[0].shape[0], outs[out].shape[2]
        for hop in range(layers - 1):
            owner = lax.rem(layer + 1 + hop, layers)
            copies.append(
                pltpu.make_async_copy(
                    refs[0].at[owner, :, pl.ds(side * columns, columns)],
                    outs[out].at[first + hop],
                    sems.at[len(copies)],
                )
            )
    for out, first, source, begin, size in plan:
        copies.append(
            pltpu.make_async_copy(
                refs[source].at[pl.ds(begin, size)],
                outs[out].at[pl.ds(first, size)],
                sems.at[len(copies)],
            )
        )
    copy_all(copies)


def packed(idx, along, fresh, plan, sizes, rows, columns):
    boxes = list({id(entry[2]): entry[2] for entry in plan}.values())
    arrays = ([] if along is None else [along]) + [box.value for box in boxes]
    skip = len(arrays) - len(boxes)
    plan = [(out, row, skip + boxes.index(box), begin, size) for out, row, box, begin, size in plan]
    count = len(fresh) * (lax.axis_size("fsdp") - 1) + len(plan)
    return pl.pallas_call(
        lambda *refs: pack_kernel(fresh, plan, len(arrays), *refs),
        out_shape=[jax.ShapeDtypeStruct((size, rows, columns), jnp.bfloat16) for size in sizes],
        in_specs=[pl.BlockSpec(memory_space=pltpu.SMEM)]
        + [pl.BlockSpec(memory_space=pl.ANY)] * len(arrays),
        out_specs=[pl.BlockSpec(memory_space=pltpu.VMEM)] * len(sizes),
        scratch_shapes=[pltpu.SemaphoreType.DMA((count,))],
        compiler_params=pltpu.CompilerParams(vmem_limit_bytes=32 * 1024 * 1024),
        cost_estimate=pl.CostEstimate(
            flops=0, bytes_accessed=4 * sum(sizes) * rows * columns, transcendentals=0
        ),
        name="pack",
    )(idx, *arrays)


def gather_steps(idx, weights, rows, columns):
    steps, layers = chip_steps(), lax.axis_size("fsdp")
    half, near = columns // 2, layers - 1
    pieces, sinks, owners = [], [], []
    for weight in weights:
        for piece, sink in weight.cuts(idx, rows, columns):
            pieces.append(piece)
            sinks.append(sink)
            owners.append(weight)
    along, flying = {}, []
    for turn in range(len(pieces) + 2 * len(steps) + 2):
        if turn < len(pieces):
            along[turn] = lax.all_gather(pieces[turn], "fsdp")
        fresh, plan, sizes, comes = [], [], {step: 0 for step in steps}, []
        used = []
        for stage in range(len(steps)):
            at = turn - 1 - 2 * stage
            if not 0 <= at < len(pieces):
                continue
            for side in range(2):
                step = (steps[side:] + steps[:side])[stage]
                out = steps.index(step)
                first = sizes[step]
                reached = []
                if stage == 0:
                    fresh.append((out, first, side))
                    used.append((at, side, [0], step, first))
                    reached, sizes[step] = [0], first + near
                for _, others, box, begin in [e for e in sinks[at] if e[0] == side]:
                    plan.append((out, sizes[step], box, begin, near * len(others)))
                    sizes[step] += near * len(others)
                    reached = reached + others
                comes.append((at, side, [other ^ (step // 2) for other in reached], step, first))
        active = [step for step in steps if sizes[step]]
        blocks = {}
        if active:
            rank = {steps.index(step): number for number, step in enumerate(active)}
            made = packed(
                idx,
                along.pop(turn - 1, None) if fresh else None,
                [(rank[out], first, side) for out, first, side in fresh],
                [(rank[out], *rest) for out, *rest in plan],
                [sizes[step] for step in active],
                rows,
                half,
            )
            blocks = dict(zip(active, made, strict=True))
        blocks, pieces = lax.optimization_barrier((blocks, pieces))
        got = {step: swap(block, step) for step, block in blocks.items()}
        whole = [
            weight
            for at, weight in enumerate(owners)
            if at == turn - 1 - 2 * len(steps) and weight not in owners[at + 1 :]
        ]
        for weight in whole:
            mine = placed(idx, weight)
            weight.ready = (mine, swap(mine, 1))
            for sink, owner in zip(sinks, owners, strict=True):
                if owner is weight:
                    sink.clear()
        kept = {step: Box(block) for step, block in blocks.items()}
        sent = {step: Box(block) for step, block in got.items()}
        for at, side, others, step, first in used:
            sinks[at].append((side, others, kept[step], first))
        for at, side, others, step, first in comes:
            sinks[at].append((side, others, sent[step], first))
        late, pieces, now, ready = yield (
            [box.value for box in flying],
            pieces,
            {turn: along[turn]} if turn in along else {},
            [weight.ready for weight in whole],
        )
        for box, value in zip(flying, late, strict=True):
            box.value = value
        flying = list(sent.values())
        along.update(now)
        for weight, pair in zip(whole, ready, strict=True):
            weight.ready = pair


def ring_steps(block, layer):
    peers, length = lax.axis_size("fsdp"), block.shape[0]
    found = [block]
    for _ in range(peers - 1):
        found.append((yield shifted(found[-1], 1)))
    ahead = found[:1] + found[:0:-1]
    twice = jnp.concatenate(ahead + ahead, 0)
    whole = lax.dynamic_slice_in_dim(
        twice, lax.rem(peers - layer, peers) * length, peers * length, 0
    )
    yield Last(whole)


def deal_steps(array, layer):
    peers = lax.axis_size("fsdp")
    width = array.shape[1] // peers

    def cut(hops):
        return lax.dynamic_slice_in_dim(array, lax.rem(layer + hops, peers) * width, width, 1)

    ahead = [cut(0)]
    for hops in range(1, peers):
        ahead.append((yield shifted(cut(peers - hops), peers - hops)))
    twice = jnp.concatenate(ahead + ahead, 0)
    length = array.shape[0]
    yield Last(
        lax.dynamic_slice_in_dim(
            twice, lax.rem(peers - layer, peers) * length, peers * length, 0
        )
    )


def every_steps(block, wait):
    found = lax.all_gather(block, "fsdp", axis=0, tiled=True)
    for _ in range(wait):
        yield ()
    yield Last(found)


def added(left_side, right_side):
    return (left_side.astype(jnp.float32) + right_side.astype(jnp.float32)).astype(jnp.bfloat16)


def weight_steps(act, grad, place, finish):
    steps, core = chip_steps(), jnp.bitwise_and(place, 1) == 1
    while any(task.result is None for task in act + grad):
        yield ()
    part = lax.dot_general(
        act[0].result, grad[0].result, (((0,), (0,)), ((), ())), preferred_element_type=jnp.float32
    ).astype(jnp.bfloat16)
    own, other = halves(core, part, 1)
    own, got = yield own, swap(other, 1)
    own = added(own, got)
    size = own.shape[0] // 2
    blocks = [own[:size], own[size:]]
    orders = [steps[side:] + steps[:side] for side in range(2)]
    for stage in range(len(steps)):
        sent = []
        for side in range(2):
            step = orders[side][stage]
            keep, send = halves(jnp.bitwise_and(place, step) != 0, blocks[side], 0)
            sent.append((keep, swap(send, step)))
        sent = yield sent
        blocks = [added(*pair) for pair in sent]
    for stage in range(len(steps))[::-1]:
        sent = yield [(blocks[side], swap(blocks[side], orders[side][stage])) for side in range(2)]
        blocks = [
            ordered(jnp.bitwise_and(place, orders[side][stage]) != 0, *sent[side], 0)
            for side in range(2)
        ]
    own = jnp.concatenate(blocks, 0)
    pair = yield own, swap(own, 1)
    yield Last(finish(pair))


def finish_kernel(segments, idx_ref, *refs):
    out_ref = refs[-1]
    for flag in (0, 1):

        @pl.when(idx_ref[1] == flag)
        def _():
            at = 0
            for number, first, last in segments:
                pair = refs[2 * number : 2 * number + 2]
                half = pair[0].shape[1]
                for part, begin, end in (
                    (pair[flag], first, min(last, half)),
                    (pair[1 - flag], max(first, half) - half, last - half),
                ):
                    if begin < end:
                        out_ref[:, at : at + end - begin] = part[:, begin:end].astype(jnp.float32)
                        at += end - begin


def finished(idx, pairs, segments, first_row=0, rows=None):
    rows = rows or pairs[0][0].shape[0]
    width = sum(last - first for _, first, last in segments)
    block = 32
    while block < 256 and rows % (2 * block) == 0 and first_row % (2 * block) == 0:
        block *= 2
    while block > 32 and block * width > 1024 * 1024:
        block //= 2
    skip = first_row // block
    flat = [part for pair in pairs for part in pair]
    return pl.pallas_call(
        lambda *refs: finish_kernel(segments, *refs),
        grid=(rows // block,),
        out_shape=jax.ShapeDtypeStruct((rows, width), jnp.float32),
        in_specs=[pl.BlockSpec(memory_space=pltpu.SMEM)]
        + [pl.BlockSpec((block, part.shape[1]), lambda i: (i + skip, 0)) for part in flat],
        out_specs=pl.BlockSpec((block, width), lambda i: (i, 0)),
        compiler_params=pltpu.CompilerParams(vmem_limit_bytes=32 * 1024 * 1024),
        cost_estimate=pl.CostEstimate(
            flops=0, bytes_accessed=6 * rows * width, transcendentals=0
        ),
        name="finish",
    )(idx, *flat)


def finish_steps(tasks, finish):
    while any(task.result is None for task in tasks):
        yield ()
    yield Last(finish(*[task.result for task in tasks]))


def along_ctx(block, place):
    for step in powers(1, lax.axis_size("ctx")):
        block = ordered(jnp.bitwise_and(place, step) != 0, block, swap(block, step), 0)
    return block


def along_ctx_steps(block, place):
    for step in powers(1, lax.axis_size("ctx")):
        got = yield swap(block, step)
        block = ordered(jnp.bitwise_and(place, step) != 0, block, got, 0)
    yield Last(block)


def summed_rows(block, place):
    for step in powers(1, lax.axis_size("ctx"))[::-1]:
        keep, send = halves(jnp.bitwise_and(place, step) != 0, block, 0)
        block = added(keep, swap(send, step))
    return block


def tile_of(width):
    return max(tile for tile in range(128, 1025, 128) if width % tile == 0)


def forth_kernel(idx_ref, left_ref, own_ref, other_ref, out_ref):
    for side, part_ref in enumerate((own_ref, other_ref)):

        @pl.when(pl.program_id(0) == side)
        def _():
            out_ref[...] = jnp.dot(
                left_ref[...], part_ref[...], preferred_element_type=jnp.float32
            ).astype(out_ref.dtype)


def back_kernel(idx_ref, grad_ref, own_ref, other_ref, out_ref):
    @pl.when((pl.program_id(0) == 0) & (pl.program_id(1) == 0))
    def _():
        out_ref[...] = jnp.zeros_like(out_ref)

    for side, part_ref in enumerate((own_ref, other_ref)):

        @pl.when(pl.program_id(0) == side)
        def _():
            out_ref[...] += lax.dot_general(
                grad_ref[...],
                part_ref[...],
                (((1,), (1,)), ((), ())),
                preferred_element_type=jnp.float32,
            )


def product_specs(depth, width):
    tile = tile_of(width)
    count = width // tile
    return (
        tile,
        count,
        pl.BlockSpec((depth, tile), lambda s, t, idx: (0, jnp.where(s == 0, t, count - 1))),
        pl.BlockSpec((depth, tile), lambda s, t, idx: (0, jnp.where(s == 0, 0, t))),
        lambda s, t, idx: (0, jnp.bitwise_xor(idx[1], s) * count + t),
    )


def forth(idx, left_side, chunk, kind=jnp.float32):
    rows, (depth, width) = left_side.shape[0], chunk[0].shape
    tile, count, own_spec, other_spec, place = product_specs(depth, width)
    return pl.pallas_call(
        forth_kernel,
        grid_spec=pltpu.PrefetchScalarGridSpec(
            num_scalar_prefetch=1,
            grid=(2, count),
            in_specs=[pl.BlockSpec((rows, depth), lambda s, t, idx: (0, 0)), own_spec, other_spec],
            out_specs=pl.BlockSpec((rows, tile), place),
        ),
        out_shape=jax.ShapeDtypeStruct((rows, 2 * width), kind),
        compiler_params=pltpu.CompilerParams(vmem_limit_bytes=40 * 1024 * 1024),
        cost_estimate=pl.CostEstimate(
            flops=4 * rows * depth * width, bytes_accessed=4 * depth * width, transcendentals=0
        ),
        name="forth",
    )(idx, left_side, *chunk)


def back(idx, grad_in, chunk):
    rows, (depth, width) = grad_in.shape[0], chunk[0].shape
    tile, count, own_spec, other_spec, place = product_specs(depth, width)
    return pl.pallas_call(
        back_kernel,
        grid_spec=pltpu.PrefetchScalarGridSpec(
            num_scalar_prefetch=1,
            grid=(2, count),
            in_specs=[pl.BlockSpec((rows, tile), place), own_spec, other_spec],
            out_specs=pl.BlockSpec((rows, depth), lambda s, t, idx: (0, 0)),
        ),
        out_shape=jax.ShapeDtypeStruct((rows, depth), jnp.float32),
        compiler_params=pltpu.CompilerParams(vmem_limit_bytes=40 * 1024 * 1024),
        cost_estimate=pl.CostEstimate(
            flops=4 * rows * depth * width, bytes_accessed=4 * depth * width, transcendentals=0
        ),
        name="back",
    )(idx, grad_in, *chunk)


def sum_steps(arrays):
    flat = jnp.concatenate([array.reshape(-1) for array in arrays])
    size = flat.shape[0]
    flat = jnp.pad(flat, (0, -size % 1024)).reshape(-1, 128)
    for axis in ("ctx", "fsdp"):
        peers = lax.axis_size(axis)
        for step in powers(1, peers):
            flat = yield flat + lax.ppermute(flat, axis, [(i, i ^ step) for i in range(peers)])
    flat, found, at = flat.reshape(-1), [], 0
    for array in arrays:
        found.append(flat[at : at + array.size].reshape(array.shape))
        at += array.size
    yield Last(found)


def body(
    tokens,
    cotangent,
    doc_ids,
    in_proj,
    dt_proj,
    conv_weight,
    conv_bias,
    dt_bias,
    a_log,
    d_skip,
    mixer_gain,
    out_proj,
    qkv_proj,
    o_proj,
    first_gain,
    second_gain,
    gate_up,
    down_proj,
):
    my_index, layer = lax.axis_index("ctx"), lax.axis_index("fsdp")
    layers = lax.axis_size("fsdp")
    core, chip = jnp.bitwise_and(my_index, 1), my_index // 2
    idx = jnp.stack([chip, core, layer]).astype(jnp.int32)
    conv_cols, qkv_cols = DS + 2 * NS, (HQ + 2 * HK) * HA
    kv_bc = jnp.concatenate([qkv_proj, in_proj[:, 2 * DS :]], 1)
    z_x = in_proj[:, : 2 * DS]
    out_o = jnp.concatenate([out_proj, o_proj], 0)
    rounds = Rounds()

    def dealt(array):
        return rounds.start(deal_steps(array, layer))

    def every(block, wait):
        return rounds.start(every_steps(block, wait))

    def weight_grad(act, grad, finish):
        return rounds.start(weight_steps(act, grad, my_index, finish))

    part = 2048
    qb_w = Weight(kv_bc, part)
    x_w = Weight(in_proj[:, DS : DS + part], part)
    xz_w = Weight(
        jnp.concatenate([in_proj[:, DS + part : 2 * DS], in_proj[:, : DS - part]], 1), part
    )
    z_w = Weight(in_proj[:, DS - part : DS], part)
    oo_w, down_w = Weight(out_o, D), Weight(down_proj, D)
    gate_w, up_w = Weight(gate_up[:, :FF], FF), Weight(gate_up[:, FF:], FF)
    rows = gate_up.shape[0] // (lax.axis_size("ctx") // 2)
    rounds.start(
        gather_steps(idx, [qb_w, x_w, xz_w, z_w, oo_w, gate_w, up_w, down_w], rows, part // 2)
    )
    dt_task = rounds.start(ring_steps(dt_proj, layer))

    hidden = tokens[0].astype(jnp.float32)
    grad_out = cotangent[0].astype(jnp.float32)
    own_ids = doc_ids[0]
    length = hidden.shape[0]
    all_ids = along_ctx(own_ids.reshape(1, length), my_index).reshape(-1)
    first_row = my_index * length
    places = first_row + jnp.arange(length, dtype=jnp.int32)
    before = first_row - (KC - 1) + jnp.arange(KC - 1, dtype=jnp.int32)
    earlier_ids = lax.dynamic_slice_in_dim(all_ids, jnp.maximum(first_row - (KC - 1), 0), KC - 1, 0)
    earlier_ids = jnp.where(before >= 0, earlier_ids, -1)
    pad_ids = jnp.concatenate([earlier_ids, own_ids], 0)
    prev_id = jnp.where(my_index > 0, all_ids[jnp.maximum(first_row - 1, 0)], -1)
    normed_in, norm_pull = jax.vjp(normed, hidden, first_gain)
    input_low = normed_in.astype(jnp.bfloat16)
    input_low, all_ids, pad_ids, prev_id = rounds.turn((input_low, all_ids, pad_ids, prev_id))
    input_dealt = dealt(input_low)
    rounds.until_ready(qb_w)
    rounds.until(dt_task)

    qb_out = forth(idx, input_low, qb_w.ready)
    attn_in, bc_out = qb_out[:, :qkv_cols], qb_out[:, qkv_cols:]
    step_raw = project(input_low, dt_task.result)
    groups = HQ // HK
    scale = HA ** (-0.5)
    query_low = rotate(attn_in[:, : HQ * HA].reshape(length, HQ, HA), places, 1.0).astype(
        jnp.bfloat16
    )
    key_low = rotate(
        attn_in[:, HQ * HA : (HQ + HK) * HA].reshape(length, HK, HA), places, 1.0
    ).astype(jnp.bfloat16)
    value_low = attn_in[:, (HQ + HK) * HA :].astype(jnp.bfloat16)
    both_low = jnp.concatenate([key_low.reshape(length, HK * HA), value_low], 1)
    query_low, both_low, step_raw, bc_out = rounds.turn((query_low, both_low, step_raw, bc_out))
    both_task = rounds.start(along_ctx_steps(both_low, my_index))
    rounds.until_ready(x_w)
    x_out = forth(idx, input_low, x_w.ready)
    x_out = rounds.turn(x_out)
    rounds.until_ready(xz_w)
    xz_out = forth(idx, input_low, xz_w.ready)
    conv_low = jnp.concatenate([x_out, xz_out[:, : DS - part], bc_out], 1).astype(jnp.bfloat16)
    tail_low = from_behind(conv_low[length - (KC - 1) :], "ctx", 1)
    conv_low, tail_low, xz_out = rounds.turn((conv_low, tail_low, xz_out))

    def front_fn(conv_in, tail_in, shift_in, kernel_in, bias_in, bias_step, log_rate):
        padded = jnp.concatenate([tail_in, conv_in], 0)
        activated = jax.nn.silu(convolve(padded, pad_ids, own_ids, kernel_in, bias_in))
        states_x = activated[:, :DS].reshape(length, NH, HP)
        b_matrix = activated[:, DS : DS + NS]
        c_matrix = activated[:, DS + NS :]
        step_size = jax.nn.softplus(shift_in + bias_step)
        log_decay = -step_size * jnp.exp(log_rate)
        y_part, local_state = ssm_local(states_x, step_size, log_decay, b_matrix, c_matrix, own_ids)
        return (y_part, local_state, states_x, c_matrix, log_decay)

    front_out, front_pull = jax.vjp(
        front_fn,
        conv_low.astype(jnp.float32),
        tail_low.astype(jnp.float32),
        step_raw,
        conv_weight,
        conv_bias,
        dt_bias,
        a_log,
    )
    y_part, local_state, states_x, c_matrix, log_decay = front_out
    decay_now, decay_pull = jax.vjp(lambda log_in: block_decay(log_in, own_ids, prev_id), log_decay)
    y_part, local_state, decay_now = rounds.turn((y_part, local_state, decay_now))
    state_task = rounds.start(entering_steps(decay_now, local_state, my_index, False))
    rounds.until(both_task)
    both_all = both_task.result
    query_groups = query_low.reshape(length, HK, groups, HA)
    seq_len = both_all.shape[0]
    keys_all = both_all[:, : HK * HA].reshape(seq_len, HK, HA)
    values_all = both_all[:, HK * HA :].reshape(seq_len, HK, HA)
    key_places = jnp.arange(seq_len, dtype=jnp.int32)
    allowed = (places[:, None] >= key_places[None, :]) & (own_ids[:, None] == all_ids[None, :])

    score = (
        jnp.einsum("qkgd,rkd->kgqr", query_groups, keys_all, preferred_element_type=jnp.float32)
        * scale
    )
    score = jnp.where(allowed[None, None], score, -1e30)
    new_top = jnp.maximum(-1e30, jnp.max(score, axis=-1))
    soft = jnp.where(allowed[None, None], jnp.exp(score - new_top[..., None]), 0.0)
    total = jnp.sum(soft, axis=-1)
    accum = jnp.einsum(
        "kgqr,rkd->qkgd",
        soft.astype(jnp.bfloat16),
        values_all,
        preferred_element_type=jnp.float32,
    )
    attended = accum / jnp.transpose(total, (2, 0, 1))[..., None]
    log_total = new_top + jnp.log(total)
    attended_low = attended.reshape(length, HQ * HA).astype(jnp.bfloat16)
    attended, log_total, attended_low = rounds.turn((attended, log_total, attended_low))

    rounds.until_ready(z_w)
    gate_z = jnp.concatenate(
        [xz_out[:, DS - part :], forth(idx, input_low, z_w.ready)], 1
    )
    gate_z = rounds.turn(gate_z)
    rounds.until(state_task)
    rounds.until_ready(oo_w)
    state_in = state_task.result
    y_carry, carry_pull = jax.vjp(
        lambda c_in, log_in, state_arg: ssm_carry(c_in, log_in, own_ids, prev_id, state_arg),
        c_matrix,
        log_decay,
        state_in,
    )
    mixer_normed, tail_pull = jax.vjp(
        mixer_tail, y_part + y_carry, states_x, gate_z, d_skip, mixer_gain
    )
    mixer_low = mixer_normed.astype(jnp.bfloat16)

    def interleaved(mixed_in, attended_in):
        return jnp.concatenate(
            [
                mixed_in.reshape(length, layers, DS // layers),
                attended_in.reshape(length, layers, HQ * HA // layers),
            ],
            2,
        ).reshape(length, DS + HQ * HA)

    def parted(both):
        both = both.reshape(length, layers, (DS + HQ * HA) // layers)
        return (
            both[:, :, : DS // layers].reshape(length, DS),
            both[:, :, DS // layers :].reshape(length, HQ * HA),
        )

    branches_low = interleaved(mixer_low, attended_low)
    middle = hidden + forth(idx, branches_low, oo_w.ready)
    normed_mid, mid_pull = jax.vjp(normed, middle, second_gain)
    mid_low = normed_mid.astype(jnp.bfloat16)
    grad_low = grad_out.astype(jnp.bfloat16)
    middle, mid_low, branches_low = rounds.turn((middle, mid_low, branches_low))
    branches_dealt = dealt(branches_low)
    rounds.until_ready(gate_w)
    gate_out = forth(idx, mid_low, gate_w.ready)
    gate_out = rounds.turn(gate_out)
    rounds.until_ready(up_w)
    cotangent_all = every(grad_low, 2)
    mid_dealt = dealt(mid_low)
    up_out = forth(idx, mid_low, up_w.ready)
    act_value, act_pull = jax.vjp(
        lambda gate_in, up_in: jax.nn.silu(gate_in) * up_in, gate_out, up_out
    )
    act_low = act_value.astype(jnp.bfloat16)
    act_low = rounds.turn(act_low)

    rounds.until_ready(down_w)
    act_dealt = dealt(act_low)
    d_act = back(idx, grad_low, down_w.ready)
    d_gate, d_up = act_pull(d_act)
    gate_low, up_low = d_gate.astype(jnp.bfloat16), d_up.astype(jnp.bfloat16)
    gate_low, up_low = rounds.turn((gate_low, up_low))
    rounds.until(cotangent_all)
    gate_all = every(gate_low, 4)
    up_all = every(up_low, 7)
    down_grad = weight_grad(
        [act_dealt], [cotangent_all], lambda pair: finished(idx, [pair], [(0, 0, D)])
    )
    d_mid_norm = back(idx, gate_low, gate_w.ready)
    mixed, d_mid_norm = rounds.turn((middle + forth(idx, act_low, down_w.ready), d_mid_norm))
    d_mid_norm = d_mid_norm + back(idx, up_low, up_w.ready)
    d_middle_part, d_second_gain = mid_pull(d_mid_norm)
    d_middle = grad_out + d_middle_part
    branch_low = d_middle.astype(jnp.bfloat16)
    branch_low, d_middle = rounds.turn((branch_low, d_middle))
    branch_all = every(branch_low, 7)
    d_mixer_norm, d_attended = parted(back(idx, branch_low, oo_w.ready))
    d_core, d_states_tail, d_gate_z, d_d_skip, d_mixer_gain = tail_pull(d_mixer_norm)
    z_low = d_gate_z.astype(jnp.bfloat16)
    z_low, d_attended, d_core = rounds.turn((z_low, d_attended, d_core))
    d_c_carry, d_log_carry, d_state_in = carry_pull(d_core)
    later_task = rounds.start(entering_steps(decay_now, d_state_in, my_index, True))
    d_out_low = d_attended.reshape(length, HK, groups, HA).astype(jnp.bfloat16)
    delta = jnp.transpose(jnp.sum(d_out_low.astype(jnp.float32) * attended, axis=-1), (1, 2, 0))
    score = (
        jnp.einsum("qkgd,rkd->kgqr", query_groups, keys_all, preferred_element_type=jnp.float32)
        * scale
    )
    prob = jnp.where(
        allowed[None, None],
        jnp.exp(jnp.where(allowed[None, None], score, 0.0) - log_total[..., None]),
        0.0,
    )
    d_prob = jnp.einsum(
        "qkgd,rkd->kgqr", d_out_low, values_all, preferred_element_type=jnp.float32
    )
    score_grad = (prob * (d_prob - delta[..., None])).astype(jnp.bfloat16)
    d_query = (
        jnp.einsum("kgqr,rkd->qkgd", score_grad, keys_all, preferred_element_type=jnp.float32)
        * scale
    )
    d_keys = (
        jnp.einsum("kgqr,qkgd->rkd", score_grad, query_groups, preferred_element_type=jnp.float32)
        * scale
    )
    d_values = jnp.einsum(
        "kgqr,qkgd->rkd", prob.astype(jnp.bfloat16), d_out_low, preferred_element_type=jnp.float32
    )
    kv_terms = jnp.concatenate(
        [d_keys.reshape(seq_len, HK * HA), d_values.reshape(seq_len, HK * HA)], 1
    ).astype(jnp.bfloat16)
    kv_terms, d_query = rounds.turn((kv_terms, d_query))
    d_kv = summed_rows(kv_terms, my_index).astype(jnp.float32)
    qkv_low = jnp.concatenate(
        [
            rotate(d_query.reshape(length, HQ, HA), places, -1.0).reshape(length, HQ * HA),
            rotate(d_kv[:, : HK * HA].reshape(length, HK, HA), places, -1.0).reshape(
                length, HK * HA
            ),
            d_kv[:, HK * HA :],
        ],
        1,
    ).astype(jnp.bfloat16)
    qkv_low = rounds.turn(qkv_low)
    zq_all = every(jnp.concatenate([z_low, qkv_low], 1), 5)
    rounds.until(later_task)
    later_grad = later_task.result
    d_decay = jnp.sum(later_grad * state_in, axis=(1, 2))
    d_log_decay = decay_pull(d_decay)[0]
    d_conv_in, d_tail, d_step_raw, d_conv_weight, d_conv_bias, d_dt_bias, d_a_log = front_pull(
        (d_core, later_grad, d_states_tail, d_c_carry, d_log_carry + d_log_decay)
    )
    d_conv_in, d_tail, d_step_raw = rounds.turn((d_conv_in, d_tail, d_step_raw))
    from_next = from_behind(d_tail.astype(jnp.bfloat16), "ctx", -1).astype(d_tail.dtype)
    d_conv_in = jnp.concatenate(
        [d_conv_in[: length - (KC - 1)], d_conv_in[length - (KC - 1) :] + from_next], 0
    )
    conv_grad_low = d_conv_in.astype(jnp.bfloat16)
    step_low = d_step_raw.astype(jnp.bfloat16)
    blank = jnp.zeros((length, 512 - NH), jnp.bfloat16)
    conv_grad_low, step_low = rounds.turn((conv_grad_low, step_low))
    tail_all = every(jnp.concatenate([conv_grad_low, step_low, blank[:, : 256 - NH]], 1), 5)
    pending = {
        "gate": (mid_dealt, gate_all, lambda pair: pair),
        "up": (mid_dealt, up_all, lambda pair: pair),
        "oo": (
            branches_dealt,
            branch_all,
            lambda pair: (
                finished(idx, [pair], [(0, 0, D)], 0, DS // layers),
                finished(idx, [pair], [(0, 0, D)], DS // layers, HQ * HA // layers),
            ),
        ),
        "zq": (input_dealt, zq_all, lambda pair: pair),
        "tail": (input_dealt, tail_all, lambda pair: pair),
    }
    grads = {
        name: weight_grad([act], [grad], finish) for name, (act, grad, finish) in pending.items()
    }
    gate_up_grad = rounds.start(
        finish_steps(
            [grads["gate"], grads["up"]],
            lambda *pairs: finished(idx, pairs, [(0, 0, FF), (1, 0, FF)]),
        )
    )
    d_normed_in = (
        back(idx, conv_grad_low[:, :part], x_w.ready)
        + back(
            idx,
            jnp.concatenate([conv_grad_low[:, part:DS], z_low[:, : DS - part]], 1),
            xz_w.ready,
        )
    )
    d_normed_in = rounds.turn(d_normed_in)
    d_normed_in = (
        d_normed_in
        + back(idx, z_low[:, DS - part :], z_w.ready)
        + back(idx, jnp.concatenate([qkv_low, conv_grad_low[:, DS:]], 1), qb_w.ready)
        + project_back(step_low, dt_task.result)
    )
    d_hidden_part, d_first_gain = norm_pull(d_normed_in)
    d_tokens = d_middle + d_hidden_part
    d_tokens, d_first_gain = rounds.turn((d_tokens, d_first_gain))
    smalls_task = rounds.start(
        sum_steps(
            (
                d_conv_weight,
                d_conv_bias,
                d_dt_bias,
                d_a_log,
                d_d_skip,
                d_mixer_gain,
                d_first_gain,
                d_second_gain,
            )
        )
    )
    rounds.until(smalls_task, gate_up_grad, down_grad, *grads.values())
    smalls = smalls_task.result
    tail_pair, zq_pair = grads["tail"].result, grads["zq"].result
    tail_half = tail_pair[0].shape[1]
    step_grad = jnp.where(core == 1, tail_pair[0], tail_pair[1])
    return (
        mixed[None].astype(jnp.bfloat16),
        d_tokens[None],
        finished(idx, [zq_pair, tail_pair], [(0, 0, DS), (1, 0, conv_cols)]),
        step_grad[:, conv_cols - tail_half : conv_cols - tail_half + NH].astype(jnp.float32),
        smalls[0],
        smalls[1],
        smalls[2],
        smalls[3],
        smalls[4],
        smalls[5],
        grads["oo"].result[0],
        finished(idx, [zq_pair], [(0, DS, DS + qkv_cols)]),
        grads["oo"].result[1],
        smalls[6],
        smalls[7],
        gate_up_grad.result,
        down_grad.result,
    )


def solution(mesh):
    return jax.shard_map(
        body,
        mesh=mesh,
        in_specs=(
            P("fsdp", "ctx", None),
            P("fsdp", "ctx", None),
            P("fsdp", "ctx"),
            P("fsdp", None),
            P("fsdp", None),
            P(),
            P(),
            P(),
            P(),
            P(),
            P(),
            P("fsdp", None),
            P("fsdp", None),
            P("fsdp", None),
            P(),
            P(),
            P("fsdp", None),
            P("fsdp", None),
        ),
        out_specs=(
            P("fsdp", "ctx", None),
            P("fsdp", "ctx", None),
            P("fsdp", None),
            P("fsdp", None),
            P(),
            P(),
            P(),
            P(),
            P(),
            P(),
            P("fsdp", None),
            P("fsdp", None),
            P("fsdp", None),
            P(),
            P(),
            P("fsdp", None),
            P("fsdp", None),
        ),
        check_vma=False,
    )
```

time: 4200 us -> 1290 us (0.31)
  waiting for transfers between devices: 3600 us -> 399 us
  Pallas kernels: 0 us -> 223 us
  matrix products: 274 us -> 90.8 us
  local copies, waits for them, and re-layouts: 68.2 us -> 233 us
  starting transfers between devices: 4.9 us -> 128 us
  blocking collectives: 91 us -> 0 us
  other arithmetic: 130 us -> 183 us
    all_gather x8 -> x18, waiting for transfers between devices: 1630 us -> 59.6 us  [the longest x12 46.9 us: gather_steps(): along[turn] = lax.all_gather(pieces[turn], 'fsdp')]
    reduce_scatter x7 -> x0, waiting for transfers between devices: 1040 us -> none  [the longest x6 1040 us: weight_grad(): lax.psum_scatter(lax.dot_general(act_in, grad_in, (((0,), (0,)), ((), ())...]
    unnamed x19 -> x18, waiting for transfers between devices: 559 us -> 0.3 us
    psum x2 -> x0, waiting for transfers between devices: 369 us -> none  [the longest x1 271 us: body(): lax.psum(shards[0].astype(jnp.bfloat16), 'ctx').astype(jnp.float32)]
    ppermute x0 -> x135, waiting for transfers between devices: none -> 340 us  [the longest x115 281 us: swap(): return lax.ppermute(block, 'ctx', [(i, i ^ distance) for i in range(peers)])]
    pallas_call x0 -> x44, Pallas kernels: none -> 223 us  [the longest x8 69.7 us: back(): pl.pallas_call(back_kernel, grid_spec=pltpu.PrefetchScalarGridSpec(num_sc...]
    unnamed x289 -> x777, local copies, waits for them, and re-layouts: 23.8 us -> 157 us
    ppermute x0 -> x135, starting transfers between devices: none -> 124 us  [the longest x115 103 us: swap(): return lax.ppermute(block, 'ctx', [(i, i ^ distance) for i in range(peers)])]
  transfers between devices with their start and end apart: 20 -> 155, of which waited for: 17 -> 55; matrix products, arithmetic and copies ran while one was open for 9% -> 29% of each run, Pallas kernels for 0% -> 14%
where the time goes in v2:
time: 1290 us; the launch traced here: 1280 us
  waiting for transfers between devices  399 us (31%)
  local copies, waits for them, and re-layouts  233 us (18%)
  Pallas kernels  223 us (17%)
  other arithmetic  183 us (14%)
  starting transfers between devices  128 us (10%)
  matrix products  90.8 us (7%)
  between operations  20.5 us (2%)
    ppermute x115, waiting for transfers between devices, swap(): return lax.ppermute(block, 'ctx', [(i, i ^ distance) for i in range(peers)])  281 us
    unnamed x777, local copies, waits for them, and re-layouts  157 us
    ppermute x115, starting transfers between devices, swap(): return lax.ppermute(block, 'ctx', [(i, i ^ distance) for i in range(peers)])  103 us
    pallas_call x8, Pallas kernels, back(): pl.pallas_call(back_kernel, grid_spec=pltpu.PrefetchScalarGridSpec(num_sc...  69.7 us
    pallas_call x8, Pallas kernels, forth(): pl.pallas_call(forth_kernel, grid_spec=pltpu.PrefetchScalarGridSpec(num_s...  52.6 us
    all_gather x12, waiting for transfers between devices, gather_steps(): along[turn] = lax.all_gather(pieces[turn], 'fsdp')  46.9 us
    pallas_call x8, Pallas kernels, placed(): pl.pallas_call(lambda *refs: place_kernel(chunks, *refs), out_shape=jax.S...  42.6 us
    ppermute x15, waiting for transfers between devices, shifted(): lax.ppermute(block, 'fsdp', [(i, (i + hops) % peers) for i in range(peers)])  36.1 us
  transfers between devices with their start and end apart: 155, of which 55 were waited for; matrix products, arithmetic and copies ran while one was open for 29% of the time, Pallas kernels for 14%

profile of v2, /device:TPU:0, one launch (start us, length us, event | category | flops | bytes accessed | tf_op | source)
XLA Modules:
  0.0 1277.7 jit_solution(2535406749932633560)
XLA Ops:
  53.0 18.1 %all-gather.44.cloned.1.call-done = bf16[512,1024]{1,0:T(8,128)(2,1)} async-done(((bf16[128,1024]{1,0:T(8,128)(2,1)}), bf16[512,1024]{1,0:T(8,128)(2,1)}) %all-gather.44.cloned.1.call-update) | async-done | bytes 1048592 | tf_op jit(solution)/shard_map/all_gather | solution.py:387
  84.0 17.0 %all-gather.46.cloned.1.call-done = bf16[512,1024]{1,0:T(8,128)(2,1)} async-done(((bf16[128,1024]{1,0:T(8,128)(2,1)}), bf16[512,1024]{1,0:T(8,128)(2,1)}) %all-gather.46.cloned.1.call-update) | async-done | bytes 1048592 | tf_op jit(solution)/shard_map/all_gather | solution.py:387
  117.3 11.8 all-gather.48.cloned.1.call-done
  138.1 18.9 %collective-permute-done.10.refs_7_.refs_3_.refs_4_ = bf16[9,128,512]{2,1,0:T(8,128)(2,1)S(1)} collective-permute-done((bf16[9,128,512]{2,1,0:T(8,128)(2,1)}, bf16[9,128,512]{2,1,0:T(8,128)(2,1)S(1)}, u32[]{:S(2)}, u32[]{:S(2)}) %collective-permute-start.10) | collective-permute-done | bytes 1179680 | tf_op jit(solution)/shard_map/ppermute | solution.py:120
  176.4 20.1 %collective-permute-done.18.refs_3_.refs_7_.refs_4_ = bf16[9,128,512]{2,1,0:T(8,128)(2,1)S(1)} collective-permute-done((bf16[9,128,512]{2,1,0:T(8,128)(2,1)}, bf16[9,128,512]{2,1,0:T(8,128)(2,1)S(1)}, u32[]{:S(2)}, u32[]{:S(2)}) %collective-permute-start.18) | collective-permute-done | bytes 1179680 | tf_op jit(solution)/shard_map/ppermute | solution.py:120
  214.8 5.8 forth.8
  261.3 5.7 forth.9
  268.0 12.7 collective-permute-done.21.refs_3_.refs_7_.refs_10_
  301.0 5.6 forth.10
  352.3 9.0 fusion.53
  375.5 6.8 place.12.own_ref
  386.9 8.6 collective-permute-done.36
  415.4 14.4 %collective-permute-done.39 = f32[24]{0:T(128)S(1)} collective-permute-done((f32[24]{0:T(128)S(1)}, f32[24]{0:T(128)S(1)}, u32[]{:S(2)}, u32[]{:S(2)}) %collective-permute-start.39) | collective-permute-done | bytes 128 | tf_op jit(solution)/shard_map/ppermute | solution.py:120
  448.7 30.4 %collective-permute-done.42 = bf16[24,64,256]{2,1,0:T(8,128)(2,1)} collective-permute-done((bf16[24,64,256]{2,1,0:T(8,128)(2,1)}, bf16[24,64,256]{2,1,0:T(8,128)(2,1)}, u32[]{:S(2)}, u32[]{:S(2)}) %collective-permute-start.42) | collective-permute-done | bytes 786464 | tf_op jit(solution)/shard_map/ppermute | solution.py:120
  498.0 7.7 place.13.own_ref
  553.0 6.8 forth.12
  567.6 7.2 place.14.own_ref
  591.8 8.0 forth.13
  604.0 8.0 forth.14
  618.9 6.8 place.15.own_ref
  635.0 16.3 %collective-permute-done.59 = bf16[128,512]{1,0:T(8,128)(2,1)S(1)} collective-permute-done((bf16[128,512]{1,0:T(8,128)(2,1)}, bf16[128,512]{1,0:T(8,128)(2,1)S(1)}, u32[]{:S(2)}, u32[]{:S(2)}) %collective-permute-start.59) | collective-permute-done | bytes 131104 | tf_op jit(solution)/shard_map/ppermute | solution.py:125
  657.8 9.9 back.8
  671.5 12.6 all-gather.66.cloned.1.call-done
  692.7 6.9 forth.15
  701.4 10.7 back.9
  712.2 7.5 collective-permute-done.62
  719.8 10.1 back.10
  738.8 10.0 back.11
  783.1 8.1 fusion.26
  801.1 7.2 back.14
  829.6 8.7 collective-permute-done.66
  867.9 5.9 collective-permute-done.72
  953.4 7.4 back.12
  960.8 7.2 back.13
  969.2 7.2 back.15
  992.0 8.9 collective-permute-done.83
  1016.4 6.8 collective-permute-done.87
  1074.9 11.6 collective-permute-done.98
  1086.5 8.8 collective-permute-done.102
  1104.6 12.9 %collective-permute-done.112 = f32[200,128]{1,0:T(8,128)S(1)} collective-permute-done((f32[200,128]{1,0:T(8,128)S(1)}, f32[200,128]{1,0:T(8,128)S(1)}, u32[]{:S(2)}, u32[]{:S(2)}) %collective-permute-start.112) | collective-permute-done | bytes 102432 | tf_op jit(solution)/shard_map/ppermute | solution.py:690
  1122.3 10.3 collective-permute-done.106
  1132.6 11.7 collective-permute-done.107
  1165.0 12.2 collective-permute-done.115
  1186.8 12.4 collective-permute-done.122
  1221.3 7.3 finish.7
  1228.6 7.2 collective-permute-done.129
  1247.8 11.2 collective-permute-done.134
  1264.1 5.8 finish.10
  (1423 shorter events, 764.6 us)
Async XLA Ops:
  7.2 36.7 %all-gather.42.cloned.1.call-start = ((), (), s32[]{:S(2)}) async-start(), calls=%async_computation.5 | async-start | bytes 1310720 | tf_op jit(solution)/shard_map/all_gather | solution.py:387
  10.8 60.3 %all-gather.44.cloned.1.call-start = ((), (), s32[]{:S(2)}) async-start(), calls=%async_computation.6 | async-start | bytes 1310720 | tf_op jit(solution)/shard_map/all_gather | solution.py:387
  10.9 33.0 %collective-permute-start.3 = (bf16[512,48]{0,1:T(8,128)(2,1)S(1)}, bf16[512,48]{0,1:T(8,128)(2,1)S(1)}, u32[]{:S(2)}, u32[]{:S(2)}) collective-permute-start(bf16[512,48]{0,1:T(8,128)(2,1)S(1)} %copy-done.272), channel_id=1, source_target_pairs={{0,1},{1,2},{2,3},{3,0},{4,5},{5,6},{6,7},{7,4},{8,9},{9,10},{10,1... | collective-permute-start | bytes 147464 | tf_op jit(solution)/shard_map/ppermute | solution.py:125
  43.9 57.0 %all-gather.46.cloned.1.call-start = ((), (), s32[]{:S(2)}) async-start(), calls=%async_computation.7 | async-start | bytes 1310720 | tf_op jit(solution)/shard_map/all_gather | solution.py:387
  71.1 57.9 %all-gather.48.cloned.1.call-start = ((), (), s32[]{:S(2)}) async-start(), calls=%async_computation.8 | async-start | bytes 1310720 | tf_op jit(solution)/shard_map/all_gather | solution.py:387
  101.0 57.2 %all-gather.50.cloned.1.call-start = ((), (), s32[]{:S(2)}) async-start(), calls=%async_computation.9 | async-start | bytes 1310720 | tf_op jit(solution)/shard_map/all_gather | solution.py:387
  129.1 69.4 %all-gather.52.cloned.1.call-start = ((), (), s32[]{:S(2)}) async-start(), calls=%async_computation.10 | async-start | bytes 1310720 | tf_op jit(solution)/shard_map/all_gather | solution.py:387
  167.6 30.9 %collective-permute-start.15 = (bf16[2048,1024]{1,0:T(8,128)(2,1)}, bf16[2048,1024]{1,0:T(8,128)(2,1)}, u32[]{:S(2)}, u32[]{:S(2)}) collective-permute-start(bf16[2048,1024]{1,0:T(8,128)(2,1)} %place.8.own_ref), channel_id=1, source_target_pairs={{0,4},{4,0},{8,12},{12,8},{16,20},{20,16},{24,28},{28,24},{1,5},{5... | collective-permute-start | bytes 12582920 | tf_op jit(solution)/shard_map/ppermute | solution.py:120
  167.7 73.9 %all-gather.54.cloned.1.call-start = ((), (), s32[]{:S(2)}) async-start(), calls=%async_computation.11 | async-start | bytes 1310720 | tf_op jit(solution)/shard_map/all_gather | solution.py:387
  209.0 32.6 %collective-permute-start.20 = (bf16[2048,1024]{1,0:T(8,128)(2,1)}, bf16[2048,1024]{1,0:T(8,128)(2,1)}, u32[]{:S(2)}, u32[]{:S(2)}) collective-permute-start(bf16[2048,1024]{1,0:T(8,128)(2,1)} %place.9.own_ref), channel_id=1, source_target_pairs={{0,4},{4,0},{8,12},{12,8},{16,20},{20,16},{24,28},{28,24},{1,5},{5... | collective-permute-start | bytes 12582920 | tf_op jit(solution)/shard_map/ppermute | solution.py:120
  210.7 72.1 %all-gather.56.cloned.1.call-start = ((), (), s32[]{:S(2)}) async-start(), calls=%async_computation.12 | async-start | bytes 1310720 | tf_op jit(solution)/shard_map/all_gather | solution.py:387
  251.4 31.3 %collective-permute-start.23 = (bf16[2048,1024]{1,0:T(8,128)(2,1)}, bf16[2048,1024]{1,0:T(8,128)(2,1)}, u32[]{:S(2)}, u32[]{:S(2)}) collective-permute-start(bf16[2048,1024]{1,0:T(8,128)(2,1)} %place.10.own_ref), channel_id=1, source_target_pairs={{0,4},{4,0},{8,12},{12,8},{16,20},{20,16},{24,28},{28,24},{1,5},{5... | collective-permute-start | bytes 12582920 | tf_op jit(solution)/shard_map/ppermute | solution.py:120
  251.5 80.1 %all-gather.58.cloned.1.call-start = ((), (), s32[]{:S(2)}) async-start(), calls=%async_computation.13 | async-start | bytes 1310720 | tf_op jit(solution)/shard_map/all_gather | solution.py:387
  292.9 38.8 %collective-permute-start.28 = (bf16[2048,1024]{1,0:T(8,128)(2,1)}, bf16[2048,1024]{1,0:T(8,128)(2,1)}, u32[]{:S(2)}, u32[]{:S(2)}) collective-permute-start(bf16[2048,1024]{1,0:T(8,128)(2,1)} %place.11.own_ref), channel_id=1, source_target_pairs={{0,4},{4,0},{8,12},{12,8},{16,20},{20,16},{24,28},{28,24},{1,5},{5... | collective-permute-start | bytes 12582920 | tf_op jit(solution)/shard_map/ppermute | solution.py:120
  299.9 66.7 %all-gather.60.cloned.1.call-start = ((), (), s32[]{:S(2)}) async-start(), calls=%async_computation.14 | async-start | bytes 1310720 | tf_op jit(solution)/shard_map/all_gather | solution.py:387
  326.0 40.6 %collective-permute-start.30 = (bf16[9,128,512]{2,1,0:T(8,128)(2,1)}, bf16[9,128,512]{2,1,0:T(8,128)(2,1)}, u32[]{:S(2)}, u32[]{:S(2)}) collective-permute-start(bf16[9,128,512]{2,1,0:T(8,128)(2,1)} %get-tuple-element.845.refs_2_.refs_8_), channel_id=1, source_target_pairs={{0,8},{4,12},{8,0},{12,4},{16,24},{20,28},{24,16},{28,20},{1,9},{5... | collective-permute-start | bytes 3538952 | tf_op jit(solution)/shard_map/ppermute | solution.py:120
  327.3 39.3 %collective-permute-start.31 = (bf16[9,128,512]{2,1,0:T(8,128)(2,1)}, bf16[9,128,512]{2,1,0:T(8,128)(2,1)}, u32[]{:S(2)}, u32[]{:S(2)}) collective-permute-start(bf16[9,128,512]{2,1,0:T(8,128)(2,1)} %get-tuple-element.846.refs_4_.refs_9_), channel_id=1, source_target_pairs={{0,16},{4,20},{8,24},{12,28},{16,0},{20,4},{24,8},{28,12},{1,17},{... | collective-permute-start | bytes 3538952 | tf_op jit(solution)/shard_map/ppermute | solution.py:120
  334.3 106.5 %all-gather.62.cloned.1.call-start = ((), (), s32[]{:S(2)}) async-start(), calls=%async_computation.15 | async-start | bytes 1310720 | tf_op jit(solution)/shard_map/all_gather | solution.py:387
  382.3 58.6 %collective-permute-start.35 = (bf16[4096,1024]{1,0:T(8,128)(2,1)}, bf16[4096,1024]{1,0:T(8,128)(2,1)}, u32[]{:S(2)}, u32[]{:S(2)}) collective-permute-start(bf16[4096,1024]{1,0:T(8,128)(2,1)} %place.12.own_ref), channel_id=1, source_target_pairs={{0,4},{4,0},{8,12},{12,8},{16,20},{20,16},{24,28},{28,24},{1,5},{5... | collective-permute-start | bytes 25165832 | tf_op jit(solution)/shard_map/ppermute | solution.py:120
  384.7 56.1 %collective-permute-start.33 = (bf16[9,128,512]{2,1,0:T(8,128)(2,1)}, bf16[9,128,512]{2,1,0:T(8,128)(2,1)}, u32[]{:S(2)}, u32[]{:S(2)}) collective-permute-start(bf16[9,128,512]{2,1,0:T(8,128)(2,1)} %copy-done.58), channel_id=1, source_target_pairs={{0,8},{4,12},{8,0},{12,4},{16,24},{20,28},{24,16},{28,20},{1,9},{5... | collective-permute-start | bytes 3538952 | tf_op jit(solution)/shard_map/ppermute | solution.py:120
  386.1 54.8 %collective-permute-start.34 = (bf16[9,128,512]{2,1,0:T(8,128)(2,1)}, bf16[9,128,512]{2,1,0:T(8,128)(2,1)}, u32[]{:S(2)}, u32[]{:S(2)}) collective-permute-start(bf16[9,128,512]{2,1,0:T(8,128)(2,1)} %copy-done.61), channel_id=1, source_target_pairs={{0,16},{4,20},{8,24},{12,28},{16,0},{20,4},{24,8},{28,12},{1,17},{... | collective-permute-start | bytes 3538952 | tf_op jit(solution)/shard_map/ppermute | solution.py:120
  386.7 106.6 %all-gather.64.cloned.1.call-start = ((), (), s32[]{:S(2)}) async-start(), calls=%async_computation.16 | async-start | bytes 1310720 | tf_op jit(solution)/shard_map/all_gather | solution.py:387
  403.9 31.3 %collective-permute-start.38 = (bf16[24,64,256]{2,1,0:T(8,128)(2,1)}, bf16[24,64,256]{2,1,0:T(8,128)(2,1)}, u32[]{:S(2)}, u32[]{:S(2)}) collective-permute-start(bf16[24,64,256]{2,1,0:T(8,128)(2,1)} %fusion.117), channel_id=1, source_target_pairs={{0,8},{4,12},{8,0},{12,4},{16,24},{20,28},{24,16},{28,20},{1,9},{5... | collective-permute-start | bytes 2359304 | tf_op jit(solution)/shard_map/ppermute | solution.py:120
  429.8 63.4 %collective-permute-start.40 = (bf16[9,128,512]{2,1,0:T(8,128)(2,1)}, bf16[9,128,512]{2,1,0:T(8,128)(2,1)}, u32[]{:S(2)}, u32[]{:S(2)}) collective-permute-start(bf16[9,128,512]{2,1,0:T(8,128)(2,1)} %get-tuple-element.884.refs_2_.refs_8_), channel_id=1, source_target_pairs={{0,8},{4,12},{8,0},{12,4},{16,24},{20,28},{24,16},{28,20},{1,9},{5... | collective-permute-start | bytes 3538952 | tf_op jit(solution)/shard_map/ppermute | solution.py:120
  435.3 58.0 %collective-permute-start.41 = (bf16[9,128,512]{2,1,0:T(8,128)(2,1)}, bf16[9,128,512]{2,1,0:T(8,128)(2,1)}, u32[]{:S(2)}, u32[]{:S(2)}) collective-permute-start(bf16[9,128,512]{2,1,0:T(8,128)(2,1)} %get-tuple-element.885.refs_4_.refs_9_), channel_id=1, source_target_pairs={{0,16},{4,20},{8,24},{12,28},{16,0},{20,4},{24,8},{28,12},{1,17},{... | collective-permute-start | bytes 3538952 | tf_op jit(solution)/shard_map/ppermute | solution.py:120
  440.9 38.3 %collective-permute-start.42 = (bf16[24,64,256]{2,1,0:T(8,128)(2,1)}, bf16[24,64,256]{2,1,0:T(8,128)(2,1)}, u32[]{:S(2)}, u32[]{:S(2)}) collective-permute-start(bf16[24,64,256]{2,1,0:T(8,128)(2,1)} %fusion.33), channel_id=1, source_target_pairs={{0,16},{4,20},{8,24},{12,28},{16,0},{20,4},{24,8},{28,12},{1,17},{... | collective-permute-start | bytes 2359304 | tf_op jit(solution)/shard_map/ppermute | solution.py:120
  446.7 237.4 %all-gather.66.cloned.1.call-start = ((), (), s32[]{:S(2)}) async-start(), calls=%async_computation.17 | async-start | bytes 2621440 | tf_op jit(solution)/shard_map/all_gather | solution.py:488
  505.6 37.9 %collective-permute-start.46 = (bf16[2048,2048]{1,0:T(8,128)(2,1)}, bf16[2048,2048]{1,0:T(8,128)(2,1)}, u32[]{:S(2)}, u32[]{:S(2)}) collective-permute-start(bf16[2048,2048]{1,0:T(8,128)(2,1)} %place.13.own_ref), channel_id=1, source_target_pairs={{0,4},{4,0},{8,12},{12,8},{16,20},{20,16},{24,28},{28,24},{1,5},{5... | collective-permute-start | bytes 25165832 | tf_op jit(solution)/shard_map/ppermute | solution.py:120
  513.6 29.1 %collective-permute-start.44 = (bf16[9,128,512]{2,1,0:T(8,128)(2,1)}, bf16[9,128,512]{2,1,0:T(8,128)(2,1)S(1)}, u32[]{:S(2)}, u32[]{:S(2)}) collective-permute-start(bf16[9,128,512]{2,1,0:T(8,128)(2,1)} %get-tuple-element.901.refs_1_.refs_2_), channel_id=1, source_target_pairs={{0,8},{4,12},{8,0},{12,4},{16,24},{20,28},{24,16},{28,20},{1,9},{5... | collective-permute-start | bytes 3538952 | tf_op jit(solution)/shard_map/ppermute | solution.py:120
  536.7 30.5 %collective-permute-start.47 = (bf16[9,128,512]{2,1,0:T(8,128)(2,1)}, bf16[9,128,512]{2,1,0:T(8,128)(2,1)}, u32[]{:S(2)}, u32[]{:S(2)}) collective-permute-start(bf16[9,128,512]{2,1,0:T(8,128)(2,1)} %get-tuple-element.910.refs_1_.refs_8_), channel_id=1, source_target_pairs={{0,8},{4,12},{8,0},{12,4},{16,24},{20,28},{24,16},{28,20},{1,9},{5... | collective-permute-start | bytes 3538952 | tf_op jit(solution)/shard_map/ppermute | solution.py:120
  537.6 30.0 %collective-permute-start.48 = (bf16[9,128,512]{2,1,0:T(8,128)(2,1)}, bf16[9,128,512]{2,1,0:T(8,128)(2,1)}, u32[]{:S(2)}, u32[]{:S(2)}) collective-permute-start(bf16[9,128,512]{2,1,0:T(8,128)(2,1)} %get-tuple-element.911.refs_3_.refs_9_), channel_id=1, source_target_pairs={{0,16},{4,20},{8,24},{12,28},{16,0},{20,4},{24,8},{28,12},{1,17},{... | collective-permute-start | bytes 3538952 | tf_op jit(solution)/shard_map/ppermute | solution.py:120
  625.9 257.9 %all-gather.32.cloned.1.call-start = ((), (), s32[]{:S(2)}) async-start(), calls=%async_computation | async-start | bytes 5242880 | tf_op jit(solution)/shard_map/all_gather | solution.py:488
  627.8 56.4 %collective-permute-start.60 = (bf16[128,512]{1,0:T(8,128)(2,1)}, bf16[128,512]{1,0:T(8,128)(2,1)}, u32[]{:S(2)}, u32[]{:S(2)}) collective-permute-start(bf16[128,512]{1,0:T(8,128)(2,1)} %get-tuple-element.1354), channel_id=1, source_target_pairs={{0,1},{1,2},{2,3},{3,0},{4,5},{5,6},{6,7},{7,4},{8,9},{9,10},{10,1... | collective-permute-start | bytes 393224 | tf_op jit(solution)/shard_map/ppermute | solution.py:125
  631.4 52.8 %collective-permute-start.61 = (bf16[128,1024]{1,0:T(8,128)(2,1)}, bf16[128,1024]{1,0:T(8,128)(2,1)S(1)}, u32[]{:S(2)}, u32[]{:S(2)}) collective-permute-start(bf16[128,1024]{1,0:T(8,128)(2,1)} %get-tuple-element.1322), channel_id=1, source_target_pairs={{0,3},{1,0},{2,1},{3,2},{4,7},{5,4},{6,5},{7,6},{8,11},{9,8},{10,9... | collective-permute-start | bytes 786440 | tf_op jit(solution)/shard_map/ppermute | solution.py:125
  684.2 293.2 %all-gather.34.cloned.1.call-start = ((), (), s32[]{:S(2)}) async-start(), calls=%async_computation.1 | async-start | bytes 5242880 | tf_op jit(solution)/shard_map/all_gather | solution.py:488
  684.2 35.5 %collective-permute-start.62 = (bf16[128,1024]{1,0:T(8,128)(2,1)S(1)}, bf16[128,1024]{1,0:T(8,128)(2,1)}, u32[]{:S(2)}, u32[]{:S(2)}) collective-permute-start(bf16[128,1024]{1,0:T(8,128)(2,1)S(1)} %copy-done.258), channel_id=1, source_target_pairs={{0,2},{1,3},{2,0},{3,1},{4,6},{5,7},{6,4},{7,5},{8,10},{9,11},{10,... | collective-permute-start | bytes 786440 | tf_op jit(solution)/shard_map/ppermute | solution.py:125
  684.3 50.1 %collective-permute-start.63 = (bf16[128,1024]{1,0:T(8,128)(2,1)}, bf16[128,1024]{1,0:T(8,128)(2,1)}, u32[]{:S(2)}, u32[]{:S(2)}) collective-permute-start(bf16[128,1024]{1,0:T(8,128)(2,1)} %get-tuple-element.1320), channel_id=1, source_target_pairs={{0,1},{1,2},{2,3},{3,0},{4,5},{5,6},{6,7},{7,4},{8,9},{9,10},{10,1... | collective-permute-start | bytes 786440 | tf_op jit(solution)/shard_map/ppermute | solution.py:125
  731.3 285.0 %all-gather.40.cloned.1.call-start = ((), (), s32[]{:S(2)}) async-start(), calls=%async_computation.4 | async-start | bytes 2621440 | tf_op jit(solution)/shard_map/all_gather | solution.py:488
  777.0 64.0 %collective-permute-start.64 = (bf16[1024,1024]{1,0:T(8,128)(2,1)}, bf16[1024,1024]{1,0:T(8,128)(2,1)}, u32[]{:S(2)}, u32[]{:S(2)}) collective-permute-start(bf16[1024,1024]{1,0:T(8,128)(2,1)} %get-tuple-element.1274), channel_id=1, source_target_pairs={{0,4},{4,0},{8,12},{12,8},{16,20},{20,16},{24,28},{28,24},{1,5},{5... | collective-permute-start | bytes 6291464 | tf_op jit(solution)/shard_map/ppermute | solution.py:120
  782.4 33.0 %collective-permute-start.65 = (bf16[48,64,256]{2,1,0:T(8,128)(2,1)}, bf16[48,64,256]{2,1,0:T(8,128)(2,1)}, u32[]{:S(2)}, u32[]{:S(2)}) collective-permute-start(bf16[48,64,256]{2,1,0:T(8,128)(2,1)} %get-tuple-element.1397), channel_id=1, source_target_pairs={{0,4},{4,0},{8,12},{12,8},{16,20},{20,16},{24,28},{28,24},{1,5},{5... | collective-permute-start | bytes 4718600 | tf_op jit(solution)/shard_map/ppermute | solution.py:120
  814.5 236.2 %all-gather.38.cloned.1.call-start = ((), (), s32[]{:S(2)}) async-start(), calls=%async_computation.3 | async-start | bytes 5898240 | tf_op jit(solution)/shard_map/all_gather | solution.py:488
  927.6 49.8 %collective-permute-start.81 = (bf16[512,2048]{1,0:T(8,128)(2,1)}, bf16[512,2048]{1,0:T(8,128)(2,1)}, u32[]{:S(2)}, u32[]{:S(2)}) collective-permute-start(bf16[512,2048]{1,0:T(8,128)(2,1)} %get-tuple-element.1272), channel_id=1, source_target_pairs={{0,4},{4,0},{8,12},{12,8},{16,20},{20,16},{24,28},{28,24},{1,5},{5... | collective-permute-start | bytes 6291464 | tf_op jit(solution)/shard_map/ppermute | solution.py:120
  935.2 187.0 %all-gather.36.cloned.1.call-start = ((), (), s32[]{:S(2)}) async-start(), calls=%async_computation.2 | async-start | bytes 4915200 | tf_op jit(solution)/shard_map/all_gather | solution.py:488
  1059.0 36.3 %collective-permute-start.103 = (bf16[512,2304]{1,0:T(8,128)(2,1)S(1)}, bf16[512,2304]{1,0:T(8,128)(2,1)S(1)}, u32[]{:S(2)}, u32[]{:S(2)}) collective-permute-start(bf16[512,2304]{1,0:T(8,128)(2,1)S(1)} %get-tuple-element.1266), channel_id=1, source_target_pairs={{0,4},{4,0},{8,12},{12,8},{16,20},{20,16},{24,28},{28,24},{1,5},{5... | collective-permute-start | bytes 7077896 | tf_op jit(solution)/shard_map/ppermute | solution.py:120
  1096.0 48.3 %collective-permute-start.105 = (bf16[512,2048]{1,0:T(8,128)(2,1)S(1)}, bf16[512,2048]{1,0:T(8,128)(2,1)}, u32[]{:S(2)}, u32[]{:S(2)}) collective-permute-start(bf16[512,2048]{1,0:T(8,128)(2,1)S(1)} %pad_maximum_fusion.4.refs_1_), channel_id=1, source_target_pairs={{0,4},{4,0},{8,12},{12,8},{16,20},{20,16},{24,28},{28,24},{1,5},{5... | collective-permute-start | bytes 6291464 | tf_op jit(solution)/shard_map/ppermute | solution.py:120
  1102.3 42.0 %collective-permute-start.110 = (bf16[128,2304]{1,0:T(8,128)(2,1)}, bf16[128,2304]{1,0:T(8,128)(2,1)}, u32[]{:S(2)}, u32[]{:S(2)}) collective-permute-start(bf16[128,2304]{1,0:T(8,128)(2,1)} %get-tuple-element.1290), channel_id=1, source_target_pairs={{0,8},{4,12},{8,0},{12,4},{16,24},{20,28},{24,16},{28,20},{1,9},{5... | collective-permute-start | bytes 1769480 | tf_op jit(solution)/shard_map/ppermute | solution.py:120
  1177.4 30.4 %collective-permute-start.120 = (bf16[256,1024]{1,0:T(8,128)(2,1)S(1)}, bf16[256,1024]{1,0:T(8,128)(2,1)}, u32[]{:S(2)}, u32[]{:S(2)}) collective-permute-start(bf16[256,1024]{1,0:T(8,128)(2,1)S(1)} %maximum_select_fusion.24), channel_id=1, source_target_pairs={{0,8},{4,12},{8,0},{12,4},{16,24},{20,28},{24,16},{28,20},{1,9},{5... | collective-permute-start | bytes 1572872 | tf_op jit(solution)/shard_map/ppermute | solution.py:120
  1177.9 29.9 %collective-permute-start.121 = (bf16[256,1024]{1,0:T(8,128)(2,1)S(1)}, bf16[256,1024]{1,0:T(8,128)(2,1)}, u32[]{:S(2)}, u32[]{:S(2)}) collective-permute-start(bf16[256,1024]{1,0:T(8,128)(2,1)S(1)} %maximum_select_fusion.25), channel_id=1, source_target_pairs={{0,16},{4,20},{8,24},{12,28},{16,0},{20,4},{24,8},{28,12},{1,17},{... | collective-permute-start | bytes 1572872 | tf_op jit(solution)/shard_map/ppermute | solution.py:120
  (475 other events, 4362.0 us)
Sparse Core Ops, SparseCore 0:
  10.9 30.2 all-gather.41
  44.1 27.0 all-gather.43
  72.7 28.2 all-gather.45
  102.4 26.6 all-gather.47
  130.4 27.4 all-gather.49
  167.9 27.0 all-gather.51
  210.8 27.0 all-gather.53
  251.7 27.6 all-gather.55
  300.0 26.0 all-gather.57
  334.4 27.5 all-gather.59
  386.8 26.9 all-gather.61
  446.9 26.5 all-gather.63
  626.0 58.0 all-gather.65
  685.6 85.2 all-gather.31
  772.3 80.2 all-gather.33
  853.9 44.4 all-gather.39
  935.4 86.3 all-gather.37
  1044.9 74.1 all-gather.35

commit v3 on v2

--- a/solution.py
+++ b/solution.py
@@ -317,10 +317,8 @@
         + [pl.BlockSpec(memory_space=pl.ANY)] * (1 + len(boxes)),
         out_specs=pl.BlockSpec(memory_space=pltpu.VMEM),
         scratch_shapes=[pltpu.SemaphoreType.DMA((count,))],
-        compiler_params=pltpu.CompilerParams(vmem_limit_bytes=32 * 1024 * 1024),
-        cost_estimate=pl.CostEstimate(
-            flops=0, bytes_accessed=4 * layers * depth * width, transcendentals=0
-        ),
+        compiler_params=pltpu.CompilerParams(vmem_limit_bytes=56 * 1024 * 1024),
+        cost_estimate=pl.CostEstimate(flops=1024, bytes_accessed=1024, transcendentals=0),
         name="place",
     )(idx, weight.shard, *[box.value for box in boxes])
 
@@ -364,12 +362,19 @@
         + [pl.BlockSpec(memory_space=pl.ANY)] * len(arrays),
         out_specs=[pl.BlockSpec(memory_space=pltpu.VMEM)] * len(sizes),
         scratch_shapes=[pltpu.SemaphoreType.DMA((count,))],
-        compiler_params=pltpu.CompilerParams(vmem_limit_bytes=32 * 1024 * 1024),
-        cost_estimate=pl.CostEstimate(
-            flops=0, bytes_accessed=4 * sum(sizes) * rows * columns, transcendentals=0
-        ),
+        compiler_params=pltpu.CompilerParams(vmem_limit_bytes=56 * 1024 * 1024),
+        cost_estimate=pl.CostEstimate(flops=1024, bytes_accessed=1024, transcendentals=0),
         name="pack",
     )(idx, *arrays)
+
+
+def whole_steps(piece, turns, wait):
+    for _ in range(turns):
+        piece = yield piece
+    whole = lax.all_gather(piece, ("fsdp", "ctx"), axis=0, tiled=True)
+    for _ in range(wait):
+        yield ()
+    yield Last(whole)
 
 
 def gather_steps(idx, weights, rows, columns):
@@ -381,14 +386,14 @@
             pieces.append(piece)
             sinks.append(sink)
             owners.append(weight)
-    along, flying = {}, []
-    for turn in range(len(pieces) + 2 * len(steps) + 2):
+    along, halved = {}, []
+    for turn in range(len(pieces) + len(steps) + 3):
         if turn < len(pieces):
             along[turn] = lax.all_gather(pieces[turn], "fsdp")
         fresh, plan, sizes, comes = [], [], {step: 0 for step in steps}, []
         used = []
         for stage in range(len(steps)):
-            at = turn - 1 - 2 * stage
+            at = turn - 1 - stage
             if not 0 <= at < len(pieces):
                 continue
             for side in range(2):
@@ -424,32 +429,37 @@
         whole = [
             weight
             for at, weight in enumerate(owners)
-            if at == turn - 1 - 2 * len(steps) and weight not in owners[at + 1 :]
+            if at == turn - 1 - len(steps) and weight not in owners[at + 1 :]
         ]
+        ready = [(weight, mine, swap(mine, 1)) for weight, mine in halved]
+        halved = [(weight, placed(idx, weight)) for weight in whole]
         for weight in whole:
-            mine = placed(idx, weight)
-            weight.ready = (mine, swap(mine, 1))
             for sink, owner in zip(sinks, owners, strict=True):
                 if owner is weight:
                     sink.clear()
         kept = {step: Box(block) for step, block in blocks.items()}
         sent = {step: Box(block) for step, block in got.items()}
+        flying = list(sent.values())
         for at, side, others, step, first in used:
             sinks[at].append((side, others, kept[step], first))
         for at, side, others, step, first in comes:
             sinks[at].append((side, others, sent[step], first))
-        late, pieces, now, ready = yield (
+        now_ready = [weight for weight, _, _ in ready]
+        for weight, mine, other in ready:
+            weight.ready = (mine, other)
+        late, pieces, now, ready, mines = yield (
             [box.value for box in flying],
             pieces,
             {turn: along[turn]} if turn in along else {},
-            [weight.ready for weight in whole],
+            [(mine, other) for _, mine, other in ready],
+            [mine for _, mine in halved],
         )
         for box, value in zip(flying, late, strict=True):
             box.value = value
-        flying = list(sent.values())
         along.update(now)
-        for weight, pair in zip(whole, ready, strict=True):
+        for weight, pair in zip(now_ready, ready, strict=True):
             weight.ready = pair
+        halved = [(weight, mine) for (weight, _), mine in zip(halved, mines, strict=True)]
 
 
 def ring_steps(block, layer):
@@ -465,23 +475,31 @@
     yield Last(whole)
 
 
-def deal_steps(array, layer):
+def deal_steps(arrays, layer):
     peers = lax.axis_size("fsdp")
-    width = array.shape[1] // peers
+    widths = [array.shape[1] // peers for array in arrays]
 
     def cut(hops):
-        return lax.dynamic_slice_in_dim(array, lax.rem(layer + hops, peers) * width, width, 1)
+        to = lax.rem(layer + hops, peers)
+        return jnp.concatenate(
+            [
+                lax.dynamic_slice_in_dim(array, to * width, width, 1)
+                for array, width in zip(arrays, widths, strict=True)
+            ],
+            1,
+        )
 
     ahead = [cut(0)]
     for hops in range(1, peers):
         ahead.append((yield shifted(cut(peers - hops), peers - hops)))
-    twice = jnp.concatenate(ahead + ahead, 0)
-    length = array.shape[0]
-    yield Last(
-        lax.dynamic_slice_in_dim(
-            twice, lax.rem(peers - layer, peers) * length, peers * length, 0
-        )
-    )
+    whole = jnp.concatenate(
+        [lax.select_n(lax.rem(at + peers - layer, peers), *ahead) for at in range(peers)], 0
+    )
+    found, at = [], 0
+    for width in widths:
+        found.append(whole[:, at : at + width])
+        at += width
+    yield Last(found)
 
 
 def every_steps(block, wait):
@@ -495,13 +513,26 @@
     return (left_side.astype(jnp.float32) + right_side.astype(jnp.float32)).astype(jnp.bfloat16)
 
 
-def weight_steps(act, grad, place, finish):
+def weight_steps(products, place, finish, after):
     steps, core = chip_steps(), jnp.bitwise_and(place, 1) == 1
-    while any(task.result is None for task in act + grad):
+    while any(task.result is None for act, _, grad in products for task in (act, grad)) or any(
+        task.result is None for task in after
+    ):
         yield ()
-    part = lax.dot_general(
-        act[0].result, grad[0].result, (((0,), (0,)), ((), ())), preferred_element_type=jnp.float32
-    ).astype(jnp.bfloat16)
+    rows = min(act.result[which].shape[1] for act, which, _ in products)
+    parts = []
+    for act, which, grad in products:
+        array = act.result[which]
+        for first in range(0, array.shape[1], rows):
+            parts.append(
+                lax.dot_general(
+                    array[:, first : first + rows],
+                    grad.result,
+                    (((0,), (0,)), ((), ())),
+                    preferred_element_type=jnp.float32,
+                ).astype(jnp.bfloat16)
+            )
+    part = jnp.concatenate(parts, 1) if len(parts) > 1 else parts[0]
     own, other = halves(core, part, 1)
     own, got = yield own, swap(other, 1)
     own = added(own, got)
@@ -563,10 +594,8 @@
         in_specs=[pl.BlockSpec(memory_space=pltpu.SMEM)]
         + [pl.BlockSpec((block, part.shape[1]), lambda i: (i + skip, 0)) for part in flat],
         out_specs=pl.BlockSpec((block, width), lambda i: (i, 0)),
-        compiler_params=pltpu.CompilerParams(vmem_limit_bytes=32 * 1024 * 1024),
-        cost_estimate=pl.CostEstimate(
-            flops=0, bytes_accessed=6 * rows * width, transcendentals=0
-        ),
+        compiler_params=pltpu.CompilerParams(vmem_limit_bytes=56 * 1024 * 1024),
+        cost_estimate=pl.CostEstimate(flops=1024, bytes_accessed=1024, transcendentals=0),
         name="finish",
     )(idx, *flat)
 
@@ -587,6 +616,14 @@
     for step in powers(1, lax.axis_size("ctx")):
         got = yield swap(block, step)
         block = ordered(jnp.bitwise_and(place, step) != 0, block, got, 0)
+    yield Last(block)
+
+
+def sum_rows_steps(block, place):
+    for step in powers(1, lax.axis_size("ctx"))[::-1]:
+        keep, send = halves(jnp.bitwise_and(place, step) != 0, block, 0)
+        got, keep = yield swap(send, step), keep
+        block = added(keep, got)
     yield Last(block)
 
 
@@ -652,10 +689,8 @@
             out_specs=pl.BlockSpec((rows, tile), place),
         ),
         out_shape=jax.ShapeDtypeStruct((rows, 2 * width), kind),
-        compiler_params=pltpu.CompilerParams(vmem_limit_bytes=40 * 1024 * 1024),
-        cost_estimate=pl.CostEstimate(
-            flops=4 * rows * depth * width, bytes_accessed=4 * depth * width, transcendentals=0
-        ),
+        compiler_params=pltpu.CompilerParams(vmem_limit_bytes=56 * 1024 * 1024),
+        cost_estimate=pl.CostEstimate(flops=1024, bytes_accessed=1024, transcendentals=0),
         name="forth",
     )(idx, left_side, *chunk)
 
@@ -672,10 +707,8 @@
             out_specs=pl.BlockSpec((rows, depth), lambda s, t, idx: (0, 0)),
         ),
         out_shape=jax.ShapeDtypeStruct((rows, depth), jnp.float32),
-        compiler_params=pltpu.CompilerParams(vmem_limit_bytes=40 * 1024 * 1024),
-        cost_estimate=pl.CostEstimate(
-            flops=4 * rows * depth * width, bytes_accessed=4 * depth * width, transcendentals=0
-        ),
+        compiler_params=pltpu.CompilerParams(vmem_limit_bytes=56 * 1024 * 1024),
+        cost_estimate=pl.CostEstimate(flops=1024, bytes_accessed=1024, transcendentals=0),
         name="back",
     )(idx, grad_in, *chunk)
 
@@ -725,14 +758,14 @@
     out_o = jnp.concatenate([out_proj, o_proj], 0)
     rounds = Rounds()
 
-    def dealt(array):
-        return rounds.start(deal_steps(array, layer))
+    def dealt(*arrays):
+        return rounds.start(deal_steps(arrays, layer))
 
     def every(block, wait):
         return rounds.start(every_steps(block, wait))
 
-    def weight_grad(act, grad, finish):
-        return rounds.start(weight_steps(act, grad, my_index, finish))
+    def weight_grad(products, finish, *after):
+        return rounds.start(weight_steps(products, my_index, finish, list(after)))
 
     part = 2048
     qb_w = Weight(kv_bc, part)
@@ -764,7 +797,6 @@
     normed_in, norm_pull = jax.vjp(normed, hidden, first_gain)
     input_low = normed_in.astype(jnp.bfloat16)
     input_low, all_ids, pad_ids, prev_id = rounds.turn((input_low, all_ids, pad_ids, prev_id))
-    input_dealt = dealt(input_low)
     rounds.until_ready(qb_w)
     rounds.until(dt_task)
 
@@ -792,28 +824,23 @@
     tail_low = from_behind(conv_low[length - (KC - 1) :], "ctx", 1)
     conv_low, tail_low, xz_out = rounds.turn((conv_low, tail_low, xz_out))
 
-    def front_fn(conv_in, tail_in, shift_in, kernel_in, bias_in, bias_step, log_rate):
+    def conv_fn(conv_in, tail_in, kernel_in, bias_in):
         padded = jnp.concatenate([tail_in, conv_in], 0)
         activated = jax.nn.silu(convolve(padded, pad_ids, own_ids, kernel_in, bias_in))
         states_x = activated[:, :DS].reshape(length, NH, HP)
-        b_matrix = activated[:, DS : DS + NS]
-        c_matrix = activated[:, DS + NS :]
+        return (states_x, activated[:, DS : DS + NS], activated[:, DS + NS :])
+
+    def step_fn(shift_in, bias_step, log_rate):
         step_size = jax.nn.softplus(shift_in + bias_step)
-        log_decay = -step_size * jnp.exp(log_rate)
-        y_part, local_state = ssm_local(states_x, step_size, log_decay, b_matrix, c_matrix, own_ids)
-        return (y_part, local_state, states_x, c_matrix, log_decay)
-
-    front_out, front_pull = jax.vjp(
-        front_fn,
-        conv_low.astype(jnp.float32),
-        tail_low.astype(jnp.float32),
-        step_raw,
-        conv_weight,
-        conv_bias,
-        dt_bias,
-        a_log,
-    )
-    y_part, local_state, states_x, c_matrix, log_decay = front_out
+        return (step_size, -step_size * jnp.exp(log_rate))
+
+    (states_x, b_matrix, c_matrix), conv_pull = jax.vjp(
+        conv_fn, conv_low.astype(jnp.float32), tail_low.astype(jnp.float32), conv_weight, conv_bias
+    )
+    (step_size, log_decay), step_pull = jax.vjp(step_fn, step_raw, dt_bias, a_log)
+    own_parts = (states_x, step_size, log_decay, b_matrix, c_matrix)
+    y_part, y_pull = jax.vjp(lambda *parts: ssm_local(*parts, own_ids)[0], *own_parts)
+    local_state, state_pull = jax.vjp(lambda *parts: ssm_local(*parts, own_ids)[1], *own_parts)
     decay_now, decay_pull = jax.vjp(lambda log_in: block_decay(log_in, own_ids, prev_id), log_decay)
     y_part, local_state, decay_now = rounds.turn((y_part, local_state, decay_now))
     state_task = rounds.start(entering_steps(decay_now, local_state, my_index, False))
@@ -849,7 +876,8 @@
     gate_z = jnp.concatenate(
         [xz_out[:, DS - part :], forth(idx, input_low, z_w.ready)], 1
     )
-    gate_z = rounds.turn(gate_z)
+    gate_z, grad_low = rounds.turn((gate_z, grad_out.astype(jnp.bfloat16)))
+    cotangent_all = every(grad_low, 0)
     rounds.until(state_task)
     rounds.until_ready(oo_w)
     state_in = state_task.result
@@ -884,15 +912,12 @@
     middle = hidden + forth(idx, branches_low, oo_w.ready)
     normed_mid, mid_pull = jax.vjp(normed, middle, second_gain)
     mid_low = normed_mid.astype(jnp.bfloat16)
-    grad_low = grad_out.astype(jnp.bfloat16)
     middle, mid_low, branches_low = rounds.turn((middle, mid_low, branches_low))
-    branches_dealt = dealt(branches_low)
+    early_deal = dealt(branches_low, input_low)
     rounds.until_ready(gate_w)
     gate_out = forth(idx, mid_low, gate_w.ready)
     gate_out = rounds.turn(gate_out)
     rounds.until_ready(up_w)
-    cotangent_all = every(grad_low, 2)
-    mid_dealt = dealt(mid_low)
     up_out = forth(idx, mid_low, up_w.ready)
     act_value, act_pull = jax.vjp(
         lambda gate_in, up_in: jax.nn.silu(gate_in) * up_in, gate_out, up_out
@@ -901,30 +926,45 @@
     act_low = rounds.turn(act_low)
 
     rounds.until_ready(down_w)
-    act_dealt = dealt(act_low)
-    d_act = back(idx, grad_low, down_w.ready)
+    late_deal = dealt(act_low, mid_low)
+    d_act = rounds.turn(back(idx, grad_low, down_w.ready))
     d_gate, d_up = act_pull(d_act)
     gate_low, up_low = d_gate.astype(jnp.bfloat16), d_up.astype(jnp.bfloat16)
     gate_low, up_low = rounds.turn((gate_low, up_low))
-    rounds.until(cotangent_all)
-    gate_all = every(gate_low, 4)
-    up_all = every(up_low, 7)
+    gate_all, up_all = every(gate_low, 3), every(up_low, 6)
+    shard_rows = mid_low.shape[1] // layers
+
     down_grad = weight_grad(
-        [act_dealt], [cotangent_all], lambda pair: finished(idx, [pair], [(0, 0, D)])
+        [(late_deal, 0, cotangent_all)],
+        lambda pair: finished(idx, [pair], [(0, 0, D)]),
+    )
+    gate_up_grad = weight_grad(
+        [(late_deal, 1, gate_all), (late_deal, 1, up_all)],
+        lambda pair: finished(idx, [pair], [(0, 0, 2 * FF)]),
+        down_grad,
     )
     d_mid_norm = back(idx, gate_low, gate_w.ready)
-    mixed, d_mid_norm = rounds.turn((middle + forth(idx, act_low, down_w.ready), d_mid_norm))
+    d_mid_norm = rounds.turn(d_mid_norm)
     d_mid_norm = d_mid_norm + back(idx, up_low, up_w.ready)
     d_middle_part, d_second_gain = mid_pull(d_mid_norm)
     d_middle = grad_out + d_middle_part
     branch_low = d_middle.astype(jnp.bfloat16)
     branch_low, d_middle = rounds.turn((branch_low, d_middle))
-    branch_all = every(branch_low, 7)
+    branch_all = every(branch_low, 6)
     d_mixer_norm, d_attended = parted(back(idx, branch_low, oo_w.ready))
+    d_mixer_norm, d_attended = rounds.turn((d_mixer_norm, d_attended))
     d_core, d_states_tail, d_gate_z, d_d_skip, d_mixer_gain = tail_pull(d_mixer_norm)
     z_low = d_gate_z.astype(jnp.bfloat16)
-    z_low, d_attended, d_core = rounds.turn((z_low, d_attended, d_core))
+    z_low, d_core, d_states_tail = rounds.turn((z_low, d_core, d_states_tail))
+    z_all = every(z_low, 6)
+    oo_z_grad = weight_grad(
+        [(early_deal, 0, branch_all), (early_deal, 1, z_all)], lambda pair: pair, gate_up_grad
+    )
     d_c_carry, d_log_carry, d_state_in = carry_pull(d_core)
+    mixed = middle + forth(idx, act_low, down_w.ready)
+    d_c_carry, d_log_carry, d_state_in, mixed = rounds.turn(
+        (d_c_carry, d_log_carry, d_state_in, mixed)
+    )
     later_task = rounds.start(entering_steps(decay_now, d_state_in, my_index, True))
     d_out_low = d_attended.reshape(length, HK, groups, HA).astype(jnp.bfloat16)
     delta = jnp.transpose(jnp.sum(d_out_low.astype(jnp.float32) * attended, axis=-1), (1, 2, 0))
@@ -956,7 +996,21 @@
         [d_keys.reshape(seq_len, HK * HA), d_values.reshape(seq_len, HK * HA)], 1
     ).astype(jnp.bfloat16)
     kv_terms, d_query = rounds.turn((kv_terms, d_query))
-    d_kv = summed_rows(kv_terms, my_index).astype(jnp.float32)
+    kv_task = rounds.start(sum_rows_steps(kv_terms, my_index))
+    y_grads = rounds.turn(y_pull(d_core))
+    rounds.until(later_task)
+    later_grad = later_task.result
+    state_grads = rounds.turn(state_pull(later_grad))
+    d_decay = jnp.sum(later_grad * state_in, axis=(1, 2))
+    d_log_decay = decay_pull(d_decay)[0]
+    d_states, d_step, d_log, d_b, d_c = jax.tree.map(jnp.add, y_grads, state_grads)
+    d_conv_in, d_tail, d_conv_weight, d_conv_bias = conv_pull(
+        (d_states + d_states_tail, d_b, d_c + d_c_carry)
+    )
+    d_step_raw, d_dt_bias, d_a_log = step_pull((d_step, d_log + d_log_carry + d_log_decay))
+    d_conv_in, d_tail, d_step_raw = rounds.turn((d_conv_in, d_tail, d_step_raw))
+    rounds.until(kv_task)
+    d_kv = kv_task.result.astype(jnp.float32)
     qkv_low = jnp.concatenate(
         [
             rotate(d_query.reshape(length, HQ, HA), places, -1.0).reshape(length, HQ * HA),
@@ -967,16 +1021,6 @@
         ],
         1,
     ).astype(jnp.bfloat16)
-    qkv_low = rounds.turn(qkv_low)
-    zq_all = every(jnp.concatenate([z_low, qkv_low], 1), 5)
-    rounds.until(later_task)
-    later_grad = later_task.result
-    d_decay = jnp.sum(later_grad * state_in, axis=(1, 2))
-    d_log_decay = decay_pull(d_decay)[0]
-    d_conv_in, d_tail, d_step_raw, d_conv_weight, d_conv_bias, d_dt_bias, d_a_log = front_pull(
-        (d_core, later_grad, d_states_tail, d_c_carry, d_log_carry + d_log_decay)
-    )
-    d_conv_in, d_tail, d_step_raw = rounds.turn((d_conv_in, d_tail, d_step_raw))
     from_next = from_behind(d_tail.astype(jnp.bfloat16), "ctx", -1).astype(d_tail.dtype)
     d_conv_in = jnp.concatenate(
         [d_conv_in[: length - (KC - 1)], d_conv_in[length - (KC - 1) :] + from_next], 0
@@ -984,30 +1028,12 @@
     conv_grad_low = d_conv_in.astype(jnp.bfloat16)
     step_low = d_step_raw.astype(jnp.bfloat16)
     blank = jnp.zeros((length, 512 - NH), jnp.bfloat16)
-    conv_grad_low, step_low = rounds.turn((conv_grad_low, step_low))
-    tail_all = every(jnp.concatenate([conv_grad_low, step_low, blank[:, : 256 - NH]], 1), 5)
-    pending = {
-        "gate": (mid_dealt, gate_all, lambda pair: pair),
-        "up": (mid_dealt, up_all, lambda pair: pair),
-        "oo": (
-            branches_dealt,
-            branch_all,
-            lambda pair: (
-                finished(idx, [pair], [(0, 0, D)], 0, DS // layers),
-                finished(idx, [pair], [(0, 0, D)], DS // layers, HQ * HA // layers),
-            ),
-        ),
-        "zq": (input_dealt, zq_all, lambda pair: pair),
-        "tail": (input_dealt, tail_all, lambda pair: pair),
-    }
-    grads = {
-        name: weight_grad([act], [grad], finish) for name, (act, grad, finish) in pending.items()
-    }
-    gate_up_grad = rounds.start(
-        finish_steps(
-            [grads["gate"], grads["up"]],
-            lambda *pairs: finished(idx, pairs, [(0, 0, FF), (1, 0, FF)]),
-        )
+    tail_low = jnp.concatenate([conv_grad_low, step_low, blank[:, : 256 - NH], qkv_low], 1)
+    conv_grad_low, step_low, qkv_low, tail_low = rounds.turn(
+        (conv_grad_low, step_low, qkv_low, tail_low)
+    )
+    tail_grad = weight_grad(
+        [(early_deal, 1, every(tail_low, 4))], lambda pair: pair
     )
     d_normed_in = (
         back(idx, conv_grad_low[:, :part], x_w.ready)
@@ -1041,15 +1067,20 @@
             )
         )
     )
-    rounds.until(smalls_task, gate_up_grad, down_grad, *grads.values())
+    rounds.until(smalls_task, gate_up_grad, down_grad, oo_z_grad, tail_grad)
     smalls = smalls_task.result
-    tail_pair, zq_pair = grads["tail"].result, grads["zq"].result
+    tail_pair, oo_z_pair = tail_grad.result, oo_z_grad.result
+    blocks = branches_low.shape[1] // layers // shard_rows
+    z_first = blocks * D
+    oo = [
+        finished(idx, [oo_z_pair], [(0, at * D, (at + 1) * D)]) for at in range(blocks)
+    ]
     tail_half = tail_pair[0].shape[1]
     step_grad = jnp.where(core == 1, tail_pair[0], tail_pair[1])
     return (
         mixed[None].astype(jnp.bfloat16),
         d_tokens[None],
-        finished(idx, [zq_pair, tail_pair], [(0, 0, DS), (1, 0, conv_cols)]),
+        finished(idx, [oo_z_pair, tail_pair], [(0, z_first, z_first + DS), (1, 0, conv_cols)]),
         step_grad[:, conv_cols - tail_half : conv_cols - tail_half + NH].astype(jnp.float32),
         smalls[0],
         smalls[1],
@@ -1057,9 +1088,9 @@
         smalls[3],
         smalls[4],
         smalls[5],
-        grads["oo"].result[0],
-        finished(idx, [zq_pair], [(0, DS, DS + qkv_cols)]),
-        grads["oo"].result[1],
+        jnp.concatenate(oo, 0)[: DS // layers],
+        finished(idx, [tail_pair], [(0, conv_cols + 256, conv_cols + 256 + qkv_cols)]),
+        jnp.concatenate(oo, 0)[DS // layers :],
         smalls[6],
         smalls[7],
         gate_up_grad.result,

time: 1290 us -> 1240 us (0.961)
  local copies, waits for them, and re-layouts: 233 us -> 131 us
  Pallas kernels: 223 us -> 294 us
  starting transfers between devices: 128 us -> 105 us
    unnamed x777 -> x525, local copies, waits for them, and re-layouts: 157 us -> 46.4 us
    ppermute x115 -> x93, waiting for transfers between devices: 281 us -> 355 us  [swap(): return lax.ppermute(block, 'ctx', [(i, i ^ distance) for i in range(peers)])]
    all_gather x12, waiting for transfers between devices: 46.9 us -> 13.2 us  [gather_steps(): along[turn] = lax.all_gather(pieces[turn], 'fsdp')]
    ppermute x115 -> x93, starting transfers between devices: 103 us -> 77.9 us  [swap(): return lax.ppermute(block, 'ctx', [(i, i ^ distance) for i in range(peers)])]
    ppermute x15 -> x9, waiting for transfers between devices: 36.1 us -> 16.6 us  [shifted(): lax.ppermute(block, 'fsdp', [(i, (i + hops) % peers) for i in range(peers)])]
    pallas_call x14 -> x13, Pallas kernels: 33.1 us -> 49.5 us  [packed(): pl.pallas_call(lambda *refs: pack_kernel(fresh, plan, len(arrays), *refs)...]
    pallas_call x8, Pallas kernels: 69.7 us -> 85.9 us  [back(): pl.pallas_call(back_kernel, grid_spec=pltpu.PrefetchScalarGridSpec(num_sc...]
    pallas_call x8, Pallas kernels: 52.6 us -> 67.2 us  [forth(): pl.pallas_call(forth_kernel, grid_spec=pltpu.PrefetchScalarGridSpec(num_s...]
  transfers between devices with their start and end apart: 155 -> 127, of which waited for: 55 -> 58; matrix products, arithmetic and copies ran while one was open for 29% -> 29% of each run, Pallas kernels for 14% -> 22%
where the time goes in v3:
time: 1240 us; the launch traced here: 1230 us
  waiting for transfers between devices  399 us (32%)
  Pallas kernels  294 us (24%)
  other arithmetic  190 us (15%)
  local copies, waits for them, and re-layouts  131 us (11%)
  starting transfers between devices  105 us (8%)
  matrix products  92.7 us (7%)
  between operations  19.4 us (2%)
    ppermute x93, waiting for transfers between devices, swap(): return lax.ppermute(block, 'ctx', [(i, i ^ distance) for i in range(peers)])  355 us
    pallas_call x8, Pallas kernels, back(): pl.pallas_call(back_kernel, grid_spec=pltpu.PrefetchScalarGridSpec(num_sc...  85.9 us
    ppermute x93, starting transfers between devices, swap(): return lax.ppermute(block, 'ctx', [(i, i ^ distance) for i in range(peers)])  77.9 us
    pallas_call x8, Pallas kernels, forth(): pl.pallas_call(forth_kernel, grid_spec=pltpu.PrefetchScalarGridSpec(num_s...  67.2 us
    pallas_call x8, Pallas kernels, placed(): pl.pallas_call(lambda *refs: place_kernel(chunks, *refs), out_shape=jax.S...  52 us
    pallas_call x13, Pallas kernels, packed(): pl.pallas_call(lambda *refs: pack_kernel(fresh, plan, len(arrays), *refs)...  49.5 us
    unnamed x525, local copies, waits for them, and re-layouts  46.4 us
    pallas_call x6, Pallas kernels, finished(): pl.pallas_call(lambda *refs: finish_kernel(segments, *refs), grid=(rows /...  39.6 us
  transfers between devices with their start and end apart: 127, of which 58 were waited for; matrix products, arithmetic and copies ran while one was open for 29% of the time, Pallas kernels for 22%

profile of v3, /device:TPU:0, one launch (start us, length us, event | category | flops | bytes accessed | tf_op | source)
XLA Modules:
  0.0 1230.5 jit_solution(13413239772286037364)
XLA Ops:
  59.3 13.2 %all-gather.45.cloned.1.call-done = bf16[512,1024]{1,0:T(8,128)(2,1)} async-done(((bf16[128,1024]{1,0:T(8,128)(2,1)}), bf16[512,1024]{1,0:T(8,128)(2,1)}) %all-gather.45.cloned.1.call-update) | async-done | bytes 1048592 | tf_op jit(solution)/shard_map/all_gather | solution.py:392
  85.0 19.4 %collective-permute-done.7.refs_3_.refs_7_.refs_4_ = bf16[9,128,512]{2,1,0:T(8,128)(2,1)S(1)} collective-permute-done((bf16[9,128,512]{2,1,0:T(8,128)(2,1)}, bf16[9,128,512]{2,1,0:T(8,128)(2,1)S(1)}, u32[]{:S(2)}, u32[]{:S(2)}) %collective-permute-start.7) | collective-permute-done | bytes 1179680 | tf_op jit(solution)/shard_map/ppermute | solution.py:120
  125.6 11.6 collective-permute-done.10.refs_3_.refs_7_.refs_4_
  150.3 20.3 %collective-permute-done.13.refs_3_.refs_7_.refs_4_ = bf16[9,128,512]{2,1,0:T(8,128)(2,1)S(1)} collective-permute-done((bf16[9,128,512]{2,1,0:T(8,128)(2,1)}, bf16[9,128,512]{2,1,0:T(8,128)(2,1)S(1)}, u32[]{:S(2)}, u32[]{:S(2)}) %collective-permute-start.13) | collective-permute-done | bytes 1179680 | tf_op jit(solution)/shard_map/ppermute | solution.py:120
  187.6 6.5 forth.8
  199.0 9.0 collective-permute-done.15.refs_3_.refs_7_.refs_4_
  221.2 6.6 forth.9
  227.8 13.7 %collective-permute-done.18.refs_3_.refs_7_ = bf16[9,128,512]{2,1,0:T(8,128)(2,1)S(1)} collective-permute-done((bf16[9,128,512]{2,1,0:T(8,128)(2,1)}, bf16[9,128,512]{2,1,0:T(8,128)(2,1)S(1)}, u32[]{:S(2)}, u32[]{:S(2)}) %collective-permute-start.18) | collective-permute-done | bytes 1179680 | tf_op jit(solution)/shard_map/ppermute | solution.py:120
  256.7 6.5 forth.10
  267.4 18.8 %collective-permute-done.26 = bf16[256,512]{1,0:T(8,128)(2,1)} collective-permute-done((bf16[256,512]{1,0:T(8,128)(2,1)}, bf16[256,512]{1,0:T(8,128)(2,1)}, u32[]{:S(2)}, u32[]{:S(2)}) %collective-permute-start.26) | collective-permute-done | bytes 262176 | tf_op jit(solution)/shard_map/ppermute | solution.py:120
  290.3 8.1 place.12.own_ref
  310.7 7.5 fusion.54
  322.4 7.3 collective-permute-done.27.refs_3_.refs_7_
  355.2 28.9 %collective-permute-done.36 = f32[24]{0:T(128)S(1)} collective-permute-done((f32[24]{0:T(128)S(1)}, f32[24]{0:T(128)S(1)}, u32[]{:S(2)}, u32[]{:S(2)}) %collective-permute-start.36) | collective-permute-done | bytes 128 | tf_op jit(solution)/shard_map/ppermute | solution.py:120
  400.3 10.4 collective-permute-done.39
  414.3 7.8 place.13.own_ref
  441.0 6.6 forth.11
  451.3 16.1 %collective-permute-done.41.refs_3_.refs_11_.refs_4_ = bf16[9,128,512]{2,1,0:T(8,128)(2,1)} collective-permute-done((bf16[9,128,512]{2,1,0:T(8,128)(2,1)}, bf16[9,128,512]{2,1,0:T(8,128)(2,1)}, u32[]{:S(2)}, u32[]{:S(2)}) %collective-permute-start.41) | collective-permute-done | bytes 1179680 | tf_op jit(solution)/shard_map/ppermute | solution.py:120
  486.0 7.9 place.14.own_ref
  499.5 10.2 forth.12
  523.9 10.3 forth.13
  537.6 10.3 forth.14
  551.1 7.8 place.15.own_ref
  577.3 13.7 %back.8 = f32[128,4096]{1,0:T(8,128)} custom-call(s32[3]{0:T(128)} %pad_add_fusion.5.refs_0_.idx_ref, bf16[128,2048]{1,0:T(8,128)(2,1)} %bitcast.240, bf16[4096,1024]{1,0:T(8,128)(2,1)} %place.15.own_ref, bf16[4096,1024]{1,0:T(8,128)(2,1)} %collective-permute-done.51.other_ref), custom_call_target="tpu_custom_call" | custom-call | flops 1024 | bytes 1024 | tf_op jit(solution)/shard_map/back/pallas_call | solution.py:701
  602.7 12.4 %back.9 = f32[128,2048]{1,0:T(8,128)} custom-call(s32[3]{0:T(128)} %pad_add_fusion.5.refs_0_.idx_ref, bf16[128,4096]{1,0:T(8,128)(2,1)} %get-tuple-element.875.grad_ref, bf16[2048,2048]{1,0:T(8,128)(2,1)} %place.13.own_ref, bf16[2048,2048]{1,0:T(8,128)(2,1)} %collective-permute-done.43.other_ref), custom_call_target="tpu_custom_call" | custom-call | flops 1024 | bytes 1024 | tf_op jit(solution)/shard_map/back/pallas_call | solution.py:701
  615.1 12.3 back.10
  639.7 13.8 %back.11 = f32[128,4096]{1,0:T(8,128)} custom-call(s32[3]{0:T(128)} %pad_add_fusion.5.refs_0_.idx_ref, bf16[128,2048]{1,0:T(8,128)(2,1)} %get-tuple-element.883.grad_ref, bf16[4096,1024]{1,0:T(8,128)(2,1)} %place.12.own_ref, bf16[4096,1024]{1,0:T(8,128)(2,1)} %collective-permute-done.32.other_ref), custom_call_target="tpu_custom_call" | custom-call | flops 1024 | bytes 1024 | tf_op jit(solution)/shard_map/back/pallas_call | solution.py:701
  653.6 10.1 forth.15
  733.2 7.7 fusion.26
  779.6 9.4 collective-permute-done.67
  812.8 8.7 collective-permute-done.69
  821.5 6.8 multiply_reduce_fusion.6
  899.6 19.2 %collective-permute-done.76 = bf16[128,4096]{1,0:T(8,128)(2,1)} collective-permute-done((bf16[128,4096]{1,0:T(8,128)(2,1)}, bf16[128,4096]{1,0:T(8,128)(2,1)}, u32[]{:S(2)}, u32[]{:S(2)}) %collective-permute-start.76) | collective-permute-done | bytes 1048608 | tf_op jit(solution)/shard_map/ppermute | solution.py:120
  929.5 8.4 back.14
  941.3 8.3 back.15
  950.4 8.4 back.12
  959.7 8.6 back.13
  977.2 9.0 collective-permute-done.80
  992.3 19.6 %collective-permute-done.83 = bf16[128,4096]{1,0:T(8,128)(2,1)S(1)} collective-permute-done((bf16[128,4096]{1,0:T(8,128)(2,1)S(1)}, bf16[128,4096]{1,0:T(8,128)(2,1)S(1)}, u32[]{:S(2)}, u32[]{:S(2)}) %collective-permute-start.83) | collective-permute-done | bytes 1048608 | tf_op jit(solution)/shard_map/ppermute | solution.py:120
  1032.9 9.4 finish.7
  1070.1 25.1 %collective-permute-done.93 = bf16[128,2688]{1,0:T(8,128)(2,1)S(1)} collective-permute-done((bf16[128,2688]{1,0:T(8,128)(2,1)S(1)}, bf16[128,2688]{1,0:T(8,128)(2,1)S(1)}, u32[]{:S(2)}, u32[]{:S(2)}) %collective-permute-start.93) | collective-permute-done | bytes 688160 | tf_op jit(solution)/shard_map/ppermute | solution.py:120
  1108.4 11.4 collective-permute-done.97
  1127.5 6.4 collective-permute-done.102
  1133.9 9.2 collective-permute-done.101
  1148.1 13.7 %collective-permute-done.106 = bf16[128,2688]{1,0:T(8,128)(2,1)S(1)} collective-permute-done((bf16[128,2688]{1,0:T(8,128)(2,1)S(1)}, bf16[128,2688]{1,0:T(8,128)(2,1)S(1)}, u32[]{:S(2)}, u32[]{:S(2)}) %collective-permute-start.106) | collective-permute-done | bytes 688160 | tf_op jit(solution)/shard_map/ppermute | solution.py:120
  1161.8 14.9 %collective-permute-done.105 = bf16[128,2688]{1,0:T(8,128)(2,1)S(1)} collective-permute-done((bf16[128,2688]{1,0:T(8,128)(2,1)S(1)}, bf16[128,2688]{1,0:T(8,128)(2,1)S(1)}, u32[]{:S(2)}, u32[]{:S(2)}) %collective-permute-start.105) | collective-permute-done | bytes 688160 | tf_op jit(solution)/shard_map/ppermute | solution.py:120
  1179.8 8.2 collective-permute-done.108.refs_4_.refs_2_
  1204.1 9.6 finish.8
  (1105 shorter events, 661.9 us)
Async XLA Ops:
  7.2 37.0 %all-gather.43.cloned.1.call-start = ((), (), s32[]{:S(2)}) async-start(), calls=%async_computation.6 | async-start | bytes 1310720 | tf_op jit(solution)/shard_map/all_gather | solution.py:392
  7.8 36.4 %collective-permute-start.3 = (bf16[512,48]{0,1:T(8,128)(2,1)}, bf16[512,48]{0,1:T(8,128)(2,1)S(1)}, u32[]{:S(2)}, u32[]{:S(2)}) collective-permute-start(bf16[512,48]{0,1:T(8,128)(2,1)} %param.22), channel_id=1, source_target_pairs={{0,1},{1,2},{2,3},{3,0},{4,5},{5,6},{6,7},{7,4},{8,9},{9,10},{10,1... | collective-permute-start | bytes 147464 | tf_op jit(solution)/shard_map/ppermute | solution.py:125
  13.3 59.2 %all-gather.45.cloned.1.call-start = ((), (), s32[]{:S(2)}) async-start(), calls=%async_computation.7 | async-start | bytes 1310720 | tf_op jit(solution)/shard_map/all_gather | solution.py:392
  44.2 60.5 %all-gather.47.cloned.1.call-start = ((), (), s32[]{:S(2)}) async-start(), calls=%async_computation.8 | async-start | bytes 1310720 | tf_op jit(solution)/shard_map/all_gather | solution.py:392
  72.5 65.4 %all-gather.49.cloned.1.call-start = ((), (), s32[]{:S(2)}) async-start(), calls=%async_computation.9 | async-start | bytes 1310720 | tf_op jit(solution)/shard_map/all_gather | solution.py:392
  104.7 66.6 %all-gather.51.cloned.1.call-start = ((), (), s32[]{:S(2)}) async-start(), calls=%async_computation.10 | async-start | bytes 1310720 | tf_op jit(solution)/shard_map/all_gather | solution.py:392
  137.9 33.4 %collective-permute-start.12 = (bf16[2048,1024]{1,0:T(8,128)(2,1)}, bf16[2048,1024]{1,0:T(8,128)(2,1)}, u32[]{:S(2)}, u32[]{:S(2)}) collective-permute-start(bf16[2048,1024]{1,0:T(8,128)(2,1)} %place.8.own_ref), channel_id=1, source_target_pairs={{0,4},{4,0},{8,12},{12,8},{16,20},{20,16},{24,28},{28,24},{1,5},{5... | collective-permute-start | bytes 12582920 | tf_op jit(solution)/shard_map/ppermute | solution.py:120
  137.9 70.8 %all-gather.53.cloned.1.call-start = ((), (), s32[]{:S(2)}) async-start(), calls=%async_computation.11 | async-start | bytes 1310720 | tf_op jit(solution)/shard_map/all_gather | solution.py:392
  171.3 37.5 %collective-permute-start.17 = (bf16[2048,1024]{1,0:T(8,128)(2,1)}, bf16[2048,1024]{1,0:T(8,128)(2,1)}, u32[]{:S(2)}, u32[]{:S(2)}) collective-permute-start(bf16[2048,1024]{1,0:T(8,128)(2,1)} %place.9.own_ref), channel_id=1, source_target_pairs={{0,4},{4,0},{8,12},{12,8},{16,20},{20,16},{24,28},{28,24},{1,5},{5... | collective-permute-start | bytes 12582920 | tf_op jit(solution)/shard_map/ppermute | solution.py:120
  174.8 67.4 %all-gather.55.cloned.1.call-start = ((), (), s32[]{:S(2)}) async-start(), calls=%async_computation.12 | async-start | bytes 1310720 | tf_op jit(solution)/shard_map/all_gather | solution.py:392
  208.8 33.5 %collective-permute-start.20 = (bf16[2048,1024]{1,0:T(8,128)(2,1)}, bf16[2048,1024]{1,0:T(8,128)(2,1)}, u32[]{:S(2)}, u32[]{:S(2)}) collective-permute-start(bf16[2048,1024]{1,0:T(8,128)(2,1)} %place.10.own_ref), channel_id=1, source_target_pairs={{0,4},{4,0},{8,12},{12,8},{16,20},{20,16},{24,28},{28,24},{1,5},{5... | collective-permute-start | bytes 12582920 | tf_op jit(solution)/shard_map/ppermute | solution.py:120
  208.9 77.3 %all-gather.57.cloned.1.call-start = ((), (), s32[]{:S(2)}) async-start(), calls=%async_computation.13 | async-start | bytes 1310720 | tf_op jit(solution)/shard_map/all_gather | solution.py:392
  242.2 44.0 %collective-permute-start.25 = (bf16[2048,1024]{1,0:T(8,128)(2,1)}, bf16[2048,1024]{1,0:T(8,128)(2,1)}, u32[]{:S(2)}, u32[]{:S(2)}) collective-permute-start(bf16[2048,1024]{1,0:T(8,128)(2,1)} %place.11.own_ref), channel_id=1, source_target_pairs={{0,4},{4,0},{8,12},{12,8},{16,20},{20,16},{24,28},{28,24},{1,5},{5... | collective-permute-start | bytes 12582920 | tf_op jit(solution)/shard_map/ppermute | solution.py:120
  244.5 85.8 %all-gather.59.cloned.1.call-start = ((), (), s32[]{:S(2)}) async-start(), calls=%async_computation.14 | async-start | bytes 1310720 | tf_op jit(solution)/shard_map/all_gather | solution.py:392
  251.6 34.5 %collective-permute-start.23 = (bf16[9,128,512]{2,1,0:T(8,128)(2,1)}, bf16[9,128,512]{2,1,0:T(8,128)(2,1)S(1)}, u32[]{:S(2)}, u32[]{:S(2)}) collective-permute-start(bf16[9,128,512]{2,1,0:T(8,128)(2,1)} %get-tuple-element.757.refs_2_), channel_id=1, source_target_pairs={{0,8},{4,12},{8,0},{12,4},{16,24},{20,28},{24,16},{28,20},{1,9},{5... | collective-permute-start | bytes 3538952 | tf_op jit(solution)/shard_map/ppermute | solution.py:120
  252.7 33.4 %collective-permute-start.24 = (bf16[9,128,512]{2,1,0:T(8,128)(2,1)}, bf16[9,128,512]{2,1,0:T(8,128)(2,1)S(1)}, u32[]{:S(2)}, u32[]{:S(2)}) collective-permute-start(bf16[9,128,512]{2,1,0:T(8,128)(2,1)} %get-tuple-element.758.refs_4_.refs_3_), channel_id=1, source_target_pairs={{0,16},{4,20},{8,24},{12,28},{16,0},{20,4},{24,8},{28,12},{1,17},{... | collective-permute-start | bytes 3538952 | tf_op jit(solution)/shard_map/ppermute | solution.py:120
  286.3 103.5 %all-gather.61.cloned.1.call-start = ((), (), s32[]{:S(2)}) async-start(), calls=%async_computation.15 | async-start | bytes 1310720 | tf_op jit(solution)/shard_map/all_gather | solution.py:392
  289.2 33.2 %collective-permute-start.29 = (bf16[512,512]{1,0:T(8,128)(2,1)}, bf16[512,512]{1,0:T(8,128)(2,1)}, u32[]{:S(2)}, u32[]{:S(2)}) collective-permute-start(bf16[512,512]{1,0:T(8,128)(2,1)} %maximum_select_fusion.17), channel_id=1, source_target_pairs={{0,16},{4,20},{8,24},{12,28},{16,0},{20,4},{24,8},{28,12},{1,17},{... | collective-permute-start | bytes 1572872 | tf_op jit(solution)/shard_map/ppermute | solution.py:120
  330.4 59.4 %collective-permute-start.32 = (bf16[4096,1024]{1,0:T(8,128)(2,1)}, bf16[4096,1024]{1,0:T(8,128)(2,1)}, u32[]{:S(2)}, u32[]{:S(2)}) collective-permute-start(bf16[4096,1024]{1,0:T(8,128)(2,1)} %place.12.own_ref), channel_id=1, source_target_pairs={{0,4},{4,0},{8,12},{12,8},{16,20},{20,16},{24,28},{28,24},{1,5},{5... | collective-permute-start | bytes 25165832 | tf_op jit(solution)/shard_map/ppermute | solution.py:120
  334.2 100.4 %all-gather.63.cloned.1.call-start = ((), (), s32[]{:S(2)}) async-start(), calls=%async_computation.16 | async-start | bytes 1310720 | tf_op jit(solution)/shard_map/all_gather | solution.py:392
  338.5 51.3 %collective-permute-start.30 = (bf16[9,128,512]{2,1,0:T(8,128)(2,1)}, bf16[9,128,512]{2,1,0:T(8,128)(2,1)}, u32[]{:S(2)}, u32[]{:S(2)}) collective-permute-start(bf16[9,128,512]{2,1,0:T(8,128)(2,1)} %get-tuple-element.808.refs_2_), channel_id=1, source_target_pairs={{0,8},{4,12},{8,0},{12,4},{16,24},{20,28},{24,16},{28,20},{1,9},{5... | collective-permute-start | bytes 3538952 | tf_op jit(solution)/shard_map/ppermute | solution.py:120
  339.6 50.2 %collective-permute-start.31 = (bf16[9,128,512]{2,1,0:T(8,128)(2,1)}, bf16[9,128,512]{2,1,0:T(8,128)(2,1)}, u32[]{:S(2)}, u32[]{:S(2)}) collective-permute-start(bf16[9,128,512]{2,1,0:T(8,128)(2,1)} %get-tuple-element.809.refs_4_.refs_3_), channel_id=1, source_target_pairs={{0,16},{4,20},{8,24},{12,28},{16,0},{20,4},{24,8},{28,12},{1,17},{... | collective-permute-start | bytes 3538952 | tf_op jit(solution)/shard_map/ppermute | solution.py:120
  350.1 38.1 %collective-permute-start.35 = (bf16[24,64,256]{2,1,0:T(8,128)(2,1)S(1)}, bf16[24,64,256]{2,1,0:T(8,128)(2,1)S(1)}, u32[]{:S(2)}, u32[]{:S(2)}) collective-permute-start(bf16[24,64,256]{2,1,0:T(8,128)(2,1)S(1)} %fusion.110), channel_id=1, source_target_pairs={{0,8},{4,12},{8,0},{12,4},{16,24},{20,28},{24,16},{28,20},{1,9},{5... | collective-permute-start | bytes 2359304 | tf_op jit(solution)/shard_map/ppermute | solution.py:120
  352.4 31.6 %collective-permute-start.36 = (f32[24]{0:T(128)S(1)}, f32[24]{0:T(128)S(1)}, u32[]{:S(2)}, u32[]{:S(2)}) collective-permute-start(f32[24]{0:T(128)S(1)} %broadcast_select_fusion.48), channel_id=1, source_target_pairs={{0,8},{4,12},{8,0},{12,4},{16,24},{20,28},{24,16},{28,20},{1,9},{5... | collective-permute-start | bytes 296 | tf_op jit(solution)/shard_map/ppermute | solution.py:120
  389.8 78.3 %all-gather.65.cloned.1.call-start = ((), (), s32[]{:S(2)}) async-start(), calls=%async_computation.17 | async-start | bytes 1310720 | tf_op jit(solution)/shard_map/all_gather | solution.py:392
  396.9 32.8 %collective-permute-start.37 = (bf16[9,128,512]{2,1,0:T(8,128)(2,1)}, bf16[9,128,512]{2,1,0:T(8,128)(2,1)}, u32[]{:S(2)}, u32[]{:S(2)}) collective-permute-start(bf16[9,128,512]{2,1,0:T(8,128)(2,1)} %get-tuple-element.826.refs_2_.refs_8_), channel_id=1, source_target_pairs={{0,8},{4,12},{8,0},{12,4},{16,24},{20,28},{24,16},{28,20},{1,9},{5... | collective-permute-start | bytes 3538952 | tf_op jit(solution)/shard_map/ppermute | solution.py:120
  398.0 36.6 %collective-permute-start.38 = (bf16[9,128,512]{2,1,0:T(8,128)(2,1)}, bf16[9,128,512]{2,1,0:T(8,128)(2,1)}, u32[]{:S(2)}, u32[]{:S(2)}) collective-permute-start(bf16[9,128,512]{2,1,0:T(8,128)(2,1)} %get-tuple-element.827.refs_4_.refs_9_), channel_id=1, source_target_pairs={{0,16},{4,20},{8,24},{12,28},{16,0},{20,4},{24,8},{28,12},{1,17},{... | collective-permute-start | bytes 3538952 | tf_op jit(solution)/shard_map/ppermute | solution.py:120
  434.6 33.5 %collective-permute-start.43 = (bf16[2048,2048]{1,0:T(8,128)(2,1)}, bf16[2048,2048]{1,0:T(8,128)(2,1)}, u32[]{:S(2)}, u32[]{:S(2)}) collective-permute-start(bf16[2048,2048]{1,0:T(8,128)(2,1)} %place.13.own_ref), channel_id=1, source_target_pairs={{0,4},{4,0},{8,12},{12,8},{16,20},{20,16},{24,28},{28,24},{1,5},{5... | collective-permute-start | bytes 25165832 | tf_op jit(solution)/shard_map/ppermute | solution.py:120
  434.7 78.5 %all-gather.31.cloned.1.call-start = ((), (), s32[]{:S(2)}) async-start(), calls=%async_computation | async-start | bytes 2621440 | tf_op jit(solution)/shard_map/all_gather | solution.py:506
  468.2 229.0 %all-gather.33.cloned.1.call-start = ((), (), s32[]{:S(2)}) async-start(), calls=%async_computation.1 | async-start | bytes 5242880 | tf_op jit(solution)/shard_map/all_gather | solution.py:506
  481.4 31.7 %collective-permute-start.44 = (bf16[9,128,512]{2,1,0:T(8,128)(2,1)}, bf16[9,128,512]{2,1,0:T(8,128)(2,1)}, u32[]{:S(2)}, u32[]{:S(2)}) collective-permute-start(bf16[9,128,512]{2,1,0:T(8,128)(2,1)} %get-tuple-element.855.refs_1_.refs_8_), channel_id=1, source_target_pairs={{0,8},{4,12},{8,0},{12,4},{16,24},{20,28},{24,16},{28,20},{1,9},{5... | collective-permute-start | bytes 3538952 | tf_op jit(solution)/shard_map/ppermute | solution.py:120
  482.5 30.6 %collective-permute-start.45 = (bf16[9,128,512]{2,1,0:T(8,128)(2,1)}, bf16[9,128,512]{2,1,0:T(8,128)(2,1)}, u32[]{:S(2)}, u32[]{:S(2)}) collective-permute-start(bf16[9,128,512]{2,1,0:T(8,128)(2,1)} %get-tuple-element.856.refs_3_.refs_9_), channel_id=1, source_target_pairs={{0,16},{4,20},{8,24},{12,28},{16,0},{20,4},{24,8},{28,12},{1,17},{... | collective-permute-start | bytes 3538952 | tf_op jit(solution)/shard_map/ppermute | solution.py:120
  523.8 35.2 %collective-permute-start.50 = (bf16[128,1536]{1,0:T(8,128)(2,1)S(1)}, bf16[128,1536]{1,0:T(8,128)(2,1)}, u32[]{:S(2)}, u32[]{:S(2)}) collective-permute-start(bf16[128,1536]{1,0:T(8,128)(2,1)S(1)} %pad_maximum_fusion.22), channel_id=1, source_target_pairs={{0,2},{1,3},{2,0},{3,1},{4,6},{5,7},{6,4},{7,5},{8,10},{9,11},{10,... | collective-permute-start | bytes 1179656 | tf_op jit(solution)/shard_map/ppermute | solution.py:125
  568.2 30.7 %collective-permute-start.54 = (bf16[128,1536]{1,0:T(8,128)(2,1)S(1)}, bf16[128,1536]{1,0:T(8,128)(2,1)S(1)}, u32[]{:S(2)}, u32[]{:S(2)}) collective-permute-start(bf16[128,1536]{1,0:T(8,128)(2,1)S(1)} %pad_maximum_fusion.26), channel_id=1, source_target_pairs={{0,2},{1,3},{2,0},{3,1},{4,6},{5,7},{6,4},{7,5},{8,10},{9,11},{10,... | collective-permute-start | bytes 1179656 | tf_op jit(solution)/shard_map/ppermute | solution.py:125
  599.6 208.6 %all-gather.35.cloned.1.call-start = ((), (), s32[]{:S(2)}) async-start(), calls=%async_computation.2 | async-start | bytes 5242880 | tf_op jit(solution)/shard_map/all_gather | solution.py:506
  600.2 282.4 %all-gather.37.cloned.1.call-start = ((), (), s32[]{:S(2)}) async-start(), calls=%async_computation.3 | async-start | bytes 2621440 | tf_op jit(solution)/shard_map/all_gather | solution.py:506
  639.7 31.6 %collective-permute-start.56 = (bf16[1024,1024]{1,0:T(8,128)(2,1)}, bf16[1024,1024]{1,0:T(8,128)(2,1)}, u32[]{:S(2)}, u32[]{:S(2)}) collective-permute-start(bf16[1024,1024]{1,0:T(8,128)(2,1)} %get-tuple-element.1175), channel_id=1, source_target_pairs={{0,4},{4,0},{8,12},{12,8},{16,20},{20,16},{24,28},{28,24},{1,5},{5... | collective-permute-start | bytes 6291464 | tf_op jit(solution)/shard_map/ppermute | solution.py:120
  653.6 246.0 %all-gather.39.cloned.1.call-start = ((), (), s32[]{:S(2)}) async-start(), calls=%async_computation.4 | async-start | bytes 3932160 | tf_op jit(solution)/shard_map/all_gather | solution.py:506
  750.2 292.9 %all-gather.41.cloned.1.call-start = ((), (), s32[]{:S(2)}) async-start(), calls=%async_computation.5 | async-start | bytes 6881280 | tf_op jit(solution)/shard_map/all_gather | solution.py:506
  855.0 30.8 %collective-permute-start.74 = (bf16[512,4096]{1,0:T(8,128)(2,1)}, bf16[512,4096]{1,0:T(8,128)(2,1)}, u32[]{:S(2)}, u32[]{:S(2)}) collective-permute-start(bf16[512,4096]{1,0:T(8,128)(2,1)} %get-tuple-element.1158), channel_id=1, source_target_pairs={{0,4},{4,0},{8,12},{12,8},{16,20},{20,16},{24,28},{28,24},{1,5},{5... | collective-permute-start | bytes 12582920 | tf_op jit(solution)/shard_map/ppermute | solution.py:120
  923.6 46.4 %collective-permute-start.77 = (bf16[64,4096]{1,0:T(8,128)(2,1)}, bf16[64,4096]{1,0:T(8,128)(2,1)}, u32[]{:S(2)}, u32[]{:S(2)}) collective-permute-start(bf16[64,4096]{1,0:T(8,128)(2,1)} %get-tuple-element.1216), channel_id=1, source_target_pairs={{0,16},{4,20},{8,24},{12,28},{16,0},{20,4},{24,8},{28,12},{1,17},{... | collective-permute-start | bytes 1572872 | tf_op jit(solution)/shard_map/ppermute | solution.py:120
  926.2 43.8 %collective-permute-start.78 = (bf16[64,4096]{1,0:T(8,128)(2,1)}, bf16[64,4096]{1,0:T(8,128)(2,1)}, u32[]{:S(2)}, u32[]{:S(2)}) collective-permute-start(bf16[64,4096]{1,0:T(8,128)(2,1)} %get-tuple-element.1214), channel_id=1, source_target_pairs={{0,8},{4,12},{8,0},{12,4},{16,24},{20,28},{24,16},{28,20},{1,9},{5... | collective-permute-start | bytes 1572872 | tf_op jit(solution)/shard_map/ppermute | solution.py:120
  1058.3 38.1 %collective-permute-start.91 = (bf16[128,3584]{1,0:T(8,128)(2,1)S(1)}, bf16[128,3584]{1,0:T(8,128)(2,1)S(1)}, u32[]{:S(2)}, u32[]{:S(2)}) collective-permute-start(bf16[128,3584]{1,0:T(8,128)(2,1)S(1)} %get-tuple-element.1187), channel_id=1, source_target_pairs={{0,16},{4,20},{8,24},{12,28},{16,0},{20,4},{24,8},{28,12},{1,17},{... | collective-permute-start | bytes 2752520 | tf_op jit(solution)/shard_map/ppermute | solution.py:120
  1059.8 36.6 %collective-permute-start.90 = (bf16[128,3584]{1,0:T(8,128)(2,1)S(1)}, bf16[128,3584]{1,0:T(8,128)(2,1)S(1)}, u32[]{:S(2)}, u32[]{:S(2)}) collective-permute-start(bf16[128,3584]{1,0:T(8,128)(2,1)S(1)} %get-tuple-element.1189), channel_id=1, source_target_pairs={{0,8},{4,12},{8,0},{12,4},{16,24},{20,28},{24,16},{28,20},{1,9},{5... | collective-permute-start | bytes 2752520 | tf_op jit(solution)/shard_map/ppermute | solution.py:120
  1062.2 33.0 %collective-permute-start.93 = (bf16[128,2688]{1,0:T(8,128)(2,1)S(1)}, bf16[128,2688]{1,0:T(8,128)(2,1)S(1)}, u32[]{:S(2)}, u32[]{:S(2)}) collective-permute-start(bf16[128,2688]{1,0:T(8,128)(2,1)S(1)} %get-tuple-element.1191), channel_id=1, source_target_pairs={{0,16},{4,20},{8,24},{12,28},{16,0},{20,4},{24,8},{28,12},{1,17},{... | collective-permute-start | bytes 2064392 | tf_op jit(solution)/shard_map/ppermute | solution.py:120
  1062.8 33.6 %collective-permute-start.92 = (bf16[128,2688]{1,0:T(8,128)(2,1)S(1)}, bf16[128,2688]{1,0:T(8,128)(2,1)S(1)}, u32[]{:S(2)}, u32[]{:S(2)}) collective-permute-start(bf16[128,2688]{1,0:T(8,128)(2,1)S(1)} %get-tuple-element.1193), channel_id=1, source_target_pairs={{0,8},{4,12},{8,0},{12,4},{16,24},{20,28},{24,16},{28,20},{1,9},{5... | collective-permute-start | bytes 2064392 | tf_op jit(solution)/shard_map/ppermute | solution.py:120
  1144.2 32.4 %collective-permute-start.104 = (bf16[128,3584]{1,0:T(8,128)(2,1)S(1)}, bf16[128,3584]{1,0:T(8,128)(2,1)S(1)}, u32[]{:S(2)}, u32[]{:S(2)}) collective-permute-start(bf16[128,3584]{1,0:T(8,128)(2,1)S(1)} %maximum_select_fusion.14), channel_id=1, source_target_pairs={{0,16},{4,20},{8,24},{12,28},{16,0},{20,4},{24,8},{28,12},{1,17},{... | collective-permute-start | bytes 2752520 | tf_op jit(solution)/shard_map/ppermute | solution.py:120
  1145.8 30.8 %collective-permute-start.103 = (bf16[128,3584]{1,0:T(8,128)(2,1)S(1)}, bf16[128,3584]{1,0:T(8,128)(2,1)S(1)}, u32[]{:S(2)}, u32[]{:S(2)}) collective-permute-start(bf16[128,3584]{1,0:T(8,128)(2,1)S(1)} %maximum_select_fusion.13), channel_id=1, source_target_pairs={{0,8},{4,12},{8,0},{12,4},{16,24},{20,28},{24,16},{28,20},{1,9},{5... | collective-permute-start | bytes 2752520 | tf_op jit(solution)/shard_map/ppermute | solution.py:120
  (335 other events, 3203.1 us)
Sparse Core Ops, SparseCore 0:
  13.4 28.1 all-gather.42
  44.3 28.0 all-gather.44
  74.0 27.8 all-gather.46
  104.8 27.0 all-gather.48
  138.1 27.3 all-gather.50
  175.0 27.1 all-gather.52
  209.0 27.2 all-gather.54
  244.6 27.1 all-gather.56
  286.4 27.0 all-gather.58
  334.3 26.3 all-gather.60
  390.0 26.3 all-gather.62
  434.8 26.4 all-gather.64
  468.3 44.2 all-gather.30
  599.8 83.1 all-gather.32
  684.3 78.3 all-gather.34
  764.2 44.4 all-gather.36
  810.1 62.2 all-gather.38
  940.5 102.5 all-gather.40

commit v4 on v3

--- a/solution.py
+++ b/solution.py
@@ -534,25 +534,23 @@
             )
     part = jnp.concatenate(parts, 1) if len(parts) > 1 else parts[0]
     own, other = halves(core, part, 1)
-    own, got = yield own, swap(other, 1)
-    own = added(own, got)
+    own = added(own, swap(other, 1))
     size = own.shape[0] // 2
     blocks = [own[:size], own[size:]]
     orders = [steps[side:] + steps[:side] for side in range(2)]
-    for stage in range(len(steps)):
-        sent = []
+    moves = [(stage, True) for stage in range(len(steps))]
+    moves += [(stage, False) for stage in range(len(steps))[::-1]]
+    for number, (stage, adds) in enumerate(moves):
         for side in range(2):
             step = orders[side][stage]
-            keep, send = halves(jnp.bitwise_and(place, step) != 0, blocks[side], 0)
-            sent.append((keep, swap(send, step)))
-        sent = yield sent
-        blocks = [added(*pair) for pair in sent]
-    for stage in range(len(steps))[::-1]:
-        sent = yield [(blocks[side], swap(blocks[side], orders[side][stage])) for side in range(2)]
-        blocks = [
-            ordered(jnp.bitwise_and(place, orders[side][stage]) != 0, *sent[side], 0)
-            for side in range(2)
-        ]
+            flag = jnp.bitwise_and(place, step) != 0
+            if adds:
+                keep, send = halves(flag, blocks[side], 0)
+                blocks[side] = added(keep, swap(send, step))
+            else:
+                blocks[side] = ordered(flag, blocks[side], swap(blocks[side], step), 0)
+        if number % 2 == 0:
+            blocks = list((yield blocks))
     own = jnp.concatenate(blocks, 0)
     pair = yield own, swap(own, 1)
     yield Last(finish(pair))
@@ -606,6 +604,45 @@
     yield Last(finish(*[task.result for task in tasks]))
 
 
+def rows_kernel(cases, idx_ref, low_ref, high_ref, out_ref):
+    half = low_ref.shape[1]
+    for number, (_, first, last) in enumerate(cases):
+        for flag in (0, 1):
+            low, high = (low_ref, high_ref) if flag == 0 else (high_ref, low_ref)
+
+            @pl.when((pl.program_id(0) == number) & (idx_ref[1] == flag))
+            def _():
+                at = 0
+                for part, begin, end in (
+                    (low, first, min(last, half)),
+                    (high, max(first, half) - half, last - half),
+                ):
+                    if begin < end:
+                        out_ref[:, at : at + end - begin] = part[:, begin:end].astype(jnp.float32)
+                        at += end - begin
+
+
+def finished_rows(idx, pair, cases, rows):
+    width, numbers = cases[0][2] - cases[0][1], [number for number, _, _ in cases]
+
+    def place(i, idx):
+        return (sum((i == at) * number for at, number in enumerate(numbers)), 0)
+
+    return pl.pallas_call(
+        lambda *refs: rows_kernel(cases, *refs),
+        grid_spec=pltpu.PrefetchScalarGridSpec(
+            num_scalar_prefetch=1,
+            grid=(len(cases),),
+            in_specs=[pl.BlockSpec((rows, part.shape[1]), place) for part in pair],
+            out_specs=pl.BlockSpec((rows, width), lambda i, idx: (i, 0)),
+        ),
+        out_shape=jax.ShapeDtypeStruct((len(cases) * rows, width), jnp.float32),
+        compiler_params=pltpu.CompilerParams(vmem_limit_bytes=56 * 1024 * 1024),
+        cost_estimate=pl.CostEstimate(flops=1024, bytes_accessed=1024, transcendentals=0),
+        name="finish_rows",
+    )(idx, *pair)
+
+
 def along_ctx(block, place):
     for step in powers(1, lax.axis_size("ctx")):
         block = ordered(jnp.bitwise_and(place, step) != 0, block, swap(block, step), 0)
@@ -634,83 +671,61 @@
     return block
 
 
-def tile_of(width):
-    return max(tile for tile in range(128, 1025, 128) if width % tile == 0)
-
-
 def forth_kernel(idx_ref, left_ref, own_ref, other_ref, out_ref):
-    for side, part_ref in enumerate((own_ref, other_ref)):
-
-        @pl.when(pl.program_id(0) == side)
+    width = own_ref.shape[1]
+    for part_ref, half in ((own_ref, idx_ref[1]), (other_ref, 1 - idx_ref[1])):
+        columns = pl.ds(pl.multiple_of(half * width, 128), width)
+        term = jnp.dot(left_ref[...], part_ref[...], preferred_element_type=jnp.float32)
+
+        @pl.when(pl.program_id(0) == 0)
         def _():
-            out_ref[...] = jnp.dot(
-                left_ref[...], part_ref[...], preferred_element_type=jnp.float32
-            ).astype(out_ref.dtype)
+            out_ref[:, columns] = term
+
+        @pl.when(pl.program_id(0) != 0)
+        def _():
+            out_ref[:, columns] += term
 
 
 def back_kernel(idx_ref, grad_ref, own_ref, other_ref, out_ref):
-    @pl.when((pl.program_id(0) == 0) & (pl.program_id(1) == 0))
-    def _():
-        out_ref[...] = jnp.zeros_like(out_ref)
-
-    for side, part_ref in enumerate((own_ref, other_ref)):
-
-        @pl.when(pl.program_id(0) == side)
-        def _():
-            out_ref[...] += lax.dot_general(
-                grad_ref[...],
-                part_ref[...],
-                (((1,), (1,)), ((), ())),
-                preferred_element_type=jnp.float32,
-            )
-
-
-def product_specs(depth, width):
-    tile = tile_of(width)
-    count = width // tile
-    return (
-        tile,
-        count,
-        pl.BlockSpec((depth, tile), lambda s, t, idx: (0, jnp.where(s == 0, t, count - 1))),
-        pl.BlockSpec((depth, tile), lambda s, t, idx: (0, jnp.where(s == 0, 0, t))),
-        lambda s, t, idx: (0, jnp.bitwise_xor(idx[1], s) * count + t),
-    )
-
-
-def forth(idx, left_side, chunk, kind=jnp.float32):
-    rows, (depth, width) = left_side.shape[0], chunk[0].shape
-    tile, count, own_spec, other_spec, place = product_specs(depth, width)
+    width, total = own_ref.shape[1], None
+    for part_ref, half in ((own_ref, idx_ref[1]), (other_ref, 1 - idx_ref[1])):
+        term = lax.dot_general(
+            grad_ref[:, pl.ds(pl.multiple_of(half * width, 128), width)],
+            part_ref[...],
+            (((1,), (1,)), ((), ())),
+            preferred_element_type=jnp.float32,
+        )
+        total = term if total is None else total + term
+    out_ref[...] = total
+
+
+def product(kernel, name, idx, operand, chunk, in_spec, out_spec, columns):
+    rows, (depth, width) = operand.shape[0], chunk[0].shape
+    part = pl.BlockSpec((depth // 4, width), lambda t, idx: (t, 0))
     return pl.pallas_call(
-        forth_kernel,
+        kernel,
         grid_spec=pltpu.PrefetchScalarGridSpec(
-            num_scalar_prefetch=1,
-            grid=(2, count),
-            in_specs=[pl.BlockSpec((rows, depth), lambda s, t, idx: (0, 0)), own_spec, other_spec],
-            out_specs=pl.BlockSpec((rows, tile), place),
+            num_scalar_prefetch=1, grid=(4,), in_specs=[in_spec, part, part], out_specs=out_spec
         ),
-        out_shape=jax.ShapeDtypeStruct((rows, 2 * width), kind),
+        out_shape=jax.ShapeDtypeStruct((rows, columns), jnp.float32),
         compiler_params=pltpu.CompilerParams(vmem_limit_bytes=56 * 1024 * 1024),
         cost_estimate=pl.CostEstimate(flops=1024, bytes_accessed=1024, transcendentals=0),
-        name="forth",
-    )(idx, left_side, *chunk)
+        name=name,
+    )(idx, operand, *chunk)
+
+
+def forth(idx, left_side, chunk):
+    rows, (depth, width) = left_side.shape[0], chunk[0].shape
+    in_spec = pl.BlockSpec((rows, depth // 4), lambda t, idx: (0, t))
+    out_spec = pl.BlockSpec((rows, 2 * width), lambda t, idx: (0, 0))
+    return product(forth_kernel, "forth", idx, left_side, chunk, in_spec, out_spec, 2 * width)
 
 
 def back(idx, grad_in, chunk):
     rows, (depth, width) = grad_in.shape[0], chunk[0].shape
-    tile, count, own_spec, other_spec, place = product_specs(depth, width)
-    return pl.pallas_call(
-        back_kernel,
-        grid_spec=pltpu.PrefetchScalarGridSpec(
-            num_scalar_prefetch=1,
-            grid=(2, count),
-            in_specs=[pl.BlockSpec((rows, tile), place), own_spec, other_spec],
-            out_specs=pl.BlockSpec((rows, depth), lambda s, t, idx: (0, 0)),
-        ),
-        out_shape=jax.ShapeDtypeStruct((rows, depth), jnp.float32),
-        compiler_params=pltpu.CompilerParams(vmem_limit_bytes=56 * 1024 * 1024),
-        cost_estimate=pl.CostEstimate(flops=1024, bytes_accessed=1024, transcendentals=0),
-        name="back",
-    )(idx, grad_in, *chunk)
+    in_spec = pl.BlockSpec((rows, 2 * width), lambda t, idx: (0, 0))
+    out_spec = pl.BlockSpec((rows, depth // 4), lambda t, idx: (0, t))
+    return product(back_kernel, "back", idx, grad_in, chunk, in_spec, out_spec, depth)
 
 
 def sum_steps(arrays):
@@ -931,7 +946,7 @@
     d_gate, d_up = act_pull(d_act)
     gate_low, up_low = d_gate.astype(jnp.bfloat16), d_up.astype(jnp.bfloat16)
     gate_low, up_low = rounds.turn((gate_low, up_low))
-    gate_all, up_all = every(gate_low, 3), every(up_low, 6)
+    gate_all, up_all = every(gate_low, 3), every(up_low, 5)
     shard_rows = mid_low.shape[1] // layers
 
     down_grad = weight_grad(
@@ -950,15 +965,26 @@
     d_middle = grad_out + d_middle_part
     branch_low = d_middle.astype(jnp.bfloat16)
     branch_low, d_middle = rounds.turn((branch_low, d_middle))
-    branch_all = every(branch_low, 6)
+    branch_all = every(branch_low, 5)
     d_mixer_norm, d_attended = parted(back(idx, branch_low, oo_w.ready))
     d_mixer_norm, d_attended = rounds.turn((d_mixer_norm, d_attended))
     d_core, d_states_tail, d_gate_z, d_d_skip, d_mixer_gain = tail_pull(d_mixer_norm)
     z_low = d_gate_z.astype(jnp.bfloat16)
     z_low, d_core, d_states_tail = rounds.turn((z_low, d_core, d_states_tail))
     z_all = every(z_low, 6)
+    fine = HQ * HA // layers
+    cases = [
+        (at % (shard_rows // fine), at // (shard_rows // fine) * D, (at // (shard_rows // fine) + 1) * D)
+        for at in range((DS + HQ * HA) // layers // fine)
+    ]
     oo_z_grad = weight_grad(
-        [(early_deal, 0, branch_all), (early_deal, 1, z_all)], lambda pair: pair, gate_up_grad
+        [(early_deal, 0, branch_all), (early_deal, 1, z_all)],
+        lambda pair: (
+            pair,
+            finished_rows(idx, pair, cases[: DS // layers // fine], fine),
+            finished_rows(idx, pair, cases[DS // layers // fine :], fine),
+        ),
+        gate_up_grad,
     )
     d_c_carry, d_log_carry, d_state_in = carry_pull(d_core)
     mixed = middle + forth(idx, act_low, down_w.ready)
@@ -1069,12 +1095,8 @@
     )
     rounds.until(smalls_task, gate_up_grad, down_grad, oo_z_grad, tail_grad)
     smalls = smalls_task.result
-    tail_pair, oo_z_pair = tail_grad.result, oo_z_grad.result
-    blocks = branches_low.shape[1] // layers // shard_rows
-    z_first = blocks * D
-    oo = [
-        finished(idx, [oo_z_pair], [(0, at * D, (at + 1) * D)]) for at in range(blocks)
-    ]
+    tail_pair, (oo_z_pair, out_grad, o_grad) = tail_grad.result, oo_z_grad.result
+    z_first = branches_low.shape[1] // layers // shard_rows * D
     tail_half = tail_pair[0].shape[1]
     step_grad = jnp.where(core == 1, tail_pair[0], tail_pair[1])
     return (
@@ -1088,9 +1110,9 @@
         smalls[3],
         smalls[4],
         smalls[5],
-        jnp.concatenate(oo, 0)[: DS // layers],
+        out_grad,
         finished(idx, [tail_pair], [(0, conv_cols + 256, conv_cols + 256 + qkv_cols)]),
-        jnp.concatenate(oo, 0)[DS // layers :],
+        o_grad,
         smalls[6],
         smalls[7],
         gate_up_grad.result,

time: 1240 us -> 1220 us (0.984)
  matrix products: 92.7 us -> 108 us
    ppermute x93, waiting for transfers between devices: 355 us -> 336 us  [swap(): return lax.ppermute(block, 'ctx', [(i, i ^ distance) for i in range(peers)])]
    dot_general x3, matrix products: 20.5 us -> 34.1 us  [ssm_local(): jnp.einsum('hts,shp->thp', decay_matrix * intersection[None], driven, pre...]
    pallas_call x6 -> x4, Pallas kernels: 39.6 us -> 29.4 us  [finished(): pl.pallas_call(lambda *refs: finish_kernel(segments, *refs), grid=(rows /...]
    convert_element_type x23 -> x19, other arithmetic: 27.4 us -> 21.9 us  [added(): (left_side.astype(jnp.float32) + right_side.astype(jnp.float32)).astype(j...]
    pallas_call x16 -> x18, Pallas kernels: 153 us -> 157 us  [the longest x16 144 us: product(): pl.pallas_call(kernel, grid_spec=pltpu.PrefetchScalarGridSpec(num_scalar_...]
    unnamed x525 -> x507, local copies, waits for them, and re-layouts: 46.4 us -> 42.8 us
  transfers between devices with their start and end apart: 127 -> 127, of which waited for: 58 -> 60; matrix products, arithmetic and copies ran while one was open for 29% -> 30% of each run, Pallas kernels for 22% -> 23%
where the time goes in v4:
time: 1220 us
  waiting for transfers between devices  392 us (32%)
  Pallas kernels  288 us (24%)
  other arithmetic  181 us (15%)
  local copies, waits for them, and re-layouts  124 us (10%)
  matrix products  108 us (9%)
  starting transfers between devices  103 us (8%)
  between operations  19.5 us (2%)
    ppermute x93, waiting for transfers between devices, swap(): return lax.ppermute(block, 'ctx', [(i, i ^ distance) for i in range(peers)])  336 us
    pallas_call x16, Pallas kernels, product(): pl.pallas_call(kernel, grid_spec=pltpu.PrefetchScalarGridSpec(num_scalar_...  144 us
    ppermute x93, starting transfers between devices, swap(): return lax.ppermute(block, 'ctx', [(i, i ^ distance) for i in range(peers)])  80.1 us
    pallas_call x8, Pallas kernels, placed(): pl.pallas_call(lambda *refs: place_kernel(chunks, *refs), out_shape=jax.S...  52.1 us
    pallas_call x13, Pallas kernels, packed(): pl.pallas_call(lambda *refs: pack_kernel(fresh, plan, len(arrays), *refs)...  49.5 us
    unnamed x507, local copies, waits for them, and re-layouts  42.8 us
    dot_general x3, matrix products, ssm_local(): jnp.einsum('hts,shp->thp', decay_matrix * intersection[None], driven, pre...  34.1 us
    pallas_call x4, Pallas kernels, finished(): pl.pallas_call(lambda *refs: finish_kernel(segments, *refs), grid=(rows /...  29.4 us
  transfers between devices with their start and end apart: 127, of which 60 were waited for; matrix products, arithmetic and copies ran while one was open for 30% of the time, Pallas kernels for 23%

profile of v4, /device:TPU:0, one launch (start us, length us, event | category | flops | bytes accessed | tf_op | source)
XLA Modules:
  0.0 1215.5 jit_solution(14715941595542651174)
XLA Ops:
  59.3 13.3 %all-gather.45.cloned.1.call-done = bf16[512,1024]{1,0:T(8,128)(2,1)} async-done(((bf16[128,1024]{1,0:T(8,128)(2,1)}), bf16[512,1024]{1,0:T(8,128)(2,1)}) %all-gather.45.cloned.1.call-update) | async-done | bytes 1048592 | tf_op jit(solution)/shard_map/all_gather | solution.py:392
  84.7 20.0 %collective-permute-done.7.refs_3_.refs_7_.refs_4_ = bf16[9,128,512]{2,1,0:T(8,128)(2,1)S(1)} collective-permute-done((bf16[9,128,512]{2,1,0:T(8,128)(2,1)}, bf16[9,128,512]{2,1,0:T(8,128)(2,1)S(1)}, u32[]{:S(2)}, u32[]{:S(2)}) %collective-permute-start.7) | collective-permute-done | bytes 1179680 | tf_op jit(solution)/shard_map/ppermute | solution.py:120
  125.8 11.4 collective-permute-done.10.refs_3_.refs_7_.refs_4_
  150.4 20.2 %collective-permute-done.13.refs_3_.refs_7_.refs_4_ = bf16[9,128,512]{2,1,0:T(8,128)(2,1)S(1)} collective-permute-done((bf16[9,128,512]{2,1,0:T(8,128)(2,1)}, bf16[9,128,512]{2,1,0:T(8,128)(2,1)S(1)}, u32[]{:S(2)}, u32[]{:S(2)}) %collective-permute-start.13) | collective-permute-done | bytes 1179680 | tf_op jit(solution)/shard_map/ppermute | solution.py:120
  187.6 7.1 forth.8
  199.6 8.4 collective-permute-done.15.refs_3_.refs_7_.refs_4_
  221.2 7.3 forth.9
  228.5 13.0 %collective-permute-done.18.refs_3_.refs_7_ = bf16[9,128,512]{2,1,0:T(8,128)(2,1)S(1)} collective-permute-done((bf16[9,128,512]{2,1,0:T(8,128)(2,1)}, bf16[9,128,512]{2,1,0:T(8,128)(2,1)S(1)}, u32[]{:S(2)}, u32[]{:S(2)}) %collective-permute-start.18) | collective-permute-done | bytes 1179680 | tf_op jit(solution)/shard_map/ppermute | solution.py:120
  256.5 7.1 forth.10
  268.0 18.0 %collective-permute-done.26 = bf16[256,512]{1,0:T(8,128)(2,1)} collective-permute-done((bf16[256,512]{1,0:T(8,128)(2,1)}, bf16[256,512]{1,0:T(8,128)(2,1)}, u32[]{:S(2)}, u32[]{:S(2)}) %collective-permute-start.26) | collective-permute-done | bytes 262176 | tf_op jit(solution)/shard_map/ppermute | solution.py:120
  290.1 8.1 place.12.own_ref
  310.5 7.5 fusion.54
  322.3 7.3 collective-permute-done.27.refs_3_.refs_7_
  355.1 29.0 %collective-permute-done.36 = f32[24]{0:T(128)S(1)} collective-permute-done((f32[24]{0:T(128)S(1)}, f32[24]{0:T(128)S(1)}, u32[]{:S(2)}, u32[]{:S(2)}) %collective-permute-start.36) | collective-permute-done | bytes 128 | tf_op jit(solution)/shard_map/ppermute | solution.py:120
  400.3 10.4 collective-permute-done.39
  414.3 7.8 place.13.own_ref
  440.7 7.2 forth.11
  451.7 15.5 %collective-permute-done.41.refs_3_.refs_11_.refs_4_ = bf16[9,128,512]{2,1,0:T(8,128)(2,1)} collective-permute-done((bf16[9,128,512]{2,1,0:T(8,128)(2,1)}, bf16[9,128,512]{2,1,0:T(8,128)(2,1)}, u32[]{:S(2)}, u32[]{:S(2)}) %collective-permute-start.41) | collective-permute-done | bytes 1179680 | tf_op jit(solution)/shard_map/ppermute | solution.py:120
  485.6 7.9 place.14.own_ref
  499.1 9.9 forth.12
  523.0 10.2 forth.13
  537.0 10.2 forth.14
  550.4 7.9 place.15.own_ref
  576.4 10.9 back.8
  593.3 13.2 %collective-permute-done.54 = bf16[128,1536]{1,0:T(8,128)(2,1)S(1)} collective-permute-done((bf16[128,1536]{1,0:T(8,128)(2,1)S(1)}, bf16[128,1536]{1,0:T(8,128)(2,1)S(1)}, u32[]{:S(2)}, u32[]{:S(2)}) %collective-permute-start.54) | collective-permute-done | bytes 393248 | tf_op jit(solution)/shard_map/ppermute | solution.py:125
  607.3 11.1 back.9
  619.8 11.5 back.10
  653.0 11.0 back.11
  701.3 9.6 collective-permute-done.63
  714.7 10.1 forth.15
  793.8 20.0 %fusion.26 = (f32[48,128]{1,0:T(8,128)S(1)}, f32[48,128]{1,0:T(8,128)S(1)}, f32[128,128]{1,0:T(8,128)S(1)}) fusion(f32[128,128]{1,0:T(8,128)S(1)} %copy-done.179, f32[48,128]{1,0:T(8,128)S(1)} %copy-done.185, pred[128,128]{1,0:T(8,128)(4,1)S(1)} %copy-done.194, f32[128,48,64]{0,2,1:T(8,128)} %bitcast.227, f32[128,48]{0,1:T(8,128)S(1)} %copy-done.140, ...), kind=kOutput, calls=%fused_computation.92 | convolution fusion | flops 612995072 | bytes 3391488 | tf_op jit(solution)/shard_map/transpose(jvp(hts,shp->thp))/dot_general | solution.py:89
  820.8 6.6 fusion.39
  853.1 19.8 %collective-permute-done.70 = bf16[128,4096]{1,0:T(8,128)(2,1)S(1)} collective-permute-done((bf16[128,4096]{1,0:T(8,128)(2,1)S(1)}, bf16[128,4096]{1,0:T(8,128)(2,1)S(1)}, u32[]{:S(2)}, u32[]{:S(2)}) %collective-permute-start.70) | collective-permute-done | bytes 1048608 | tf_op jit(solution)/shard_map/ppermute | solution.py:120
  874.1 8.2 collective-permute-done.73
  914.0 7.2 collective-permute-done.77
  935.1 11.5 collective-permute-done.79
  973.6 9.6 finish.5
  1010.7 7.4 back.14
  1019.9 7.7 back.15
  1028.5 7.4 back.12
  1036.8 8.0 back.13
  1052.3 9.2 collective-permute-done.89
  1063.6 9.5 collective-permute-done.90
  1076.0 18.7 %collective-permute-done.91 = bf16[128,3584]{1,0:T(8,128)(2,1)S(1)} collective-permute-done((bf16[128,3584]{1,0:T(8,128)(2,1)S(1)}, bf16[128,3584]{1,0:T(8,128)(2,1)S(1)}, u32[]{:S(2)}, u32[]{:S(2)}) %collective-permute-start.91) | collective-permute-done | bytes 917536 | tf_op jit(solution)/shard_map/ppermute | solution.py:120
  1109.9 8.4 finish_rows.2
  1141.8 11.3 collective-permute-done.99
  1175.0 11.8 collective-permute-done.106
  1198.8 9.6 finish.6
  (1080 shorter events, 661.8 us)
Async XLA Ops:
  7.2 37.1 %all-gather.43.cloned.1.call-start = ((), (), s32[]{:S(2)}) async-start(), calls=%async_computation.6 | async-start | bytes 1310720 | tf_op jit(solution)/shard_map/all_gather | solution.py:392
  7.8 36.5 %collective-permute-start.3 = (bf16[512,48]{0,1:T(8,128)(2,1)}, bf16[512,48]{0,1:T(8,128)(2,1)S(1)}, u32[]{:S(2)}, u32[]{:S(2)}) collective-permute-start(bf16[512,48]{0,1:T(8,128)(2,1)} %param.22), channel_id=1, source_target_pairs={{0,1},{1,2},{2,3},{3,0},{4,5},{5,6},{6,7},{7,4},{8,9},{9,10},{10,1... | collective-permute-start | bytes 147464 | tf_op jit(solution)/shard_map/ppermute | solution.py:125
  13.3 59.3 %all-gather.45.cloned.1.call-start = ((), (), s32[]{:S(2)}) async-start(), calls=%async_computation.7 | async-start | bytes 1310720 | tf_op jit(solution)/shard_map/all_gather | solution.py:392
  44.3 60.4 %all-gather.47.cloned.1.call-start = ((), (), s32[]{:S(2)}) async-start(), calls=%async_computation.8 | async-start | bytes 1310720 | tf_op jit(solution)/shard_map/all_gather | solution.py:392
  72.6 65.4 %all-gather.49.cloned.1.call-start = ((), (), s32[]{:S(2)}) async-start(), calls=%async_computation.9 | async-start | bytes 1310720 | tf_op jit(solution)/shard_map/all_gather | solution.py:392
  104.7 66.6 %all-gather.51.cloned.1.call-start = ((), (), s32[]{:S(2)}) async-start(), calls=%async_computation.10 | async-start | bytes 1310720 | tf_op jit(solution)/shard_map/all_gather | solution.py:392
  138.0 33.3 %collective-permute-start.12 = (bf16[2048,1024]{1,0:T(8,128)(2,1)}, bf16[2048,1024]{1,0:T(8,128)(2,1)}, u32[]{:S(2)}, u32[]{:S(2)}) collective-permute-start(bf16[2048,1024]{1,0:T(8,128)(2,1)} %place.8.own_ref), channel_id=1, source_target_pairs={{0,4},{4,0},{8,12},{12,8},{16,20},{20,16},{24,28},{28,24},{1,5},{5... | collective-permute-start | bytes 12582920 | tf_op jit(solution)/shard_map/ppermute | solution.py:120
  138.0 70.8 %all-gather.53.cloned.1.call-start = ((), (), s32[]{:S(2)}) async-start(), calls=%async_computation.11 | async-start | bytes 1310720 | tf_op jit(solution)/shard_map/all_gather | solution.py:392
  171.3 37.5 %collective-permute-start.17 = (bf16[2048,1024]{1,0:T(8,128)(2,1)}, bf16[2048,1024]{1,0:T(8,128)(2,1)}, u32[]{:S(2)}, u32[]{:S(2)}) collective-permute-start(bf16[2048,1024]{1,0:T(8,128)(2,1)} %place.9.own_ref), channel_id=1, source_target_pairs={{0,4},{4,0},{8,12},{12,8},{16,20},{20,16},{24,28},{28,24},{1,5},{5... | collective-permute-start | bytes 12582920 | tf_op jit(solution)/shard_map/ppermute | solution.py:120
  174.9 67.3 %all-gather.55.cloned.1.call-start = ((), (), s32[]{:S(2)}) async-start(), calls=%async_computation.12 | async-start | bytes 1310720 | tf_op jit(solution)/shard_map/all_gather | solution.py:392
  179.7 28.3 %collective-permute-start.15 = (bf16[9,128,512]{2,1,0:T(8,128)(2,1)}, bf16[9,128,512]{2,1,0:T(8,128)(2,1)S(1)}, u32[]{:S(2)}, u32[]{:S(2)}) collective-permute-start(bf16[9,128,512]{2,1,0:T(8,128)(2,1)} %get-tuple-element.638.refs_2_), channel_id=1, source_target_pairs={{0,8},{4,12},{8,0},{12,4},{16,24},{20,28},{24,16},{28,20},{1,9},{5... | collective-permute-start | bytes 3538952 | tf_op jit(solution)/shard_map/ppermute | solution.py:120
  208.8 33.4 %collective-permute-start.20 = (bf16[2048,1024]{1,0:T(8,128)(2,1)}, bf16[2048,1024]{1,0:T(8,128)(2,1)}, u32[]{:S(2)}, u32[]{:S(2)}) collective-permute-start(bf16[2048,1024]{1,0:T(8,128)(2,1)} %place.10.own_ref), channel_id=1, source_target_pairs={{0,4},{4,0},{8,12},{12,8},{16,20},{20,16},{24,28},{28,24},{1,5},{5... | collective-permute-start | bytes 12582920 | tf_op jit(solution)/shard_map/ppermute | solution.py:120
  208.9 77.1 %all-gather.57.cloned.1.call-start = ((), (), s32[]{:S(2)}) async-start(), calls=%async_computation.13 | async-start | bytes 1310720 | tf_op jit(solution)/shard_map/all_gather | solution.py:392
  242.2 43.9 %collective-permute-start.25 = (bf16[2048,1024]{1,0:T(8,128)(2,1)}, bf16[2048,1024]{1,0:T(8,128)(2,1)}, u32[]{:S(2)}, u32[]{:S(2)}) collective-permute-start(bf16[2048,1024]{1,0:T(8,128)(2,1)} %place.11.own_ref), channel_id=1, source_target_pairs={{0,4},{4,0},{8,12},{12,8},{16,20},{20,16},{24,28},{28,24},{1,5},{5... | collective-permute-start | bytes 12582920 | tf_op jit(solution)/shard_map/ppermute | solution.py:120
  244.5 85.8 %all-gather.59.cloned.1.call-start = ((), (), s32[]{:S(2)}) async-start(), calls=%async_computation.14 | async-start | bytes 1310720 | tf_op jit(solution)/shard_map/all_gather | solution.py:392
  251.5 34.5 %collective-permute-start.23 = (bf16[9,128,512]{2,1,0:T(8,128)(2,1)}, bf16[9,128,512]{2,1,0:T(8,128)(2,1)S(1)}, u32[]{:S(2)}, u32[]{:S(2)}) collective-permute-start(bf16[9,128,512]{2,1,0:T(8,128)(2,1)} %get-tuple-element.707.refs_2_), channel_id=1, source_target_pairs={{0,8},{4,12},{8,0},{12,4},{16,24},{20,28},{24,16},{28,20},{1,9},{5... | collective-permute-start | bytes 3538952 | tf_op jit(solution)/shard_map/ppermute | solution.py:120
  252.6 33.4 %collective-permute-start.24 = (bf16[9,128,512]{2,1,0:T(8,128)(2,1)}, bf16[9,128,512]{2,1,0:T(8,128)(2,1)S(1)}, u32[]{:S(2)}, u32[]{:S(2)}) collective-permute-start(bf16[9,128,512]{2,1,0:T(8,128)(2,1)} %get-tuple-element.708.refs_4_.refs_3_), channel_id=1, source_target_pairs={{0,16},{4,20},{8,24},{12,28},{16,0},{20,4},{24,8},{28,12},{1,17},{... | collective-permute-start | bytes 3538952 | tf_op jit(solution)/shard_map/ppermute | solution.py:120
  255.6 30.4 %collective-permute-start.26 = (bf16[256,512]{1,0:T(8,128)(2,1)}, bf16[256,512]{1,0:T(8,128)(2,1)}, u32[]{:S(2)}, u32[]{:S(2)}) collective-permute-start(bf16[256,512]{1,0:T(8,128)(2,1)} %maximum_select_fusion.20), channel_id=1, source_target_pairs={{0,8},{4,12},{8,0},{12,4},{16,24},{20,28},{24,16},{28,20},{1,9},{5... | collective-permute-start | bytes 786440 | tf_op jit(solution)/shard_map/ppermute | solution.py:120
  286.1 103.7 %all-gather.61.cloned.1.call-start = ((), (), s32[]{:S(2)}) async-start(), calls=%async_computation.15 | async-start | bytes 1310720 | tf_op jit(solution)/shard_map/all_gather | solution.py:392
  289.0 33.3 %collective-permute-start.29 = (bf16[512,512]{1,0:T(8,128)(2,1)}, bf16[512,512]{1,0:T(8,128)(2,1)}, u32[]{:S(2)}, u32[]{:S(2)}) collective-permute-start(bf16[512,512]{1,0:T(8,128)(2,1)} %maximum_select_fusion.17), channel_id=1, source_target_pairs={{0,16},{4,20},{8,24},{12,28},{16,0},{20,4},{24,8},{28,12},{1,17},{... | collective-permute-start | bytes 1572872 | tf_op jit(solution)/shard_map/ppermute | solution.py:120
  330.3 59.5 %collective-permute-start.32 = (bf16[4096,1024]{1,0:T(8,128)(2,1)}, bf16[4096,1024]{1,0:T(8,128)(2,1)}, u32[]{:S(2)}, u32[]{:S(2)}) collective-permute-start(bf16[4096,1024]{1,0:T(8,128)(2,1)} %place.12.own_ref), channel_id=1, source_target_pairs={{0,4},{4,0},{8,12},{12,8},{16,20},{20,16},{24,28},{28,24},{1,5},{5... | collective-permute-start | bytes 25165832 | tf_op jit(solution)/shard_map/ppermute | solution.py:120
  334.1 100.4 %all-gather.63.cloned.1.call-start = ((), (), s32[]{:S(2)}) async-start(), calls=%async_computation.16 | async-start | bytes 1310720 | tf_op jit(solution)/shard_map/all_gather | solution.py:392
  338.6 51.2 %collective-permute-start.30 = (bf16[9,128,512]{2,1,0:T(8,128)(2,1)}, bf16[9,128,512]{2,1,0:T(8,128)(2,1)}, u32[]{:S(2)}, u32[]{:S(2)}) collective-permute-start(bf16[9,128,512]{2,1,0:T(8,128)(2,1)} %get-tuple-element.758.refs_2_), channel_id=1, source_target_pairs={{0,8},{4,12},{8,0},{12,4},{16,24},{20,28},{24,16},{28,20},{1,9},{5... | collective-permute-start | bytes 3538952 | tf_op jit(solution)/shard_map/ppermute | solution.py:120
  339.7 50.0 %collective-permute-start.31 = (bf16[9,128,512]{2,1,0:T(8,128)(2,1)}, bf16[9,128,512]{2,1,0:T(8,128)(2,1)}, u32[]{:S(2)}, u32[]{:S(2)}) collective-permute-start(bf16[9,128,512]{2,1,0:T(8,128)(2,1)} %get-tuple-element.759.refs_4_.refs_3_), channel_id=1, source_target_pairs={{0,16},{4,20},{8,24},{12,28},{16,0},{20,4},{24,8},{28,12},{1,17},{... | collective-permute-start | bytes 3538952 | tf_op jit(solution)/shard_map/ppermute | solution.py:120
  350.0 38.2 %collective-permute-start.35 = (bf16[24,64,256]{2,1,0:T(8,128)(2,1)S(1)}, bf16[24,64,256]{2,1,0:T(8,128)(2,1)S(1)}, u32[]{:S(2)}, u32[]{:S(2)}) collective-permute-start(bf16[24,64,256]{2,1,0:T(8,128)(2,1)S(1)} %fusion.110), channel_id=1, source_target_pairs={{0,8},{4,12},{8,0},{12,4},{16,24},{20,28},{24,16},{28,20},{1,9},{5... | collective-permute-start | bytes 2359304 | tf_op jit(solution)/shard_map/ppermute | solution.py:120
  352.3 31.7 %collective-permute-start.36 = (f32[24]{0:T(128)S(1)}, f32[24]{0:T(128)S(1)}, u32[]{:S(2)}, u32[]{:S(2)}) collective-permute-start(f32[24]{0:T(128)S(1)} %broadcast_select_fusion.28), channel_id=1, source_target_pairs={{0,8},{4,12},{8,0},{12,4},{16,24},{20,28},{24,16},{28,20},{1,9},{5... | collective-permute-start | bytes 296 | tf_op jit(solution)/shard_map/ppermute | solution.py:120
  389.8 78.2 %all-gather.65.cloned.1.call-start = ((), (), s32[]{:S(2)}) async-start(), calls=%async_computation.17 | async-start | bytes 1310720 | tf_op jit(solution)/shard_map/all_gather | solution.py:392
  396.9 32.9 %collective-permute-start.37 = (bf16[9,128,512]{2,1,0:T(8,128)(2,1)}, bf16[9,128,512]{2,1,0:T(8,128)(2,1)}, u32[]{:S(2)}, u32[]{:S(2)}) collective-permute-start(bf16[9,128,512]{2,1,0:T(8,128)(2,1)} %get-tuple-element.776.refs_2_.refs_8_), channel_id=1, source_target_pairs={{0,8},{4,12},{8,0},{12,4},{16,24},{20,28},{24,16},{28,20},{1,9},{5... | collective-permute-start | bytes 3538952 | tf_op jit(solution)/shard_map/ppermute | solution.py:120
  397.9 36.5 %collective-permute-start.38 = (bf16[9,128,512]{2,1,0:T(8,128)(2,1)}, bf16[9,128,512]{2,1,0:T(8,128)(2,1)}, u32[]{:S(2)}, u32[]{:S(2)}) collective-permute-start(bf16[9,128,512]{2,1,0:T(8,128)(2,1)} %get-tuple-element.777.refs_4_.refs_9_), channel_id=1, source_target_pairs={{0,16},{4,20},{8,24},{12,28},{16,0},{20,4},{24,8},{28,12},{1,17},{... | collective-permute-start | bytes 3538952 | tf_op jit(solution)/shard_map/ppermute | solution.py:120
  434.4 33.5 %collective-permute-start.43 = (bf16[2048,2048]{1,0:T(8,128)(2,1)}, bf16[2048,2048]{1,0:T(8,128)(2,1)}, u32[]{:S(2)}, u32[]{:S(2)}) collective-permute-start(bf16[2048,2048]{1,0:T(8,128)(2,1)} %place.13.own_ref), channel_id=1, source_target_pairs={{0,4},{4,0},{8,12},{12,8},{16,20},{20,16},{24,28},{28,24},{1,5},{5... | collective-permute-start | bytes 25165832 | tf_op jit(solution)/shard_map/ppermute | solution.py:120
  434.5 78.1 %all-gather.31.cloned.1.call-start = ((), (), s32[]{:S(2)}) async-start(), calls=%async_computation | async-start | bytes 2621440 | tf_op jit(solution)/shard_map/all_gather | solution.py:506
  438.4 28.8 %collective-permute-start.41 = (bf16[9,128,512]{2,1,0:T(8,128)(2,1)}, bf16[9,128,512]{2,1,0:T(8,128)(2,1)}, u32[]{:S(2)}, u32[]{:S(2)}) collective-permute-start(bf16[9,128,512]{2,1,0:T(8,128)(2,1)} %get-tuple-element.794.refs_2_), channel_id=1, source_target_pairs={{0,8},{4,12},{8,0},{12,4},{16,24},{20,28},{24,16},{28,20},{1,9},{5... | collective-permute-start | bytes 3538952 | tf_op jit(solution)/shard_map/ppermute | solution.py:120
  439.5 28.4 %collective-permute-start.42 = (bf16[9,128,512]{2,1,0:T(8,128)(2,1)}, bf16[9,128,512]{2,1,0:T(8,128)(2,1)}, u32[]{:S(2)}, u32[]{:S(2)}) collective-permute-start(bf16[9,128,512]{2,1,0:T(8,128)(2,1)} %get-tuple-element.795.refs_4_.refs_3_), channel_id=1, source_target_pairs={{0,16},{4,20},{8,24},{12,28},{16,0},{20,4},{24,8},{28,12},{1,17},{... | collective-permute-start | bytes 3538952 | tf_op jit(solution)/shard_map/ppermute | solution.py:120
  468.0 230.9 %all-gather.33.cloned.1.call-start = ((), (), s32[]{:S(2)}) async-start(), calls=%async_computation.1 | async-start | bytes 5242880 | tf_op jit(solution)/shard_map/all_gather | solution.py:506
  481.1 31.4 %collective-permute-start.44 = (bf16[9,128,512]{2,1,0:T(8,128)(2,1)}, bf16[9,128,512]{2,1,0:T(8,128)(2,1)}, u32[]{:S(2)}, u32[]{:S(2)}) collective-permute-start(bf16[9,128,512]{2,1,0:T(8,128)(2,1)} %get-tuple-element.805.refs_1_.refs_8_), channel_id=1, source_target_pairs={{0,8},{4,12},{8,0},{12,4},{16,24},{20,28},{24,16},{28,20},{1,9},{5... | collective-permute-start | bytes 3538952 | tf_op jit(solution)/shard_map/ppermute | solution.py:120
  482.3 30.3 %collective-permute-start.45 = (bf16[9,128,512]{2,1,0:T(8,128)(2,1)}, bf16[9,128,512]{2,1,0:T(8,128)(2,1)}, u32[]{:S(2)}, u32[]{:S(2)}) collective-permute-start(bf16[9,128,512]{2,1,0:T(8,128)(2,1)} %get-tuple-element.806.refs_3_.refs_9_), channel_id=1, source_target_pairs={{0,16},{4,20},{8,24},{12,28},{16,0},{20,4},{24,8},{28,12},{1,17},{... | collective-permute-start | bytes 3538952 | tf_op jit(solution)/shard_map/ppermute | solution.py:120
  522.9 35.3 %collective-permute-start.50 = (bf16[128,1536]{1,0:T(8,128)(2,1)S(1)}, bf16[128,1536]{1,0:T(8,128)(2,1)}, u32[]{:S(2)}, u32[]{:S(2)}) collective-permute-start(bf16[128,1536]{1,0:T(8,128)(2,1)S(1)} %pad_maximum_fusion.21), channel_id=1, source_target_pairs={{0,2},{1,3},{2,0},{3,1},{4,6},{5,7},{6,4},{7,5},{8,10},{9,11},{10,... | collective-permute-start | bytes 1179656 | tf_op jit(solution)/shard_map/ppermute | solution.py:125
  567.3 39.2 %collective-permute-start.54 = (bf16[128,1536]{1,0:T(8,128)(2,1)S(1)}, bf16[128,1536]{1,0:T(8,128)(2,1)S(1)}, u32[]{:S(2)}, u32[]{:S(2)}) collective-permute-start(bf16[128,1536]{1,0:T(8,128)(2,1)S(1)} %pad_maximum_fusion.25), channel_id=1, source_target_pairs={{0,2},{1,3},{2,0},{3,1},{4,6},{5,7},{6,4},{7,5},{8,10},{9,11},{10,... | collective-permute-start | bytes 1179656 | tf_op jit(solution)/shard_map/ppermute | solution.py:125
  569.6 48.8 %collective-permute-start.55 = (bf16[128,1536]{1,0:T(8,128)(2,1)}, bf16[128,1536]{1,0:T(8,128)(2,1)}, u32[]{:S(2)}, u32[]{:S(2)}) collective-permute-start(bf16[128,1536]{1,0:T(8,128)(2,1)} %pad_maximum_fusion.26), channel_id=1, source_target_pairs={{0,1},{1,2},{2,3},{3,0},{4,5},{5,6},{6,7},{7,4},{8,9},{9,10},{10,1... | collective-permute-start | bytes 1179656 | tf_op jit(solution)/shard_map/ppermute | solution.py:125
  618.4 164.2 %all-gather.35.cloned.1.call-start = ((), (), s32[]{:S(2)}) async-start(), calls=%async_computation.2 | async-start | bytes 5242880 | tf_op jit(solution)/shard_map/all_gather | solution.py:506
  671.4 254.7 %all-gather.37.cloned.1.call-start = ((), (), s32[]{:S(2)}) async-start(), calls=%async_computation.3 | async-start | bytes 2621440 | tf_op jit(solution)/shard_map/all_gather | solution.py:506
  741.0 250.0 %all-gather.39.cloned.1.call-start = ((), (), s32[]{:S(2)}) async-start(), calls=%async_computation.4 | async-start | bytes 3932160 | tf_op jit(solution)/shard_map/all_gather | solution.py:506
  793.7 46.8 %collective-permute-start.68 = (bf16[512,4096]{1,0:T(8,128)(2,1)}, bf16[512,4096]{1,0:T(8,128)(2,1)}, u32[]{:S(2)}, u32[]{:S(2)}) collective-permute-start(bf16[512,4096]{1,0:T(8,128)(2,1)} %get-tuple-element.1163), channel_id=1, source_target_pairs={{0,4},{4,0},{8,12},{12,8},{16,20},{20,16},{24,28},{28,24},{1,5},{5... | collective-permute-start | bytes 12582920 | tf_op jit(solution)/shard_map/ppermute | solution.py:120
  815.6 307.5 %all-gather.41.cloned.1.call-start = ((), (), s32[]{:S(2)}) async-start(), calls=%async_computation.5 | async-start | bytes 6881280 | tf_op jit(solution)/shard_map/all_gather | solution.py:506
  849.7 32.6 %collective-permute-start.73 = (bf16[512,512]{1,0:T(8,128)(2,1)S(1)}, bf16[512,512]{1,0:T(8,128)(2,1)S(1)}, u32[]{:S(2)}, u32[]{:S(2)}) collective-permute-start(bf16[512,512]{1,0:T(8,128)(2,1)S(1)} %get-tuple-element.1107), channel_id=1, source_target_pairs={{0,16},{4,20},{8,24},{12,28},{16,0},{20,4},{24,8},{28,12},{1,17},{... | collective-permute-start | bytes 1572872 | tf_op jit(solution)/shard_map/ppermute | solution.py:120
  934.0 36.1 %collective-permute-start.82 = (bf16[128,512]{1,0:T(8,128)(2,1)S(1)}, bf16[128,512]{1,0:T(8,128)(2,1)S(1)}, u32[]{:S(2)}, u32[]{:S(2)}) collective-permute-start(bf16[128,512]{1,0:T(8,128)(2,1)S(1)} %get-tuple-element.1135), channel_id=1, source_target_pairs={{0,4},{4,0},{8,12},{12,8},{16,20},{20,16},{24,28},{28,24},{1,5},{5... | collective-permute-start | bytes 393224 | tf_op jit(solution)/shard_map/ppermute | solution.py:120
  1007.4 38.7 %collective-permute-start.86 = (bf16[128,3584]{1,0:T(8,128)(2,1)}, bf16[128,3584]{1,0:T(8,128)(2,1)}, u32[]{:S(2)}, u32[]{:S(2)}) collective-permute-start(bf16[128,3584]{1,0:T(8,128)(2,1)} %get-tuple-element.1081), channel_id=1, source_target_pairs={{0,16},{4,20},{8,24},{12,28},{16,0},{20,4},{24,8},{28,12},{1,17},{... | collective-permute-start | bytes 2752520 | tf_op jit(solution)/shard_map/ppermute | solution.py:120
  1008.8 37.4 %collective-permute-start.85 = (bf16[128,3584]{1,0:T(8,128)(2,1)}, bf16[128,3584]{1,0:T(8,128)(2,1)}, u32[]{:S(2)}, u32[]{:S(2)}) collective-permute-start(bf16[128,3584]{1,0:T(8,128)(2,1)} %get-tuple-element.1082), channel_id=1, source_target_pairs={{0,8},{4,12},{8,0},{12,4},{16,24},{20,28},{24,16},{28,20},{1,9},{5... | collective-permute-start | bytes 2752520 | tf_op jit(solution)/shard_map/ppermute | solution.py:120
  (325 other events, 3223.5 us)
Sparse Core Ops, SparseCore 0:
  13.4 28.1 all-gather.42
  44.4 28.1 all-gather.44
  74.1 27.6 all-gather.46
  104.9 27.1 all-gather.48
  138.2 27.1 all-gather.50
  175.0 27.0 all-gather.52
  209.0 27.1 all-gather.54
  244.6 27.0 all-gather.56
  286.2 26.9 all-gather.58
  334.2 26.1 all-gather.60
  389.9 26.1 all-gather.62
  434.6 26.2 all-gather.64
  468.1 44.0 all-gather.30
  618.5 78.4 all-gather.32
  698.4 79.2 all-gather.34
  779.2 44.4 all-gather.36
  825.1 62.2 all-gather.38
  1018.3 99.4 all-gather.40

commit v5 on v4

--- a/solution.py
+++ b/solution.py
@@ -598,10 +598,12 @@
     )(idx, *flat)
 
 
-def finish_steps(tasks, finish):
-    while any(task.result is None for task in tasks):
+def finish_steps(task, wait, finish, after):
+    while task.result is None or after.result is None:
         yield ()
-    yield Last(finish(*[task.result for task in tasks]))
+    for _ in range(wait):
+        yield ()
+    yield Last(finish(task.result))
 
 
 def rows_kernel(cases, idx_ref, low_ref, high_ref, out_ref):
@@ -950,12 +952,11 @@
     shard_rows = mid_low.shape[1] // layers
 
     down_grad = weight_grad(
-        [(late_deal, 0, cotangent_all)],
-        lambda pair: finished(idx, [pair], [(0, 0, D)]),
+        [(late_deal, 0, cotangent_all)], lambda pair: pair
     )
     gate_up_grad = weight_grad(
         [(late_deal, 1, gate_all), (late_deal, 1, up_all)],
-        lambda pair: finished(idx, [pair], [(0, 0, 2 * FF)]),
+        lambda pair: pair,
         down_grad,
     )
     d_mid_norm = back(idx, gate_low, gate_w.ready)
@@ -979,11 +980,7 @@
     ]
     oo_z_grad = weight_grad(
         [(early_deal, 0, branch_all), (early_deal, 1, z_all)],
-        lambda pair: (
-            pair,
-            finished_rows(idx, pair, cases[: DS // layers // fine], fine),
-            finished_rows(idx, pair, cases[DS // layers // fine :], fine),
-        ),
+        lambda pair: pair,
         gate_up_grad,
     )
     d_c_carry, d_log_carry, d_state_in = carry_pull(d_core)
@@ -1061,6 +1058,29 @@
     tail_grad = weight_grad(
         [(early_deal, 1, every(tail_low, 4))], lambda pair: pair
     )
+    main_done = Task(None)
+    main_done.result = ()
+    down_out = rounds.start(
+        finish_steps(
+            down_grad, 1, lambda pair: finished(idx, [pair], [(0, 0, D)]), main_done
+        )
+    )
+    gate_up_out_grad = rounds.start(
+        finish_steps(
+            gate_up_grad, 2, lambda pair: finished(idx, [pair], [(0, 0, 2 * FF)]), main_done
+        )
+    )
+    oo_out = rounds.start(
+        finish_steps(
+            oo_z_grad,
+            0,
+            lambda pair: (
+                finished_rows(idx, pair, cases[: DS // layers // fine], fine),
+                finished_rows(idx, pair, cases[DS // layers // fine :], fine),
+            ),
+            main_done,
+        )
+    )
     d_normed_in = (
         back(idx, conv_grad_low[:, :part], x_w.ready)
         + back(
@@ -1093,9 +1113,10 @@
             )
         )
     )
-    rounds.until(smalls_task, gate_up_grad, down_grad, oo_z_grad, tail_grad)
+    rounds.until(smalls_task, gate_up_out_grad, down_out, oo_out, tail_grad)
     smalls = smalls_task.result
-    tail_pair, (oo_z_pair, out_grad, o_grad) = tail_grad.result, oo_z_grad.result
+    tail_pair, oo_z_pair = tail_grad.result, oo_z_grad.result
+    out_grad, o_grad = oo_out.result
     z_first = branches_low.shape[1] // layers // shard_rows * D
     tail_half = tail_pair[0].shape[1]
     step_grad = jnp.where(core == 1, tail_pair[0], tail_pair[1])
@@ -1115,8 +1136,8 @@
         o_grad,
         smalls[6],
         smalls[7],
-        gate_up_grad.result,
-        down_grad.result,
+        gate_up_out_grad.result,
+        down_out.result,
     )
 
 

time: 1220 us -> 1220 us (level)
    unnamed x507 -> x503, local copies, waits for them, and re-layouts: 42.8 us -> 41.7 us
  transfers between devices with their start and end apart: 127 -> 127, of which waited for: 60 -> 59; matrix products, arithmetic and copies ran while one was open for 30% -> 30% of each run, Pallas kernels for 23% -> 23%
where the time goes in v5:
time: 1220 us; the launch traced here: 1200 us
  waiting for transfers between devices  395 us (32%)
  Pallas kernels  287 us (24%)
  other arithmetic  181 us (15%)
  local copies, waits for them, and re-layouts  123 us (10%)
  starting transfers between devices  101 us (8%)
  matrix products  97.4 us (8%)
  between operations  19.5 us (2%)
    ppermute x93, waiting for transfers between devices, swap(): return lax.ppermute(block, 'ctx', [(i, i ^ distance) for i in range(peers)])  342 us
    pallas_call x16, Pallas kernels, product(): pl.pallas_call(kernel, grid_spec=pltpu.PrefetchScalarGridSpec(num_scalar_...  144 us
    ppermute x93, starting transfers between devices, swap(): return lax.ppermute(block, 'ctx', [(i, i ^ distance) for i in range(peers)])  79.5 us
    pallas_call x8, Pallas kernels, placed(): pl.pallas_call(lambda *refs: place_kernel(chunks, *refs), out_shape=jax.S...  51.8 us
    pallas_call x13, Pallas kernels, packed(): pl.pallas_call(lambda *refs: pack_kernel(fresh, plan, len(arrays), *refs)...  49.5 us
    unnamed x503, local copies, waits for them, and re-layouts  41.7 us
    pallas_call x4, Pallas kernels, finished(): pl.pallas_call(lambda *refs: finish_kernel(segments, *refs), grid=(rows /...  28.9 us
    dot_general x7, matrix products, weight_steps(): lax.dot_general(array[:, first:first + rows], grad.result, (((0,), (0,)),...  28.9 us
  transfers between devices with their start and end apart: 127, of which 59 were waited for; matrix products, arithmetic and copies ran while one was open for 30% of the time, Pallas kernels for 23%

profile of v5, /device:TPU:0, one launch (start us, length us, event | category | flops | bytes accessed | tf_op | source)
XLA Modules:
  0.0 1204.4 jit_solution(10850286789797165334)
XLA Ops:
  59.3 13.3 %all-gather.45.cloned.1.call-done = bf16[512,1024]{1,0:T(8,128)(2,1)} async-done(((bf16[128,1024]{1,0:T(8,128)(2,1)}), bf16[512,1024]{1,0:T(8,128)(2,1)}) %all-gather.45.cloned.1.call-update) | async-done | bytes 1048592 | tf_op jit(solution)/shard_map/all_gather | solution.py:392
  84.7 20.1 %collective-permute-done.7.refs_3_.refs_7_.refs_4_ = bf16[9,128,512]{2,1,0:T(8,128)(2,1)S(1)} collective-permute-done((bf16[9,128,512]{2,1,0:T(8,128)(2,1)}, bf16[9,128,512]{2,1,0:T(8,128)(2,1)S(1)}, u32[]{:S(2)}, u32[]{:S(2)}) %collective-permute-start.7) | collective-permute-done | bytes 1179680 | tf_op jit(solution)/shard_map/ppermute | solution.py:120
  125.9 11.6 collective-permute-done.10.refs_3_.refs_7_.refs_4_
  150.7 20.2 %collective-permute-done.13.refs_3_.refs_7_.refs_4_ = bf16[9,128,512]{2,1,0:T(8,128)(2,1)S(1)} collective-permute-done((bf16[9,128,512]{2,1,0:T(8,128)(2,1)}, bf16[9,128,512]{2,1,0:T(8,128)(2,1)S(1)}, u32[]{:S(2)}, u32[]{:S(2)}) %collective-permute-start.13) | collective-permute-done | bytes 1179680 | tf_op jit(solution)/shard_map/ppermute | solution.py:120
  187.9 7.1 forth.8
  199.9 8.4 collective-permute-done.15.refs_3_.refs_7_.refs_4_
  221.5 7.3 forth.9
  228.8 13.0 %collective-permute-done.18.refs_3_.refs_7_ = bf16[9,128,512]{2,1,0:T(8,128)(2,1)S(1)} collective-permute-done((bf16[9,128,512]{2,1,0:T(8,128)(2,1)}, bf16[9,128,512]{2,1,0:T(8,128)(2,1)S(1)}, u32[]{:S(2)}, u32[]{:S(2)}) %collective-permute-start.18) | collective-permute-done | bytes 1179680 | tf_op jit(solution)/shard_map/ppermute | solution.py:120
  256.8 7.1 forth.10
  268.3 18.0 %collective-permute-done.26 = bf16[256,512]{1,0:T(8,128)(2,1)} collective-permute-done((bf16[256,512]{1,0:T(8,128)(2,1)}, bf16[256,512]{1,0:T(8,128)(2,1)}, u32[]{:S(2)}, u32[]{:S(2)}) %collective-permute-start.26) | collective-permute-done | bytes 262176 | tf_op jit(solution)/shard_map/ppermute | solution.py:120
  290.4 8.1 place.12.own_ref
  310.8 7.5 fusion.54
  322.6 7.3 collective-permute-done.27.refs_3_.refs_7_
  355.4 29.0 %collective-permute-done.36 = f32[24]{0:T(128)S(1)} collective-permute-done((f32[24]{0:T(128)S(1)}, f32[24]{0:T(128)S(1)}, u32[]{:S(2)}, u32[]{:S(2)}) %collective-permute-start.36) | collective-permute-done | bytes 128 | tf_op jit(solution)/shard_map/ppermute | solution.py:120
  400.6 10.4 collective-permute-done.39
  414.6 7.8 place.13.own_ref
  441.1 7.2 forth.11
  452.0 15.5 %collective-permute-done.41.refs_3_.refs_11_.refs_4_ = bf16[9,128,512]{2,1,0:T(8,128)(2,1)} collective-permute-done((bf16[9,128,512]{2,1,0:T(8,128)(2,1)}, bf16[9,128,512]{2,1,0:T(8,128)(2,1)}, u32[]{:S(2)}, u32[]{:S(2)}) %collective-permute-start.41) | collective-permute-done | bytes 1179680 | tf_op jit(solution)/shard_map/ppermute | solution.py:120
  485.9 7.9 place.14.own_ref
  499.4 9.9 forth.12
  522.9 10.2 forth.13
  537.2 10.2 forth.14
  550.5 7.7 place.15.own_ref
  576.3 10.9 back.8
  593.2 13.4 %collective-permute-done.54 = bf16[128,1536]{1,0:T(8,128)(2,1)S(1)} collective-permute-done((bf16[128,1536]{1,0:T(8,128)(2,1)S(1)}, bf16[128,1536]{1,0:T(8,128)(2,1)S(1)}, u32[]{:S(2)}, u32[]{:S(2)}) %collective-permute-start.54) | collective-permute-done | bytes 393248 | tf_op jit(solution)/shard_map/ppermute | solution.py:125
  607.3 11.1 back.9
  619.9 11.5 back.10
  652.9 11.0 back.11
  701.3 9.5 collective-permute-done.63
  714.6 10.1 forth.15
  793.3 9.2 fusion.26
  809.5 6.8 fusion.39
  842.7 19.4 %collective-permute-done.70 = bf16[128,4096]{1,0:T(8,128)(2,1)S(1)} collective-permute-done((bf16[128,4096]{1,0:T(8,128)(2,1)S(1)}, bf16[128,4096]{1,0:T(8,128)(2,1)S(1)}, u32[]{:S(2)}, u32[]{:S(2)}) %collective-permute-start.70) | collective-permute-done | bytes 1048608 | tf_op jit(solution)/shard_map/ppermute | solution.py:120
  863.3 8.0 collective-permute-done.73
  902.8 7.1 collective-permute-done.77
  924.3 10.9 collective-permute-done.79
  990.1 7.4 back.14
  1004.4 7.6 back.15
  1012.8 7.4 back.12
  1021.1 8.0 back.13
  1036.3 9.8 collective-permute-done.89
  1047.7 10.1 collective-permute-done.90
  1060.3 18.4 %collective-permute-done.91 = bf16[128,3584]{1,0:T(8,128)(2,1)S(1)} collective-permute-done((bf16[128,3584]{1,0:T(8,128)(2,1)S(1)}, bf16[128,3584]{1,0:T(8,128)(2,1)S(1)}, u32[]{:S(2)}, u32[]{:S(2)}) %collective-permute-start.91) | collective-permute-done | bytes 917536 | tf_op jit(solution)/shard_map/ppermute | solution.py:120
  1083.6 9.4 finish.5
  1102.5 8.4 finish_rows.2
  1130.6 10.4 collective-permute-done.99
  1163.5 11.8 collective-permute-done.106
  1186.9 9.6 finish.6
  (1076 shorter events, 662.7 us)
Async XLA Ops:
  7.2 37.2 %all-gather.43.cloned.1.call-start = ((), (), s32[]{:S(2)}) async-start(), calls=%async_computation.6 | async-start | bytes 1310720 | tf_op jit(solution)/shard_map/all_gather | solution.py:392
  7.8 36.6 %collective-permute-start.3 = (bf16[512,48]{0,1:T(8,128)(2,1)}, bf16[512,48]{0,1:T(8,128)(2,1)S(1)}, u32[]{:S(2)}, u32[]{:S(2)}) collective-permute-start(bf16[512,48]{0,1:T(8,128)(2,1)} %param.22), channel_id=1, source_target_pairs={{0,1},{1,2},{2,3},{3,0},{4,5},{5,6},{6,7},{7,4},{8,9},{9,10},{10,1... | collective-permute-start | bytes 147464 | tf_op jit(solution)/shard_map/ppermute | solution.py:125
  13.3 59.4 %all-gather.45.cloned.1.call-start = ((), (), s32[]{:S(2)}) async-start(), calls=%async_computation.7 | async-start | bytes 1310720 | tf_op jit(solution)/shard_map/all_gather | solution.py:392
  44.4 60.5 %all-gather.47.cloned.1.call-start = ((), (), s32[]{:S(2)}) async-start(), calls=%async_computation.8 | async-start | bytes 1310720 | tf_op jit(solution)/shard_map/all_gather | solution.py:392
  72.7 65.6 %all-gather.49.cloned.1.call-start = ((), (), s32[]{:S(2)}) async-start(), calls=%async_computation.9 | async-start | bytes 1310720 | tf_op jit(solution)/shard_map/all_gather | solution.py:392
  104.9 66.7 %all-gather.51.cloned.1.call-start = ((), (), s32[]{:S(2)}) async-start(), calls=%async_computation.10 | async-start | bytes 1310720 | tf_op jit(solution)/shard_map/all_gather | solution.py:392
  138.3 33.3 %collective-permute-start.12 = (bf16[2048,1024]{1,0:T(8,128)(2,1)}, bf16[2048,1024]{1,0:T(8,128)(2,1)}, u32[]{:S(2)}, u32[]{:S(2)}) collective-permute-start(bf16[2048,1024]{1,0:T(8,128)(2,1)} %place.8.own_ref), channel_id=1, source_target_pairs={{0,4},{4,0},{8,12},{12,8},{16,20},{20,16},{24,28},{28,24},{1,5},{5... | collective-permute-start | bytes 12582920 | tf_op jit(solution)/shard_map/ppermute | solution.py:120
  138.3 70.8 %all-gather.53.cloned.1.call-start = ((), (), s32[]{:S(2)}) async-start(), calls=%async_computation.11 | async-start | bytes 1310720 | tf_op jit(solution)/shard_map/all_gather | solution.py:392
  171.6 37.5 %collective-permute-start.17 = (bf16[2048,1024]{1,0:T(8,128)(2,1)}, bf16[2048,1024]{1,0:T(8,128)(2,1)}, u32[]{:S(2)}, u32[]{:S(2)}) collective-permute-start(bf16[2048,1024]{1,0:T(8,128)(2,1)} %place.9.own_ref), channel_id=1, source_target_pairs={{0,4},{4,0},{8,12},{12,8},{16,20},{20,16},{24,28},{28,24},{1,5},{5... | collective-permute-start | bytes 12582920 | tf_op jit(solution)/shard_map/ppermute | solution.py:120
  175.2 67.3 %all-gather.55.cloned.1.call-start = ((), (), s32[]{:S(2)}) async-start(), calls=%async_computation.12 | async-start | bytes 1310720 | tf_op jit(solution)/shard_map/all_gather | solution.py:392
  180.0 28.3 %collective-permute-start.15 = (bf16[9,128,512]{2,1,0:T(8,128)(2,1)}, bf16[9,128,512]{2,1,0:T(8,128)(2,1)S(1)}, u32[]{:S(2)}, u32[]{:S(2)}) collective-permute-start(bf16[9,128,512]{2,1,0:T(8,128)(2,1)} %get-tuple-element.642.refs_2_), channel_id=1, source_target_pairs={{0,8},{4,12},{8,0},{12,4},{16,24},{20,28},{24,16},{28,20},{1,9},{5... | collective-permute-start | bytes 3538952 | tf_op jit(solution)/shard_map/ppermute | solution.py:120
  209.1 33.4 %collective-permute-start.20 = (bf16[2048,1024]{1,0:T(8,128)(2,1)}, bf16[2048,1024]{1,0:T(8,128)(2,1)}, u32[]{:S(2)}, u32[]{:S(2)}) collective-permute-start(bf16[2048,1024]{1,0:T(8,128)(2,1)} %place.10.own_ref), channel_id=1, source_target_pairs={{0,4},{4,0},{8,12},{12,8},{16,20},{20,16},{24,28},{28,24},{1,5},{5... | collective-permute-start | bytes 12582920 | tf_op jit(solution)/shard_map/ppermute | solution.py:120
  209.2 77.1 %all-gather.57.cloned.1.call-start = ((), (), s32[]{:S(2)}) async-start(), calls=%async_computation.13 | async-start | bytes 1310720 | tf_op jit(solution)/shard_map/all_gather | solution.py:392
  242.5 43.9 %collective-permute-start.25 = (bf16[2048,1024]{1,0:T(8,128)(2,1)}, bf16[2048,1024]{1,0:T(8,128)(2,1)}, u32[]{:S(2)}, u32[]{:S(2)}) collective-permute-start(bf16[2048,1024]{1,0:T(8,128)(2,1)} %place.11.own_ref), channel_id=1, source_target_pairs={{0,4},{4,0},{8,12},{12,8},{16,20},{20,16},{24,28},{28,24},{1,5},{5... | collective-permute-start | bytes 12582920 | tf_op jit(solution)/shard_map/ppermute | solution.py:120
  244.8 85.8 %all-gather.59.cloned.1.call-start = ((), (), s32[]{:S(2)}) async-start(), calls=%async_computation.14 | async-start | bytes 1310720 | tf_op jit(solution)/shard_map/all_gather | solution.py:392
  251.8 34.5 %collective-permute-start.23 = (bf16[9,128,512]{2,1,0:T(8,128)(2,1)}, bf16[9,128,512]{2,1,0:T(8,128)(2,1)S(1)}, u32[]{:S(2)}, u32[]{:S(2)}) collective-permute-start(bf16[9,128,512]{2,1,0:T(8,128)(2,1)} %get-tuple-element.711.refs_2_), channel_id=1, source_target_pairs={{0,8},{4,12},{8,0},{12,4},{16,24},{20,28},{24,16},{28,20},{1,9},{5... | collective-permute-start | bytes 3538952 | tf_op jit(solution)/shard_map/ppermute | solution.py:120
  252.9 33.4 %collective-permute-start.24 = (bf16[9,128,512]{2,1,0:T(8,128)(2,1)}, bf16[9,128,512]{2,1,0:T(8,128)(2,1)S(1)}, u32[]{:S(2)}, u32[]{:S(2)}) collective-permute-start(bf16[9,128,512]{2,1,0:T(8,128)(2,1)} %get-tuple-element.712.refs_4_.refs_3_), channel_id=1, source_target_pairs={{0,16},{4,20},{8,24},{12,28},{16,0},{20,4},{24,8},{28,12},{1,17},{... | collective-permute-start | bytes 3538952 | tf_op jit(solution)/shard_map/ppermute | solution.py:120
  255.8 30.5 %collective-permute-start.26 = (bf16[256,512]{1,0:T(8,128)(2,1)}, bf16[256,512]{1,0:T(8,128)(2,1)}, u32[]{:S(2)}, u32[]{:S(2)}) collective-permute-start(bf16[256,512]{1,0:T(8,128)(2,1)} %maximum_select_fusion.20), channel_id=1, source_target_pairs={{0,8},{4,12},{8,0},{12,4},{16,24},{20,28},{24,16},{28,20},{1,9},{5... | collective-permute-start | bytes 786440 | tf_op jit(solution)/shard_map/ppermute | solution.py:120
  286.4 103.7 %all-gather.61.cloned.1.call-start = ((), (), s32[]{:S(2)}) async-start(), calls=%async_computation.15 | async-start | bytes 1310720 | tf_op jit(solution)/shard_map/all_gather | solution.py:392
  289.3 33.3 %collective-permute-start.29 = (bf16[512,512]{1,0:T(8,128)(2,1)}, bf16[512,512]{1,0:T(8,128)(2,1)}, u32[]{:S(2)}, u32[]{:S(2)}) collective-permute-start(bf16[512,512]{1,0:T(8,128)(2,1)} %maximum_select_fusion.17), channel_id=1, source_target_pairs={{0,16},{4,20},{8,24},{12,28},{16,0},{20,4},{24,8},{28,12},{1,17},{... | collective-permute-start | bytes 1572872 | tf_op jit(solution)/shard_map/ppermute | solution.py:120
  330.5 59.6 %collective-permute-start.32 = (bf16[4096,1024]{1,0:T(8,128)(2,1)}, bf16[4096,1024]{1,0:T(8,128)(2,1)}, u32[]{:S(2)}, u32[]{:S(2)}) collective-permute-start(bf16[4096,1024]{1,0:T(8,128)(2,1)} %place.12.own_ref), channel_id=1, source_target_pairs={{0,4},{4,0},{8,12},{12,8},{16,20},{20,16},{24,28},{28,24},{1,5},{5... | collective-permute-start | bytes 25165832 | tf_op jit(solution)/shard_map/ppermute | solution.py:120
  334.3 100.4 %all-gather.63.cloned.1.call-start = ((), (), s32[]{:S(2)}) async-start(), calls=%async_computation.16 | async-start | bytes 1310720 | tf_op jit(solution)/shard_map/all_gather | solution.py:392
  338.9 51.2 %collective-permute-start.30 = (bf16[9,128,512]{2,1,0:T(8,128)(2,1)}, bf16[9,128,512]{2,1,0:T(8,128)(2,1)}, u32[]{:S(2)}, u32[]{:S(2)}) collective-permute-start(bf16[9,128,512]{2,1,0:T(8,128)(2,1)} %get-tuple-element.762.refs_2_), channel_id=1, source_target_pairs={{0,8},{4,12},{8,0},{12,4},{16,24},{20,28},{24,16},{28,20},{1,9},{5... | collective-permute-start | bytes 3538952 | tf_op jit(solution)/shard_map/ppermute | solution.py:120
  340.0 50.0 %collective-permute-start.31 = (bf16[9,128,512]{2,1,0:T(8,128)(2,1)}, bf16[9,128,512]{2,1,0:T(8,128)(2,1)}, u32[]{:S(2)}, u32[]{:S(2)}) collective-permute-start(bf16[9,128,512]{2,1,0:T(8,128)(2,1)} %get-tuple-element.763.refs_4_.refs_3_), channel_id=1, source_target_pairs={{0,16},{4,20},{8,24},{12,28},{16,0},{20,4},{24,8},{28,12},{1,17},{... | collective-permute-start | bytes 3538952 | tf_op jit(solution)/shard_map/ppermute | solution.py:120
  350.2 38.3 %collective-permute-start.35 = (bf16[24,64,256]{2,1,0:T(8,128)(2,1)S(1)}, bf16[24,64,256]{2,1,0:T(8,128)(2,1)S(1)}, u32[]{:S(2)}, u32[]{:S(2)}) collective-permute-start(bf16[24,64,256]{2,1,0:T(8,128)(2,1)S(1)} %fusion.110), channel_id=1, source_target_pairs={{0,8},{4,12},{8,0},{12,4},{16,24},{20,28},{24,16},{28,20},{1,9},{5... | collective-permute-start | bytes 2359304 | tf_op jit(solution)/shard_map/ppermute | solution.py:120
  352.6 31.8 %collective-permute-start.36 = (f32[24]{0:T(128)S(1)}, f32[24]{0:T(128)S(1)}, u32[]{:S(2)}, u32[]{:S(2)}) collective-permute-start(f32[24]{0:T(128)S(1)} %broadcast_select_fusion.28), channel_id=1, source_target_pairs={{0,8},{4,12},{8,0},{12,4},{16,24},{20,28},{24,16},{28,20},{1,9},{5... | collective-permute-start | bytes 296 | tf_op jit(solution)/shard_map/ppermute | solution.py:120
  390.1 78.1 %all-gather.65.cloned.1.call-start = ((), (), s32[]{:S(2)}) async-start(), calls=%async_computation.17 | async-start | bytes 1310720 | tf_op jit(solution)/shard_map/all_gather | solution.py:392
  397.2 32.8 %collective-permute-start.37 = (bf16[9,128,512]{2,1,0:T(8,128)(2,1)}, bf16[9,128,512]{2,1,0:T(8,128)(2,1)}, u32[]{:S(2)}, u32[]{:S(2)}) collective-permute-start(bf16[9,128,512]{2,1,0:T(8,128)(2,1)} %get-tuple-element.780.refs_2_.refs_8_), channel_id=1, source_target_pairs={{0,8},{4,12},{8,0},{12,4},{16,24},{20,28},{24,16},{28,20},{1,9},{5... | collective-permute-start | bytes 3538952 | tf_op jit(solution)/shard_map/ppermute | solution.py:120
  398.3 36.4 %collective-permute-start.38 = (bf16[9,128,512]{2,1,0:T(8,128)(2,1)}, bf16[9,128,512]{2,1,0:T(8,128)(2,1)}, u32[]{:S(2)}, u32[]{:S(2)}) collective-permute-start(bf16[9,128,512]{2,1,0:T(8,128)(2,1)} %get-tuple-element.781.refs_4_.refs_9_), channel_id=1, source_target_pairs={{0,16},{4,20},{8,24},{12,28},{16,0},{20,4},{24,8},{28,12},{1,17},{... | collective-permute-start | bytes 3538952 | tf_op jit(solution)/shard_map/ppermute | solution.py:120
  434.8 33.5 %collective-permute-start.43 = (bf16[2048,2048]{1,0:T(8,128)(2,1)}, bf16[2048,2048]{1,0:T(8,128)(2,1)}, u32[]{:S(2)}, u32[]{:S(2)}) collective-permute-start(bf16[2048,2048]{1,0:T(8,128)(2,1)} %place.13.own_ref), channel_id=1, source_target_pairs={{0,4},{4,0},{8,12},{12,8},{16,20},{20,16},{24,28},{28,24},{1,5},{5... | collective-permute-start | bytes 25165832 | tf_op jit(solution)/shard_map/ppermute | solution.py:120
  434.8 77.9 %all-gather.31.cloned.1.call-start = ((), (), s32[]{:S(2)}) async-start(), calls=%async_computation | async-start | bytes 2621440 | tf_op jit(solution)/shard_map/all_gather | solution.py:506
  438.7 28.8 %collective-permute-start.41 = (bf16[9,128,512]{2,1,0:T(8,128)(2,1)}, bf16[9,128,512]{2,1,0:T(8,128)(2,1)}, u32[]{:S(2)}, u32[]{:S(2)}) collective-permute-start(bf16[9,128,512]{2,1,0:T(8,128)(2,1)} %get-tuple-element.798.refs_2_), channel_id=1, source_target_pairs={{0,8},{4,12},{8,0},{12,4},{16,24},{20,28},{24,16},{28,20},{1,9},{5... | collective-permute-start | bytes 3538952 | tf_op jit(solution)/shard_map/ppermute | solution.py:120
  439.8 28.4 %collective-permute-start.42 = (bf16[9,128,512]{2,1,0:T(8,128)(2,1)}, bf16[9,128,512]{2,1,0:T(8,128)(2,1)}, u32[]{:S(2)}, u32[]{:S(2)}) collective-permute-start(bf16[9,128,512]{2,1,0:T(8,128)(2,1)} %get-tuple-element.799.refs_4_.refs_3_), channel_id=1, source_target_pairs={{0,16},{4,20},{8,24},{12,28},{16,0},{20,4},{24,8},{28,12},{1,17},{... | collective-permute-start | bytes 3538952 | tf_op jit(solution)/shard_map/ppermute | solution.py:120
  468.3 230.5 %all-gather.33.cloned.1.call-start = ((), (), s32[]{:S(2)}) async-start(), calls=%async_computation.1 | async-start | bytes 5242880 | tf_op jit(solution)/shard_map/all_gather | solution.py:506
  481.4 31.3 %collective-permute-start.44 = (bf16[9,128,512]{2,1,0:T(8,128)(2,1)}, bf16[9,128,512]{2,1,0:T(8,128)(2,1)}, u32[]{:S(2)}, u32[]{:S(2)}) collective-permute-start(bf16[9,128,512]{2,1,0:T(8,128)(2,1)} %get-tuple-element.809.refs_1_.refs_8_), channel_id=1, source_target_pairs={{0,8},{4,12},{8,0},{12,4},{16,24},{20,28},{24,16},{28,20},{1,9},{5... | collective-permute-start | bytes 3538952 | tf_op jit(solution)/shard_map/ppermute | solution.py:120
  482.4 30.2 %collective-permute-start.45 = (bf16[9,128,512]{2,1,0:T(8,128)(2,1)}, bf16[9,128,512]{2,1,0:T(8,128)(2,1)}, u32[]{:S(2)}, u32[]{:S(2)}) collective-permute-start(bf16[9,128,512]{2,1,0:T(8,128)(2,1)} %get-tuple-element.810.refs_3_.refs_9_), channel_id=1, source_target_pairs={{0,16},{4,20},{8,24},{12,28},{16,0},{20,4},{24,8},{28,12},{1,17},{... | collective-permute-start | bytes 3538952 | tf_op jit(solution)/shard_map/ppermute | solution.py:120
  522.9 35.4 %collective-permute-start.50 = (bf16[128,1536]{1,0:T(8,128)(2,1)S(1)}, bf16[128,1536]{1,0:T(8,128)(2,1)}, u32[]{:S(2)}, u32[]{:S(2)}) collective-permute-start(bf16[128,1536]{1,0:T(8,128)(2,1)S(1)} %pad_maximum_fusion.21), channel_id=1, source_target_pairs={{0,2},{1,3},{2,0},{3,1},{4,6},{5,7},{6,4},{7,5},{8,10},{9,11},{10,... | collective-permute-start | bytes 1179656 | tf_op jit(solution)/shard_map/ppermute | solution.py:125
  567.2 39.4 %collective-permute-start.54 = (bf16[128,1536]{1,0:T(8,128)(2,1)S(1)}, bf16[128,1536]{1,0:T(8,128)(2,1)S(1)}, u32[]{:S(2)}, u32[]{:S(2)}) collective-permute-start(bf16[128,1536]{1,0:T(8,128)(2,1)S(1)} %pad_maximum_fusion.25), channel_id=1, source_target_pairs={{0,2},{1,3},{2,0},{3,1},{4,6},{5,7},{6,4},{7,5},{8,10},{9,11},{10,... | collective-permute-start | bytes 1179656 | tf_op jit(solution)/shard_map/ppermute | solution.py:125
  569.5 49.0 %collective-permute-start.55 = (bf16[128,1536]{1,0:T(8,128)(2,1)}, bf16[128,1536]{1,0:T(8,128)(2,1)}, u32[]{:S(2)}, u32[]{:S(2)}) collective-permute-start(bf16[128,1536]{1,0:T(8,128)(2,1)} %pad_maximum_fusion.26), channel_id=1, source_target_pairs={{0,1},{1,2},{2,3},{3,0},{4,5},{5,6},{6,7},{7,4},{8,9},{9,10},{10,1... | collective-permute-start | bytes 1179656 | tf_op jit(solution)/shard_map/ppermute | solution.py:125
  618.4 163.8 %all-gather.35.cloned.1.call-start = ((), (), s32[]{:S(2)}) async-start(), calls=%async_computation.2 | async-start | bytes 5242880 | tf_op jit(solution)/shard_map/all_gather | solution.py:506
  671.4 243.5 %all-gather.37.cloned.1.call-start = ((), (), s32[]{:S(2)}) async-start(), calls=%async_computation.3 | async-start | bytes 2621440 | tf_op jit(solution)/shard_map/all_gather | solution.py:506
  740.9 229.0 %all-gather.39.cloned.1.call-start = ((), (), s32[]{:S(2)}) async-start(), calls=%async_computation.4 | async-start | bytes 3932160 | tf_op jit(solution)/shard_map/all_gather | solution.py:506
  793.3 36.0 %collective-permute-start.68 = (bf16[512,4096]{1,0:T(8,128)(2,1)}, bf16[512,4096]{1,0:T(8,128)(2,1)}, u32[]{:S(2)}, u32[]{:S(2)}) collective-permute-start(bf16[512,4096]{1,0:T(8,128)(2,1)} %get-tuple-element.1171), channel_id=1, source_target_pairs={{0,4},{4,0},{8,12},{12,8},{16,20},{20,16},{24,28},{28,24},{1,5},{5... | collective-permute-start | bytes 12582920 | tf_op jit(solution)/shard_map/ppermute | solution.py:120
  804.4 306.6 %all-gather.41.cloned.1.call-start = ((), (), s32[]{:S(2)}) async-start(), calls=%async_computation.5 | async-start | bytes 6881280 | tf_op jit(solution)/shard_map/all_gather | solution.py:506
  839.4 31.9 %collective-permute-start.73 = (bf16[512,512]{1,0:T(8,128)(2,1)S(1)}, bf16[512,512]{1,0:T(8,128)(2,1)S(1)}, u32[]{:S(2)}, u32[]{:S(2)}) collective-permute-start(bf16[512,512]{1,0:T(8,128)(2,1)S(1)} %get-tuple-element.1115), channel_id=1, source_target_pairs={{0,16},{4,20},{8,24},{12,28},{16,0},{20,4},{24,8},{28,12},{1,17},{... | collective-permute-start | bytes 1572872 | tf_op jit(solution)/shard_map/ppermute | solution.py:120
  923.2 35.6 %collective-permute-start.82 = (bf16[128,512]{1,0:T(8,128)(2,1)S(1)}, bf16[128,512]{1,0:T(8,128)(2,1)S(1)}, u32[]{:S(2)}, u32[]{:S(2)}) collective-permute-start(bf16[128,512]{1,0:T(8,128)(2,1)S(1)} %get-tuple-element.1143), channel_id=1, source_target_pairs={{0,4},{4,0},{8,12},{12,8},{16,20},{20,16},{24,28},{28,24},{1,5},{5... | collective-permute-start | bytes 393224 | tf_op jit(solution)/shard_map/ppermute | solution.py:120
  986.4 44.1 %collective-permute-start.86 = (bf16[128,3584]{1,0:T(8,128)(2,1)}, bf16[128,3584]{1,0:T(8,128)(2,1)}, u32[]{:S(2)}, u32[]{:S(2)}) collective-permute-start(bf16[128,3584]{1,0:T(8,128)(2,1)} %get-tuple-element.1089), channel_id=1, source_target_pairs={{0,16},{4,20},{8,24},{12,28},{16,0},{20,4},{24,8},{28,12},{1,17},{... | collective-permute-start | bytes 2752520 | tf_op jit(solution)/shard_map/ppermute | solution.py:120
  987.7 42.8 %collective-permute-start.85 = (bf16[128,3584]{1,0:T(8,128)(2,1)}, bf16[128,3584]{1,0:T(8,128)(2,1)}, u32[]{:S(2)}, u32[]{:S(2)}) collective-permute-start(bf16[128,3584]{1,0:T(8,128)(2,1)} %get-tuple-element.1090), channel_id=1, source_target_pairs={{0,8},{4,12},{8,0},{12,4},{16,24},{20,28},{24,16},{28,20},{1,9},{5... | collective-permute-start | bytes 2752520 | tf_op jit(solution)/shard_map/ppermute | solution.py:120
  (323 other events, 3212.1 us)
Sparse Core Ops, SparseCore 0:
  13.4 28.1 all-gather.42
  44.5 28.1 all-gather.44
  74.3 27.4 all-gather.46
  105.0 27.0 all-gather.48
  138.5 26.9 all-gather.50
  175.3 26.8 all-gather.52
  209.3 26.9 all-gather.54
  244.9 26.8 all-gather.56
  286.5 26.8 all-gather.58
  334.5 25.9 all-gather.60
  390.2 25.9 all-gather.62
  434.9 26.0 all-gather.64
  468.4 43.8 all-gather.30
  618.5 78.3 all-gather.32
  698.4 79.2 all-gather.34
  779.1 44.4 all-gather.36
  825.0 62.2 all-gather.38
  1003.6 99.3 all-gather.40
